TPU v7x, 32 devices: a whole 2x2x4 slice. The times are simulated.
32 devices in a mesh: seq: 8 (over z, x), head: 4 (over y, core).
Axes of the slice: x: 2, y: 2, z: 4, core: 2. Of those that a mesh axis runs over, the one named last changes fastest.
Arguments:
- queries: bfloat16 [8192, 4096], P('seq', 'head'), may hold values from -6 to 6
- key_rows: bfloat16 [8192, 4096], P('seq', 'head'), may hold values from -6 to 6
- value_rows: bfloat16 [8192, 4096], P('seq', 'head'), may hold values from -6 to 6
- gate_logits: bfloat16 [8192, 4096], P('seq', 'head'), may hold values from -6 to 6
- norm_gain: float32 [4096], P('head'), may hold values from 0.1 to 1.9
- out_weight: bfloat16 [4096, 6144], P('head', 'seq'), may hold values from -0.125 to 0.125
- doc_lengths: int32 [16], replicated, may hold values from 1 to 4096, 8192 in all
Outputs:
- layer_out: bfloat16 [8192, 6144], P('seq', 'head')
Inputs may be any that keep to these rules, and one draw needn't show every extreme that they name: `doc_lengths`: the lengths sum to 8192; the longest document has exactly 4096 positions.
All inputs are finite; a program needn't handle non-finite values.
Results may differ from a plain program's by a relative error of at most 0.0057.
Values may be sent and summed in bfloat16 or wider, within the bound.
No kernel may reach another device: no remote copies, remote signals or barrier semaphores. Data moves between devices by JAX's collectives and lax.ppermute only.
A program may use at most 128 MiB of HBM per device.

v0:
```python
import jax
import jax.numpy as jnp
from jax import lax
from jax.sharding import PartitionSpec as P

HS = 128


norm_eps = 1e-05


def doc_index(doc_lengths, positions):
    starts_all = jnp.cumsum(doc_lengths) - doc_lengths
    hits = (starts_all[None, :] <= positions[:, None]).astype(jnp.int32)
    return jnp.sum(hits, axis=1) - 1


def shards(queries, key_rows, value_rows, gate_logits, norm_gain, out_weight, doc_lengths):
    tok_rows = queries.shape[0]
    width_here = queries.shape[1]
    head_here = width_here // HS
    seq_index = lax.axis_index("seq")
    first_pos = seq_index * tok_rows
    positions = first_pos + jnp.arange(tok_rows, dtype=jnp.int32)
    doc_ids = doc_index(doc_lengths, positions)
    prev_id = doc_index(doc_lengths, jnp.reshape(first_pos - 1, (1,)))[0]
    query_heads = queries.reshape(tok_rows, head_here, HS)
    key_heads = key_rows.reshape(tok_rows, head_here, HS)
    value_heads = value_rows.reshape(tok_rows, head_here, HS)
    causal = jnp.arange(tok_rows)[:, None] >= jnp.arange(tok_rows)[None, :]
    same_doc = causal & (doc_ids[:, None] == doc_ids[None, :])
    scores = jnp.einsum("thd,shd->hts", query_heads, key_heads, preferred_element_type=jnp.float32)
    weights_intra = jnp.where(same_doc[None], scores, 0.0).astype(jnp.bfloat16)
    intra_part = jnp.einsum(
        "hts,shd->thd", weights_intra, value_heads, preferred_element_type=jnp.float32
    )
    final_id = doc_ids[-1]
    key_masked = jnp.where(
        (doc_ids == final_id)[:, None, None], key_heads, jnp.zeros_like(key_heads)
    )
    summary = jnp.einsum(
        "thd,the->hde", key_masked, value_heads, preferred_element_type=jnp.float32
    )
    resets = jnp.reshape((prev_id != final_id).astype(jnp.float32), (1,))
    gathered_states, reset_flags = (
        lax.all_gather(summary[None], "seq", axis=0, tiled=True),
        lax.all_gather(resets, "seq", axis=0, tiled=True),
    )
    device_order = jnp.arange(gathered_states.shape[0], dtype=jnp.int32)
    reset_marks = jnp.where((device_order < seq_index) & (reset_flags > 0.5), device_order, -1)
    first_live = jnp.max(reset_marks)
    fold_weights = ((device_order >= first_live) & (device_order < seq_index)).astype(jnp.float32)
    incoming = jnp.einsum(
        "n,nhde->hde", fold_weights, gathered_states, precision=lax.Precision.HIGHEST
    )
    carried_mask = (doc_ids == prev_id)[:, None, None]
    inter_part = jnp.einsum(
        "thd,hde->the",
        query_heads,
        incoming.astype(jnp.bfloat16),
        preferred_element_type=jnp.float32,
    )
    attended = intra_part + jnp.where(carried_mask, inter_part, 0.0)
    gain_rows = norm_gain.reshape(head_here, HS)
    gate_heads = jax.nn.sigmoid(gate_logits.astype(jnp.float32).reshape(tok_rows, head_here, HS))
    scale = lax.rsqrt(jnp.mean(attended * attended, axis=-1, keepdims=True) + norm_eps)
    normed = attended * scale * gain_rows * gate_heads
    head_out = normed.astype(jnp.bfloat16).reshape(tok_rows, width_here)
    partial_terms = jnp.dot(
        head_out,
        lax.all_gather(out_weight, "seq", axis=1, tiled=True),
        preferred_element_type=jnp.float32,
    )
    summed = lax.psum_scatter(partial_terms, "head", scatter_dimension=1, tiled=True)
    return summed.astype(jnp.bfloat16)


def solution(mesh):
    return jax.shard_map(
        shards,
        mesh=mesh,
        in_specs=(
            P("seq", "head"),
            P("seq", "head"),
            P("seq", "head"),
            P("seq", "head"),
            P("head"),
            P("head", "seq"),
            P(),
        ),
        out_specs=P("seq", "head"),
        check_vma=False,
    )
```

profile of v0, /device:TPU:26, one launch (start us, length us, event | category | flops | bytes accessed | tf_op | source)
XLA Modules:
  0.0 481.1 jit_solution(12560502383877154799)
XLA Ops:
  6.5 0.0 copy-start
  6.5 0.0 all-gather.6.cloned.1.call-start
  6.5 0.9 copy.28
  7.5 0.1 reduce.2
  7.6 1.3 fusion.28
  9.5 0.1 convert_reduce_fusion
  9.6 0.6 slice.3
  10.2 3.9 copy.39
  14.1 0.6 broadcast_compare_fusion.1
  14.8 0.0 copy-start.3
  14.8 3.8 fusion.9
  18.6 0.0 all-gather.6.cloned.1.call-update
  18.6 0.0 all-gather.4.cloned.1.call-start
  18.7 0.7 all-gather.4.cloned.1.call-update
  19.4 0.0 reduce-scatter.2.cloned.1.call-start
  20.1 0.0 copy-done.3
  20.1 0.6 dynamic-slice
  20.7 0.7 dynamic-update-slice
  21.4 17.0 %all-reduce = f32[8]{0:T(128)S(1)} all-reduce(f32[8]{0:T(128)S(1)} %dynamic-update-slice), channel_id=1, replica_groups=mesh['seq'=8,'head'=4] {'seq'}, use_global_device_ids=true, to_apply=%add | all-reduce | flops 8 | bytes 64
  38.4 4.7 add_divide_fusion
  43.1 5.3 %copy.35 = f32[1024,1024]{0,1:T(8,128)} copy(f32[1024,1024]{1,0:T(8,128)} %add_divide_fusion) | data formatting | bytes 8388608 | tf_op jit(solution)/shard_map/div | solution.py:65
  48.4 0.7 fusion.29
  49.1 1.7 fusion.7
  50.8 39.9 %all-gather.6.cloned.1.call-done = f32[64,128,128]{2,1,0:T(8,128)} async-done(((f32[8,128,128]{2,1,0:T(8,128)}), f32[64,128,128]{2,1,0:T(8,128)}) %all-gather.6.cloned.1.call-update) | async-done | bytes 4194320 | tf_op jit(solution)/shard_map/all_gather | solution.py:46
  90.7 7.1 %fusion.5 = bf16[1,8,128,128]{3,0,2,1:T(2,128)(2,1)S(1)} fusion(f32[8,8,128,128]{3,2,1,0:T(8,128)} %bitcast.55, s32[]{:T(128)} %fusion.29, s32[]{:T(128)S(6)} %axis_index.15), kind=kOutput, calls=%fused_computation.6 | convolution fusion | flops 12582936 | bytes 4456456 | tf_op jit(solution)/shard_map/n,nhde->hde/dot_general | solution.py:53
  97.9 0.4 copy.38
  98.3 0.0 copy-done
  98.3 2.6 fusion.11
  100.9 0.0 copy-start.2
  100.9 15.0 %multiply_reduce_fusion = (f32[1024,8]{0,1:T(8,128)S(1)}, f32[1024,8,128]{0,2,1:T(8,128)}) fusion(f32[8,128,1024]{2,1,0:T(8,128)} %fusion.11, pred[1024]{0:T(1024)(128)(4,1)S(1)} %get-tuple-element.7, pred[1024,1024]{1,0:T(8,128)(4,1)} %fusion.7, bf16[1024,8,128]{0,2,1:T(8,128)(2,1)} %bitcast.58, bf16[1024,1024]{1,0:T(8,128)(2,1)} %param.9, ...), kind=kOutput, calls=%fused_computation.10 | convolution fusion | flops 4315930624 | bytes 15762432 | tf_op jit(solution)/shard_map/hts,shd->thd/dot_general | solution.py:34
  115.9 0.0 copy-done.2
  115.9 4.2 multiply_convert_fusion
  120.2 147.0 %all-gather.4.cloned.1.call-done = bf16[1024,6144]{1,0:T(8,128)(2,1)} async-done(((bf16[1024,768]{1,0:T(8,128)(2,1)}), bf16[1024,6144]{1,0:T(8,128)(2,1)}) %all-gather.4.cloned.1.call-update) | async-done | bytes 12582928 | tf_op jit(solution)/shard_map/all_gather | solution.py:71
  267.2 20.9 %fusion.37 = f32[1024,6144]{1,0:T(8,128)} fusion(bf16[1024,1024]{0,1:T(8,128)(2,1)S(1)} %bitcast.56, bf16[1024,6144]{1,0:T(8,128)(2,1)} %all-gather.4.cloned.1.call-done), kind=kOutput, calls=%fused_computation.47 | convolution fusion | flops 12884901888 | bytes 39845888 | tf_op jit(solution)/shard_map/dot_general | solution.py:69
  288.1 0.0 reduce-scatter.2.cloned.1.call-update
  288.1 0.0 copy-start.1
  288.1 181.7 %reduce-scatter.2.cloned.1.call-done = f32[1024,1536]{1,0:T(8,128)} async-done(((f32[1024,6144]{1,0:T(8,128)}), f32[1024,1536]{1,0:T(8,128)}) %reduce-scatter.2.cloned.1.call-update) | async-done | bytes 6291472 | tf_op jit(solution)/shard_map/reduce_scatter | solution.py:74
  469.8 4.8 %convert_element_type.30 = bf16[1024,1536]{1,0:T(8,128)(2,1)} convert(f32[1024,1536]{1,0:T(8,128)} %reduce-scatter.2.cloned.1.call-done) | non-fusion elementwise | flops 1572864 | bytes 9437184 | tf_op jit(solution)/shard_map/convert_element_type | solution.py:75
  474.6 0.0 copy-done.1
  (5 shorter events, 0.1 us)
Async XLA Ops:
  6.5 91.7 %copy-start = (bf16[1024,1024]{1,0:T(8,128)(2,1)S(1)}, bf16[1024,1024]{1,0:T(8,128)(2,1)}, u32[]{:S(2)}) copy-start(bf16[1024,1024]{1,0:T(8,128)(2,1)} %param.7) | copy-start | bytes 6291460
  6.5 84.2 %all-gather.6.cloned.1.call-start = ((), (), s32[]{:S(2)}) async-start(), calls=%async_computation.3 | async-start | bytes 4718592 | tf_op jit(solution)/shard_map/all_gather | solution.py:46
  14.8 5.3 %copy-start.3 = (u32[32]{0:T(128)S(1)}, u32[32]{0:T(128)}, u32[]{:S(2)}) copy-start(u32[32]{0:T(128)} %constant.40) | copy-start | bytes 388
  18.6 248.5 %all-gather.4.cloned.1.call-start = ((), (), s32[]{:S(2)}) async-start(), calls=%async_computation.1 | async-start | bytes 14155776 | tf_op jit(solution)/shard_map/all_gather | solution.py:71
  19.4 450.4 %reduce-scatter.2.cloned.1.call-start = ((), (), s32[]{:S(2)}) async-start(), calls=%async_computation.2 | async-start | bytes 31457280 | tf_op jit(solution)/shard_map/reduce_scatter | solution.py:74
  100.9 15.0 %copy-start.2 = (f32[1024]{0:T(1024)S(1)}, f32[1024]{0:T(1024)}, u32[]{:S(2)}) copy-start(f32[1024]{0:T(1024)} %param.11) | copy-start | bytes 12292
  288.1 186.5 %copy-start.1 = (bf16[1024,1024]{1,0:T(8,128)(2,1)S(1)}, bf16[1024,1024]{1,0:T(8,128)(2,1)}, u32[]{:S(2)}) copy-start(bf16[1024,1024]{1,0:T(8,128)(2,1)} %param.7) | copy-start | bytes 6291460
Sparse Core Ops, SparseCore 0:
  18.8 71.9 all-gather.5
  92.9 174.1 all-gather.3
  288.2 181.5 reduce-scatter.1
where the time goes:
time: 483 us; the launch traced here: 481 us
  waiting for transfers between devices  369 us (76%)
  matrix products  49.5 us (10%)
  other arithmetic  18.2 us (4%)
  blocking collectives  17 us (4%)
  between operations  14.5 us (3%)
  local copies, waits for them, and re-layouts  12.5 us (3%)
    reduce_scatter x1, waiting for transfers between devices, shards(): lax.psum_scatter(partial_terms, 'head', scatter_dimension=1, tiled=True)  182 us
    all_gather x1, waiting for transfers between devices, shards(): lax.all_gather(out_weight, 'seq', axis=1, tiled=True)  147 us
    all_gather x1, waiting for transfers between devices, shards(): lax.all_gather(summary[None], 'seq', axis=0, tiled=True)  39.9 us
    dot_general x1, matrix products, shards(): jnp.dot(head_out, lax.all_gather(out_weight, 'seq', axis=1, tiled=True),...  20.9 us
    unnamed x1, blocking collectives  17 us
    dot_general x1, matrix products, shards(): jnp.einsum('hts,shd->thd', weights_intra, value_heads, preferred_element_...  15 us
  transfers between devices with their start and end apart: 3, of which 3 were waited for; matrix products, arithmetic and copies ran while one was open for 9% of the time, Pallas kernels for 0%

commit v1 on v0

v1 whole, which is shorter than its diff:
```python
import functools

import jax
import jax.numpy as jnp
from jax import lax
from jax.experimental import pallas as pl
from jax.experimental.pallas import tpu as pltpu
from jax.sharding import PartitionSpec as P

HS = 128
EPS = 1e-05
BOTH = ("seq", "head")
VMEM_LIMIT = 64 * 1024 * 1024
COST_SCALE = 4096
F32 = jnp.float32
BF16 = jnp.bfloat16


def params():
    return pltpu.CompilerParams(vmem_limit_bytes=VMEM_LIMIT)


def cost(flops, nbytes):
    return pl.CostEstimate(flops=flops // COST_SCALE, bytes_accessed=nbytes // COST_SCALE, transcendentals=0)


def tie(value, *before):
    return lax.optimization_barrier((value, *before))[0]


def doc_start_of(lengths_ref, position):
    def step(c, carry):
        start, found = carry
        found = jnp.where(start <= position, start, found)
        return start + lengths_ref[c], found

    _, found = lax.fori_loop(0, lengths_ref.shape[0], step, (jnp.int32(0), jnp.int32(0)))
    return found


def doc_start_rows(lengths_ref, first_pos, rows):
    positions = lax.broadcasted_iota(jnp.int32, (rows, HS), 0)
    found = jnp.full((rows, HS), -first_pos, jnp.int32)
    start = -first_pos
    for c in range(lengths_ref.shape[0]):
        found = jnp.where(start <= positions, start, found)
        start = start + lengths_ref[c]
    return found


def summary_kernel(lengths_ref, key_ref, value_ref, out_ref):
    rows = key_ref.shape[0]
    first_pos = lax.axis_index("seq") * rows
    last_start = doc_start_of(lengths_ref, first_pos + rows - 1) - first_pos
    mask = lax.broadcasted_iota(jnp.int32, (rows, HS), 0) >= last_start
    for h in range(out_ref.shape[0]):
        at = slice(h * HS, (h + 1) * HS)
        keys = jnp.where(mask, key_ref[:, at].astype(F32), 0.0).astype(BF16)
        total = lax.dot_general(keys, value_ref[:, at], (((0,), (0,)), ((), ())), preferred_element_type=F32)
        out_ref[h] = total.astype(BF16)


def pair_kernel(lengths_ref, own_ref, other_ref, out_ref, *, rows):
    index = lax.axis_index("seq")
    odd = lax.rem(index, 2)
    odd_first = (index - odd + 1) * rows
    keep = (doc_start_of(lengths_ref, odd_first + rows - 1) < odd_first).astype(F32)
    own_scale = jnp.where(odd == 1, 1.0, keep)
    other_scale = jnp.where(odd == 1, keep, 1.0)
    out_ref[...] = (own_scale * own_ref[...].astype(F32) + other_scale * other_ref[...].astype(F32)).astype(BF16)


def intra_kernel(lengths_ref, query_ref, key_ref, value_ref, out_ref, start_ref, *, tile):
    rows = query_ref.shape[0]

    @pl.when(pl.program_id(0) == 0)
    def _():
        start_ref[...] = doc_start_rows(lengths_ref, lax.axis_index("seq") * rows, rows)

    for t in range(rows // tile):
        at = pl.ds(t * tile, tile)
        query = query_ref[at, :]
        starts = start_ref[at, 0:1]
        span = (t + 1) * tile
        scores = lax.dot_general(
            query, key_ref[pl.ds(0, span), :], (((1,), (1,)), ((), ())), preferred_element_type=F32
        )
        s = lax.broadcasted_iota(jnp.int32, (tile, span), 1)
        p = lax.broadcasted_iota(jnp.int32, (tile, span), 0) + t * tile
        weights = jnp.where((s <= p) & (s >= starts), scores, 0.0).astype(BF16)
        out_ref[at, :] = jnp.dot(weights, value_ref[pl.ds(0, span), :], preferred_element_type=F32)


def finish_kernel(
    lengths_ref, query_ref, low_ref, high_ref, gate_ref, gain_ref, other_ref, *rest, rows, heads_low
):
    pair_refs, (out_ref, scalars_ref) = rest[:-2], rest[-2:]
    index = lax.axis_index("seq")
    odd = lax.rem(index, 2)
    first_pos = index * rows
    pair_first = (index - odd) * rows

    @pl.when(pl.program_id(0) == 0)
    def _():
        start, before, end = jnp.int32(0), jnp.int32(0), jnp.int32(0)
        for c in range(lengths_ref.shape[0]):
            following = start + lengths_ref[c]
            inside = start <= first_pos - 1
            before = jnp.where(inside, start, before)
            end = jnp.where(inside, following, end)
            start = following
        scalars_ref[0] = before
        scalars_ref[1] = end

    before, end = scalars_ref[0], scalars_ref[1]
    incoming = odd.astype(F32) * other_ref[0].astype(F32)
    for j, pair_ref in enumerate(pair_refs):
        live = (before < pair_first - j * 2 * rows).astype(F32)
        incoming = incoming + live * pair_ref[0].astype(F32)
    carried = incoming.astype(BF16)
    inter = jnp.dot(query_ref[...], carried, preferred_element_type=F32)
    inside = lax.broadcasted_iota(jnp.int32, (rows, HS), 0) < end - first_pos
    intra = jnp.where(pl.program_id(0) < heads_low, low_ref[...], high_ref[...])
    a = intra + jnp.where(inside, inter, 0.0)
    scale = lax.rsqrt(jnp.mean(a * a, axis=-1, keepdims=True) + EPS)
    gate = jax.nn.sigmoid(gate_ref[...].astype(F32))
    out_ref[...] = (a * scale * gain_ref[...] * gate).astype(BF16)


def merge_kernel(mine_ref, gathered_ref, out_ref):
    rows = mine_ref.shape[0]
    wide = out_ref.shape[2]
    for i in range(out_ref.shape[0]):
        out_ref[i, :rows, :] = mine_ref[:, i * wide : (i + 1) * wide]
        out_ref[i, rows:, :] = gathered_ref[:, i * wide : (i + 1) * wide]


def split_kernel(*refs):
    half = len(refs) // 3
    for i, ref in enumerate(refs[:half]):
        for j in range(2):
            refs[half + 2 * i + j][...] = ref[j : j + 1]


def partial_kernel(table_ref, own_ref, other_ref, *rest, slots, at):
    weights, (sent_ref, kept_ref, buffer_ref, sems) = rest[:slots], rest[slots:]
    width = own_ref.shape[1]
    pieces, _, columns = weights[0].shape

    def copies(slot):
        return [
            pltpu.make_async_copy(
                weights[slot].at[piece],
                buffer_ref.at[slot, :, pl.ds(piece * columns, columns)],
                sems.at[slot, piece],
            )
            for piece in range(pieces)
        ]

    @pl.when(pl.program_id(0) == 0)
    def _():
        for slot in range(slots):

            @pl.when(table_ref[at + slot] != 0)
            def _():
                for copy in copies(slot):
                    copy.start()

    for slot in range(slots):
        role = table_ref[at + slot]

        @pl.when((role != 0) & (pl.program_id(0) == 0))
        def _():
            for copy in copies(slot):
                copy.wait()

        @pl.when(role != 0)
        def _():
            total = jnp.dot(own_ref[...], buffer_ref[slot, :width, :], preferred_element_type=F32)
            total += jnp.dot(other_ref[...], buffer_ref[slot, width:, :], preferred_element_type=F32)

            @pl.when(role == 1)
            def _():
                kept_ref[...] = total

            @pl.when(role == 2)
            def _():
                sent_ref[...] = total.astype(BF16)


def add_kernel(table_ref, kept_ref, *rest, at, shares):
    received, out_ref = rest[:shares], rest[-1]

    @pl.when(table_ref[at] == 1)
    def _():
        total = kept_ref[...]
        for ref in received:
            total = total + ref[...].astype(F32)
        out_ref[...] = total.astype(BF16).reshape(out_ref.shape)

    @pl.when(table_ref[at] != 1)
    def _():
        out_ref[...] = rest[shares][...] if len(rest) > shares + 1 else jnp.zeros_like(out_ref)


def plan(n, heads, pieces):
    ring = list(range(0, n, 2)) + list(range(n - 1, 0, -2))
    spot = {s: p for p, s in enumerate(ring)}
    per_head = n // heads
    half = n // 2
    everything = tuple(range(pieces))
    wanted = [((0,), everything)]
    for k in range(1, half):
        if k < half - 1:
            wanted.append(((-k, k), everything))
        else:
            wanted += [((-k, k), (i,)) for i in everything]
    wanted += [((half,), (i,)) for i in everything]

    def block(s, slot):
        return ring[(spot[s] + slot) % n]

    def role(s, h, slot):
        owner = block(s, slot) // per_head
        if owner % 2 != h % 2:
            return 0
        return 1 if owner == h else 2

    groups = []
    for slots, chosen in wanted:
        clash = any(
            [role(s, h, slot) for slot in slots].count(r) > 1 for s in range(n) for h in range(heads) for r in (1, 2)
        )
        groups += [((slot,), chosen) for slot in slots] if clash else [(slots, chosen)]
    places, rows = [], [[] for _ in range(n * heads)]
    for slots, chosen in groups:
        places.append(len(rows[0]))
        for s in range(n):
            for h in range(heads):
                roles = [role(s, h, slot) for slot in slots]
                mine = [slot for slot, r in zip(slots, roles) if r == 1]
                column = block(s, mine[0]) % per_head if mine else 0
                if len(chosen) < pieces:
                    column = column * pieces + chosen[0]
                rows[s * heads + h] += [int(bool(mine)), column] + roles
    return ring, groups, places, rows, block


def solution(mesh):
    n, heads = mesh.shape["seq"], mesh.shape["head"]
    pairs = heads // 2
    per_head = n // heads
    half = n // 2

    def shards(queries, key_rows, value_rows, gate_logits, norm_gain, out_weight, doc_lengths):
        rows, width = queries.shape
        heads_here = width // HS
        columns = out_weight.shape[1]
        pieces = 2 if columns % 256 == 0 else 1
        part = columns // pieces
        ring, groups, places, table_rows, block = plan(n, heads, pieces)
        device = lax.axis_index("seq") * heads + lax.axis_index("head")
        table = lax.dynamic_index_in_dim(jnp.asarray(table_rows, jnp.int32), device, 0, keepdims=False)
        smem = pl.BlockSpec(memory_space=pltpu.SMEM)
        anywhere = pl.BlockSpec(memory_space=pl.ANY)
        head_block = pl.BlockSpec((rows, HS), lambda h: (0, h))
        two_heads = pl.BlockSpec((rows, 2 * HS), lambda h: (0, h))
        state_block = pl.BlockSpec((1, HS, HS), lambda h: (h, 0, 0))

        def core_of(s, slot):
            return (block(s, slot) // per_head) % 2

        def call(kernel, name, **options):
            return pl.pallas_call(kernel, compiler_params=params(), name=name, **options)

        summary = call(
            summary_kernel,
            "summary",
            grid=(heads_here // 2,),
            in_specs=[smem, two_heads, two_heads],
            out_specs=pl.BlockSpec((2, HS, HS), lambda h: (h, 0, 0)),
            out_shape=jax.ShapeDtypeStruct((heads_here, HS, HS), BF16),
            cost_estimate=cost(2 * rows * width * HS, 4 * rows * width),
        )(doc_lengths, key_rows, value_rows)

        def along(slot, step):
            target = {s: block(s, -step) for s in range(n)}
            return [
                (s * heads + 2 * y + core_of(s, slot), target[s] * heads + 2 * y + core_of(s, slot))
                for s in range(n)
                for y in range(pairs)
            ]

        gather = [
            (s * heads + 2 * y + 1 - core_of(s, 0), s * heads + 2 * y + core_of(s, 0))
            for s in range(n)
            for y in range(pairs)
        ]
        arrived = {}

        def send_on(k, i, *before):
            steps = (-1, 1) if k < half else (-1 if i % 2 == 0 else 1,)
            for step in steps:
                source = step * (k - 1)
                here = arrived.get((source, None), arrived.get((source, i)))
                if i is None or here.shape[0] == 1:
                    here = tie(here, *before)
                if i is not None and here.shape[0] > 1:
                    if (source, i) not in arrived:
                        both = [tie(arrived[x, None], *before) for x in (-source, source)]
                        split = call(
                            split_kernel,
                            "split",
                            out_shape=[jax.ShapeDtypeStruct((1, *here.shape[1:]), BF16)] * (2 * len(both)),
                            cost_estimate=cost(width * columns, 16 * width * columns),
                        )(*both)
                        for x, halves in zip((-source, source), (split[:2], split[2:])):
                            for j in range(2):
                                arrived[x, j] = halves[j]
                    here = arrived[source, i]
                arrived[half if k == half else step * k, i] = lax.ppermute(here, BOTH, along(source, step))

        def there(k, i):
            return [arrived[key] for key in ((-k, i), (k, i)) if key in arrived]

        gathered = lax.ppermute(out_weight, BOTH, gather)
        merged = call(
            merge_kernel,
            "merge",
            out_shape=jax.ShapeDtypeStruct((pieces, 2 * width, part), BF16),
            cost_estimate=cost(width * part, 8 * width * columns),
        )(out_weight, tie(gathered, summary))
        arrived[0, None] = merged

        other_state = lax.ppermute(summary, "seq", [(s, s ^ 1) for s in range(n)])

        def intra_of(first, count, *before):
            block_at = pl.BlockSpec((rows, HS), lambda h: (0, first + h))
            return call(
                functools.partial(intra_kernel, tile=256),
                "intra",
                grid=(count,),
                in_specs=[smem, block_at, block_at, block_at],
                out_specs=head_block,
                out_shape=jax.ShapeDtypeStruct((rows, count * HS), F32),
                scratch_shapes=[pltpu.VMEM((rows, HS), jnp.int32)],
                cost_estimate=cost(4 * rows * rows * count * HS, 10 * rows * count * HS),
            )(tie(doc_lengths, *before), queries, key_rows, value_rows)

        count = heads_here // 2
        whole_state = pl.BlockSpec((heads_here, HS, HS), lambda: (0, 0, 0))
        pair_state = call(
            functools.partial(pair_kernel, rows=rows),
            "pair_state",
            in_specs=[smem, whole_state, whole_state],
            out_specs=whole_state,
            out_shape=jax.ShapeDtypeStruct((heads_here, HS, HS), BF16),
            cost_estimate=cost(heads_here * HS * HS, 6 * heads_here * HS * HS),
        )(doc_lengths, tie(summary, merged), other_state)
        earlier = [
            lax.ppermute(pair_state, "seq", [(s, s + 2 * d) for s in range(n - 2 * d)]) for d in range(1, n // 4 + 1)
        ]
        intra_low = intra_of(0, count, pair_state)
        intra_high = intra_of(count, count, intra_low)
        send_on(1, None, *earlier)
        for k in range(2, min(3, half - 1)):
            send_on(k, None, intra_high)

        low = pl.BlockSpec((rows, HS), lambda h: (0, jnp.minimum(h, count - 1)))
        high = pl.BlockSpec((rows, HS), lambda h: (0, jnp.maximum(h - count, 0)))
        head_out = call(
            functools.partial(finish_kernel, rows=rows, heads_low=count),
            "finish",
            grid=(heads_here,),
            in_specs=[smem, head_block, low, high, head_block, pl.BlockSpec((1, HS), lambda h: (0, h)), state_block]
            + [state_block] * len(earlier),
            out_specs=head_block,
            out_shape=jax.ShapeDtypeStruct((rows, width), BF16),
            scratch_shapes=[pltpu.SMEM((2,), jnp.int32)],
            cost_estimate=cost(2 * rows * width * HS, 12 * rows * width),
        )(
            doc_lengths,
            queries,
            intra_low,
            intra_high,
            gate_logits,
            norm_gain.reshape(1, width),
            other_state,
            *earlier,
        )
        head_other = lax.ppermute(head_out, "head", [(h, h ^ 1) for h in range(heads)])

        tile = min(rows, 512)
        by_columns = part % 128 == 0
        out = []
        out_dims = (rows, per_head * columns) if by_columns else (per_head, rows, columns)
        row_tile = pl.BlockSpec((tile, width), lambda i: (i, 0))

        def share(g, *before):
            (slots, chosen), at = groups[g], places[g]
            wide = part * len(chosen)
            weights = [arrived[slot, None if (slot, None) in arrived else chosen[0]] for slot in slots]
            sent, kept = call(
                functools.partial(partial_kernel, slots=len(slots), at=at + 2),
                "partial",
                grid=(rows // tile,),
                in_specs=[smem, row_tile, row_tile] + [anywhere] * len(weights),
                out_specs=[pl.BlockSpec((tile, wide), lambda i: (i, 0))] * 2,
                out_shape=[jax.ShapeDtypeStruct((rows, wide), BF16), jax.ShapeDtypeStruct((rows, wide), F32)],
                scratch_shapes=[
                    pltpu.VMEM((len(slots), 2 * width, wide), BF16),
                    pltpu.SemaphoreType.DMA((len(slots), len(chosen))),
                ],
                cost_estimate=cost(4 * rows * width * wide, 4 * rows * width + 10 * rows * wide),
            )(tie(table, *before), head_out, head_other, *weights)
            received = []
            for d in range(1, pairs):
                to_owner = []
                for s in range(n):
                    for slot in slots:
                        y, core = divmod(block(s, slot) // per_head, 2)
                        to_owner.append((s * heads + 2 * ((y + d) % pairs) + core, s * heads + 2 * y + core))
                received.append(lax.ppermute(sent, BOTH, to_owner))
            return kept, received, sent

        def add(g, shares, *before):
            nonlocal out
            (slots, chosen), at = groups[g], places[g]
            kept, received, _ = shares
            wide = part * len(chosen)
            tiles = pl.BlockSpec((tile, wide), lambda i, t: (i * t[at], 0))
            if by_columns:
                target = pl.BlockSpec((tile, wide), lambda i, t: (i * t[at], t[at + 1]))
            else:
                target = pl.BlockSpec((1, tile, wide), lambda i, t: (t[at + 1], i * t[at], 0))
            out = [
                call(
                    functools.partial(add_kernel, at=at, shares=len(received)),
                    "add_shares",
                    grid_spec=pltpu.PrefetchScalarGridSpec(
                        num_scalar_prefetch=1,
                        grid=(rows // tile,),
                        in_specs=[tiles] * (1 + len(received)) + [target] * len(out),
                        out_specs=target,
                    ),
                    out_shape=jax.ShapeDtypeStruct(out_dims, BF16),
                    input_output_aliases={2 + len(received): 0} if out else {},
                    cost_estimate=cost(2 * rows * wide, 10 * rows * wide),
                )(tie(table, *before), kept, *received, *out)
            ]

        waiting, last = [], [head_out]
        for g, (slots, chosen) in enumerate(groups):
            k, i = abs(slots[0]), chosen[0]
            arrival = []
            if k == 2 and slots[0] < 0:
                if half > 4:
                    send_on(3, None, *last)
                else:
                    for j in range(pieces):
                        send_on(3, j, *last)
            elif 2 < k < half - 1 and slots[0] < 0:
                arrival = there(k, None)
                if k + 1 < half - 1:
                    send_on(k + 1, None, *last)
                else:
                    for j in range(pieces):
                        send_on(k + 1, j, *last)
            elif k == half - 1 and (half, i) not in arrived:
                send_on(half, i, *last)
            shares = share(g, *last, *arrival)
            waiting.append((g, shares))
            last = [shares[2]]
            if len(waiting) > 2:
                add(*waiting.pop(0), *last)
                last = out
        for g, pending in waiting:
            add(g, pending)
        out = out[0]
        if not by_columns:
            out = jnp.transpose(out, (1, 0, 2)).reshape(rows, per_head * columns)
        return out

    return jax.shard_map(
        shards,
        mesh=mesh,
        in_specs=(
            P("seq", "head"),
            P("seq", "head"),
            P("seq", "head"),
            P("seq", "head"),
            P("head"),
            P("head", "seq"),
            P(),
        ),
        out_specs=P("seq", "head"),
        check_vma=False,
    )
```

time: 483 us -> 234 us (0.48)
  waiting for transfers between devices: 369 us -> 71.4 us
  Pallas kernels: 0 us -> 112 us
  matrix products: 49.5 us -> 0 us
  starting transfers between devices: 0.08 us -> 45.8 us
  other arithmetic: 18.2 us -> 0 us
  blocking collectives: 17 us -> 0 us
  between operations: 14.5 us -> 0.21 us
  local copies, waits for them, and re-layouts: 12.5 us -> 1.29 us
    all_gather x2 -> x0, waiting for transfers between devices: 187 us -> none  [the longest x1 147 us: shards(): lax.all_gather(out_weight, 'seq', axis=1, tiled=True)]
    reduce_scatter x1 -> x0, waiting for transfers between devices: 182 us -> none  [shards(): lax.psum_scatter(partial_terms, 'head', scatter_dimension=1, tiled=True)]
    pallas_call x0 -> x21, Pallas kernels: none -> 112 us  [the longest x7 48.8 us: share(): call(functools.partial(partial_kernel, slots=len(slots), at=at + 2), 'par...]
    ppermute x0 -> x22, waiting for transfers between devices: none -> 71.4 us  [the longest x10 35.1 us: send_on(): lax.ppermute(here, BOTH, along(source, step))]
    dot_general x5 -> x0, matrix products: 49.5 us -> none  [the longest x1 20.9 us: shards(): jnp.dot(head_out, lax.all_gather(out_weight, 'seq', axis=1, tiled=True),...]
    ppermute x0 -> x22, starting transfers between devices: none -> 45.8 us  [the longest x10 25.7 us: send_on(): lax.ppermute(here, BOTH, along(source, step))]
    unnamed x1 -> x0, blocking collectives: 17 us -> none
    convert_element_type x2 -> x0, other arithmetic: 9.07 us -> none  [the longest x1 4.83 us: shards(): return summed.astype(jnp.bfloat16)]
  transfers between devices with their start and end apart: 3 -> 22, of which waited for: 3 -> 11; matrix products, arithmetic and copies ran while one was open for 9% -> 1% of each run, Pallas kernels for 0% -> 46%
where the time goes in v1:
time: 234 us; the launch traced here: 231 us
  Pallas kernels  112 us (48%)
  waiting for transfers between devices  71.4 us (31%)
  starting transfers between devices  45.8 us (20%)
    pallas_call x7, Pallas kernels, share(): call(functools.partial(partial_kernel, slots=len(slots), at=at + 2), 'par...  48.8 us
    ppermute x10, waiting for transfers between devices, send_on(): lax.ppermute(here, BOTH, along(source, step))  35.1 us
    ppermute x10, starting transfers between devices, send_on(): lax.ppermute(here, BOTH, along(source, step))  25.7 us
    pallas_call x7, Pallas kernels, add(): call(functools.partial(add_kernel, at=at, shares=len(received)), 'add_sha...  23.9 us
    ppermute x7, waiting for transfers between devices, share(): received.append(lax.ppermute(sent, BOTH, to_owner))  15.7 us
    ppermute x2, waiting for transfers between devices, shards(): lax.ppermute(pair_state, 'seq', [(s, s + 2 * d) for s in range(n - 2 * d)])  14.9 us
    pallas_call x2, Pallas kernels, intra_of(): call(functools.partial(intra_kernel, tile=256), 'intra', grid=(count,), i...  14.5 us
    ppermute x7, starting transfers between devices, share(): received.append(lax.ppermute(sent, BOTH, to_owner))  14 us
  transfers between devices with their start and end apart: 22, of which 11 were waited for; matrix products, arithmetic and copies ran while one was open for 1% of the time, Pallas kernels for 46%

profile of v1, /device:TPU:26, one launch (start us, length us, event | category | flops | bytes accessed | tf_op | source)
XLA Modules:
  0.0 231.2 jit_solution(11893185308224021700)
XLA Ops:
  0.0 2.9 %collective-permute-start = (bf16[1024,768]{1,0:T(8,128)(2,1)}, bf16[1024,768]{1,0:T(8,128)(2,1)}, u32[]{:S(2)}, u32[]{:S(2)}) collective-permute-start(bf16[1024,768]{1,0:T(8,128)(2,1)} %mine_ref.1), channel_id=1, source_target_pairs={{1,0},{3,2},{5,4},{7,6},{8,9},{10,11},{12,13},{14,15},{17,16},{19,... | collective-permute-start | bytes 4718600 | tf_op jit(solution)/shard_map/ppermute | solution.py:326
  2.9 4.7 %summary.1.own_ref = bf16[8,128,128]{2,1,0:T(8,128)(2,1)} custom-call(s32[16]{0:T(128)} %lengths_ref.7, bf16[1024,1024]{1,0:T(8,128)(2,1)} %key_ref.5, bf16[1024,1024]{1,0:T(8,128)(2,1)} %value_ref.5), custom_call_target="tpu_custom_call" | custom-call | flops 65536 | bytes 1024 | tf_op jit(solution)/shard_map/summary/pallas_call | solution.py:276
  8.2 3.8 %merge.1.rest_0_ = bf16[2,2048,384]{2,1,0:T(8,128)(2,1)} custom-call(bf16[1024,768]{1,0:T(8,128)(2,1)} %mine_ref.1, bf16[1024,768]{1,0:T(8,128)(2,1)} %collective-permute-done.gathered_ref), custom_call_target="tpu_custom_call" | custom-call | flops 96 | bytes 1536 | tf_op jit(solution)/shard_map/merge/pallas_call | solution.py:327
  12.0 2.4 %collective-permute-done.1.other_ref = bf16[8,128,128]{2,1,0:T(8,128)(2,1)} collective-permute-done((bf16[8,128,128]{2,1,0:T(8,128)(2,1)}, bf16[8,128,128]{2,1,0:T(8,128)(2,1)}, u32[]{:S(2)}, u32[]{:S(2)}) %collective-permute-start.1) | collective-permute-done | bytes 262176 | tf_op jit(solution)/shard_map/ppermute | solution.py:335
  14.4 2.0 pair_state.1
  17.6 1.3 collective-permute-start.2
  18.9 14.9 %collective-permute-done.3.rest_1_ = bf16[8,128,128]{2,1,0:T(8,128)(2,1)} collective-permute-done((bf16[8,128,128]{2,1,0:T(8,128)(2,1)}, bf16[8,128,128]{2,1,0:T(8,128)(2,1)}, u32[]{:S(2)}, u32[]{:S(2)}) %collective-permute-start.3) | collective-permute-done | bytes 262176 | tf_op jit(solution)/shard_map/ppermute | solution.py:361
  33.9 2.3 collective-permute-start.5
  37.5 7.3 %intra.2.low_ref = f32[1024,512]{1,0:T(8,128)} custom-call(s32[16]{0:T(128)} %lengths_ref.7, bf16[1024,1024]{1,0:T(8,128)(2,1)} %query_ref.5, bf16[1024,1024]{1,0:T(8,128)(2,1)} %key_ref.5, bf16[1024,1024]{1,0:T(8,128)(2,1)} %value_ref.5), custom_call_target="tpu_custom_call" | custom-call | flops 524288 | bytes 1280 | tf_op jit(solution)/shard_map/intra/pallas_call | solution.py:339
  44.7 7.2 %intra.3.high_ref = f32[1024,512]{1,0:T(8,128)} custom-call(s32[16]{0:T(128)} %lengths_ref.7, bf16[1024,1024]{1,0:T(8,128)(2,1)} %query_ref.5, bf16[1024,1024]{1,0:T(8,128)(2,1)} %key_ref.5, bf16[1024,1024]{1,0:T(8,128)(2,1)} %value_ref.5), custom_call_target="tpu_custom_call" | custom-call | flops 524288 | bytes 1280 | tf_op jit(solution)/shard_map/intra/pallas_call | solution.py:339
  53.2 23.9 %collective-permute-done.6.rest_1_ = bf16[2,2048,384]{2,1,0:T(8,128)(2,1)} collective-permute-done((bf16[2,2048,384]{2,1,0:T(8,128)(2,1)}, bf16[2,2048,384]{2,1,0:T(8,128)(2,1)}, u32[]{:S(2)}, u32[]{:S(2)}) %collective-permute-start.6) | collective-permute-done | bytes 3145760 | tf_op jit(solution)/shard_map/ppermute | solution.py:321
  77.2 3.9 %collective-permute-start.8 = (bf16[2,2048,384]{2,1,0:T(8,128)(2,1)}, bf16[2,2048,384]{2,1,0:T(8,128)(2,1)}, u32[]{:S(2)}, u32[]{:S(2)}) collective-permute-start(bf16[2,2048,384]{2,1,0:T(8,128)(2,1)} %collective-permute-done.6.rest_1_), channel_id=1, source_target_pairs={{1,5},{3,7},{4,12},{6,14},{8,0},{10,2},{12,20},{14,22},{17,9},{19,... | collective-permute-start | bytes 9437192 | tf_op jit(solution)/shard_map/ppermute | solution.py:321
  81.1 8.8 %finish.1.own_ref = bf16[1024,1024]{1,0:T(8,128)(2,1)} custom-call(s32[16]{0:T(128)} %lengths_ref.7, bf16[1024,1024]{1,0:T(8,128)(2,1)} %query_ref.5, f32[1024,512]{1,0:T(8,128)} %intra.2.low_ref, f32[1024,512]{1,0:T(8,128)} %intra.3.high_ref, bf16[1024,1024]{1,0:T(8,128)(2,1)} %gate_ref.1, f32[1,1024]{1,0:T(1,128)} %bitcast.3, ...), custom_call_target="tpu_custom_call" | custom-call | flops 65536 | bytes 3072 | tf_op jit(solution)/shard_map/finish/pallas_call | solution.py:371
  90.0 1.3 dynamic-slice_bitcast_fusion.table_ref
  91.3 3.2 %collective-permute-done.4.other_ref = bf16[1024,1024]{1,0:T(8,128)(2,1)} collective-permute-done((bf16[1024,1024]{1,0:T(8,128)(2,1)}, bf16[1024,1024]{1,0:T(8,128)(2,1)}, u32[]{:S(2)}, u32[]{:S(2)}) %collective-permute-start.4) | collective-permute-done | bytes 2097184 | tf_op jit(solution)/shard_map/ppermute | solution.py:391
  94.5 3.7 %partial.7 = (bf16[1024,768]{1,0:T(8,128)(2,1)}, f32[1024,768]{1,0:T(8,128)}) custom-call(s32[25]{0:T(128)} %dynamic-slice_bitcast_fusion.table_ref, bf16[1024,1024]{1,0:T(8,128)(2,1)} %finish.1.own_ref, bf16[1024,1024]{1,0:T(8,128)(2,1)} %collective-permute-done.4.other_ref, bf16[2,2048,384]{2,1,0:T(8,128)(2,1)} %merge.1.rest_0_), custom_call_target="tpu_custom_call" | custom-call | flops 786432 | bytes 2944 | tf_op jit(solution)/shard_map/partial/pallas_call | solution.py:403
  98.2 1.8 collective-permute-start.9
  100.0 8.9 %partial.8 = (bf16[1024,768]{1,0:T(8,128)(2,1)}, f32[1024,768]{1,0:T(8,128)}) custom-call(s32[25]{0:T(128)} %dynamic-slice_bitcast_fusion.table_ref, bf16[1024,1024]{1,0:T(8,128)(2,1)} %finish.1.own_ref, bf16[1024,1024]{1,0:T(8,128)(2,1)} %collective-permute-done.4.other_ref, bf16[2,2048,384]{2,1,0:T(8,128)(2,1)} %collective-permute-done.5.rest_0_, ...), custom_call_target="tpu_custom_call" | custom-call | flops 786432 | bytes 2944 | tf_op jit(solution)/shard_map/partial/pallas_call | solution.py:403
  109.0 2.5 %collective-permute-done.7.rest_0_.refs_1_ = bf16[2,2048,384]{2,1,0:T(8,128)(2,1)} collective-permute-done((bf16[2,2048,384]{2,1,0:T(8,128)(2,1)}, bf16[2,2048,384]{2,1,0:T(8,128)(2,1)}, u32[]{:S(2)}, u32[]{:S(2)}) %collective-permute-start.7) | collective-permute-done | bytes 3145760 | tf_op jit(solution)/shard_map/ppermute | solution.py:321
  111.5 3.1 %collective-permute-done.8.rest_1_.refs_0_ = bf16[2,2048,384]{2,1,0:T(8,128)(2,1)} collective-permute-done((bf16[2,2048,384]{2,1,0:T(8,128)(2,1)}, bf16[2,2048,384]{2,1,0:T(8,128)(2,1)}, u32[]{:S(2)}, u32[]{:S(2)}) %collective-permute-start.8) | collective-permute-done | bytes 3145760 | tf_op jit(solution)/shard_map/ppermute | solution.py:321
  114.6 6.0 %split.1 = (bf16[1,2048,384]{2,1,0:T(8,128)(2,1)}, bf16[1,2048,384]{2,1,0:T(8,128)(2,1)}, bf16[1,2048,384]{2,1,0:T(8,128)(2,1)}, bf16[1,2048,384]{2,1,0:T(8,128)(2,1)}) custom-call(bf16[2,2048,384]{2,1,0:T(8,128)(2,1)} %collective-permute-done.8.rest_1_.refs_0_, bf16[2,2048,384]{2,1,0:T(8,128)(2,1)} %collective-permute-done.7.rest_0_.refs_1_), custom_call_target="tpu_custom_call" | custom-call | flops 192 | bytes 3072 | tf_op jit(solution)/shard_map/split/pallas_call | solution.py:311
  120.6 5.2 %collective-permute-start.10 = (bf16[1,2048,384]{2,1,0:T(8,128)(2,1)}, bf16[1,2048,384]{2,1,0:T(8,128)(2,1)}, u32[]{:S(2)}, u32[]{:S(2)}) collective-permute-start(bf16[1,2048,384]{2,1,0:T(8,128)(2,1)} %get-tuple-element.64), channel_id=1, source_target_pairs={{1,9},{3,11},{4,0},{6,2},{8,16},{10,18},{13,5},{15,7},{16,24},{18,... | collective-permute-start | bytes 4718600 | tf_op jit(solution)/shard_map/ppermute | solution.py:321
  127.1 4.6 %collective-permute-start.12 = (bf16[1024,768]{1,0:T(8,128)(2,1)}, bf16[1024,768]{1,0:T(8,128)(2,1)}, u32[]{:S(2)}, u32[]{:S(2)}) collective-permute-start(bf16[1024,768]{1,0:T(8,128)(2,1)} %get-tuple-element.54), channel_id=1, source_target_pairs={{2,0},{3,1},{7,5},{6,4},{10,8},{8,10},{12,14},{14,12},{19,17},{17,... | collective-permute-start | bytes 4718600 | tf_op jit(solution)/shard_map/ppermute | solution.py:423
  131.7 1.5 collective-permute-start.14
  133.2 8.9 %partial.9 = (bf16[1024,768]{1,0:T(8,128)(2,1)}, f32[1024,768]{1,0:T(8,128)}) custom-call(s32[25]{0:T(128)} %dynamic-slice_bitcast_fusion.table_ref, bf16[1024,1024]{1,0:T(8,128)(2,1)} %finish.1.own_ref, bf16[1024,1024]{1,0:T(8,128)(2,1)} %collective-permute-done.4.other_ref, bf16[2,2048,384]{2,1,0:T(8,128)(2,1)} %collective-permute-done.7.rest_0_.refs_1_, ...), custom_call_target="tpu_custom_call" | custom-call | flops 786432 | bytes 2944 | tf_op jit(solution)/shard_map/partial/pallas_call | solution.py:403
  142.0 5.8 %collective-permute-start.13 = (bf16[1,2048,384]{2,1,0:T(8,128)(2,1)}, bf16[1,2048,384]{2,1,0:T(8,128)(2,1)}, u32[]{:S(2)}, u32[]{:S(2)}) collective-permute-start(bf16[1,2048,384]{2,1,0:T(8,128)(2,1)} %get-tuple-element.70), channel_id=1, source_target_pairs={{1,9},{3,11},{4,0},{6,2},{8,16},{10,18},{13,5},{15,7},{16,24},{18,... | collective-permute-start | bytes 4718600 | tf_op jit(solution)/shard_map/ppermute | solution.py:321
  147.8 3.3 %add_shares.7.rest_1_ = bf16[1024,1536]{1,0:T(8,128)(2,1)} custom-call(s32[25]{0:T(128)} %dynamic-slice_bitcast_fusion.table_ref, f32[1024,768]{1,0:T(8,128)} %get-tuple-element.60.kept_ref, bf16[1024,768]{1,0:T(8,128)(2,1)} %collective-permute-done.9.rest_0_), custom_call_target="tpu_custom_call" | custom-call | flops 384 | bytes 1920 | tf_op jit(solution)/shard_map/add_shares/pallas_call | solution.py:437
  151.1 2.4 %collective-permute-start.15 = (bf16[1024,768]{1,0:T(8,128)(2,1)}, bf16[1024,768]{1,0:T(8,128)(2,1)}, u32[]{:S(2)}, u32[]{:S(2)}) collective-permute-start(bf16[1024,768]{1,0:T(8,128)(2,1)} %get-tuple-element.58), channel_id=1, source_target_pairs={{3,1},{0,2},{4,6},{7,5},{10,8},{9,11},{13,15},{14,12},{18,16},{17,... | collective-permute-start | bytes 4718600 | tf_op jit(solution)/shard_map/ppermute | solution.py:423
  154.9 6.8 %partial.10 = (bf16[1024,384]{1,0:T(8,128)(2,1)}, f32[1024,384]{1,0:T(8,128)}) custom-call(s32[25]{0:T(128)} %dynamic-slice_bitcast_fusion.table_ref, bf16[1024,1024]{1,0:T(8,128)(2,1)} %finish.1.own_ref, bf16[1024,1024]{1,0:T(8,128)(2,1)} %collective-permute-done.4.other_ref, bf16[1,2048,384]{2,1,0:T(8,128)(2,1)} %collective-permute-done.10.rest_0_, ...), custom_call_target="tpu_custom_call" | custom-call | flops 393216 | bytes 1984 | tf_op jit(solution)/shard_map/partial/pallas_call | solution.py:403
  161.7 3.5 %collective-permute-done.12.rest_0_ = bf16[1024,768]{1,0:T(8,128)(2,1)} collective-permute-done((bf16[1024,768]{1,0:T(8,128)(2,1)}, bf16[1024,768]{1,0:T(8,128)(2,1)}, u32[]{:S(2)}, u32[]{:S(2)}) %collective-permute-start.12) | collective-permute-done | bytes 1572896 | tf_op jit(solution)/shard_map/ppermute | solution.py:423
  165.2 3.6 %add_shares.8.rest_1_ = bf16[1024,1536]{1,0:T(8,128)(2,1)} custom-call(s32[25]{0:T(128)} %dynamic-slice_bitcast_fusion.table_ref, f32[1024,768]{1,0:T(8,128)} %get-tuple-element.68.kept_ref, bf16[1024,768]{1,0:T(8,128)(2,1)} %collective-permute-done.12.rest_0_, bf16[1024,1536]{1,0:T(8,128)(2,1)} %add_shares.7.rest_1_), custom_call_target="tpu_custom_call", output_to_operand_aliasing={{}: (3, {})} | custom-call | flops 384 | bytes 1920 | tf_op jit(solution)/shard_map/add_shares/pallas_call | solution.py:437
  168.8 1.9 collective-permute-start.18
  170.7 1.3 collective-permute-start.17
  172.0 5.6 %collective-permute-done.13.rest_0_ = bf16[1,2048,384]{2,1,0:T(8,128)(2,1)} collective-permute-done((bf16[1,2048,384]{2,1,0:T(8,128)(2,1)}, bf16[1,2048,384]{2,1,0:T(8,128)(2,1)}, u32[]{:S(2)}, u32[]{:S(2)}) %collective-permute-start.13) | collective-permute-done | bytes 1572896 | tf_op jit(solution)/shard_map/ppermute | solution.py:321
  177.6 6.9 %partial.11 = (bf16[1024,384]{1,0:T(8,128)(2,1)}, f32[1024,384]{1,0:T(8,128)}) custom-call(s32[25]{0:T(128)} %dynamic-slice_bitcast_fusion.table_ref, bf16[1024,1024]{1,0:T(8,128)(2,1)} %finish.1.own_ref, bf16[1024,1024]{1,0:T(8,128)(2,1)} %collective-permute-done.4.other_ref, bf16[1,2048,384]{2,1,0:T(8,128)(2,1)} %collective-permute-done.13.rest_0_, ...), custom_call_target="tpu_custom_call" | custom-call | flops 393216 | bytes 1984 | tf_op jit(solution)/shard_map/partial/pallas_call | solution.py:403
  184.4 1.3 collective-permute-start.21
  185.8 3.6 %add_shares.9.rest_1_ = bf16[1024,1536]{1,0:T(8,128)(2,1)} custom-call(s32[25]{0:T(128)} %dynamic-slice_bitcast_fusion.table_ref, f32[1024,768]{1,0:T(8,128)} %get-tuple-element.74.kept_ref, bf16[1024,768]{1,0:T(8,128)(2,1)} %collective-permute-done.15.rest_0_, bf16[1024,1536]{1,0:T(8,128)(2,1)} %add_shares.8.rest_1_), custom_call_target="tpu_custom_call", output_to_operand_aliasing={{}: (3, {})} | custom-call | flops 384 | bytes 1920 | tf_op jit(solution)/shard_map/add_shares/pallas_call | solution.py:437
  189.3 6.8 %partial.12 = (bf16[1024,384]{1,0:T(8,128)(2,1)}, f32[1024,384]{1,0:T(8,128)}) custom-call(s32[25]{0:T(128)} %dynamic-slice_bitcast_fusion.table_ref, bf16[1024,1024]{1,0:T(8,128)(2,1)} %finish.1.own_ref, bf16[1024,1024]{1,0:T(8,128)(2,1)} %collective-permute-done.4.other_ref, bf16[1,2048,384]{2,1,0:T(8,128)(2,1)} %collective-permute-done.16.rest_0_), custom_call_target="tpu_custom_call" | custom-call | flops 393216 | bytes 1984 | tf_op jit(solution)/shard_map/partial/pallas_call | solution.py:403
  196.1 1.3 collective-permute-start.20
  197.4 3.4 %add_shares.10.rest_1_ = bf16[1024,1536]{1,0:T(8,128)(2,1)} custom-call(s32[25]{0:T(128)} %dynamic-slice_bitcast_fusion.table_ref, f32[1024,384]{1,0:T(8,128)} %get-tuple-element.79.kept_ref, bf16[1024,384]{1,0:T(8,128)(2,1)} %collective-permute-done.17.rest_0_, bf16[1024,1536]{1,0:T(8,128)(2,1)} %add_shares.9.rest_1_), custom_call_target="tpu_custom_call", output_to_operand_aliasing={{}: (3, {})} | custom-call | flops 192 | bytes 960 | tf_op jit(solution)/shard_map/add_shares/pallas_call | solution.py:437
  200.8 6.8 %partial.13 = (bf16[1024,384]{1,0:T(8,128)(2,1)}, f32[1024,384]{1,0:T(8,128)}) custom-call(s32[25]{0:T(128)} %dynamic-slice_bitcast_fusion.table_ref, bf16[1024,1024]{1,0:T(8,128)(2,1)} %finish.1.own_ref, bf16[1024,1024]{1,0:T(8,128)(2,1)} %collective-permute-done.4.other_ref, bf16[1,2048,384]{2,1,0:T(8,128)(2,1)} %collective-permute-done.18.rest_0_), custom_call_target="tpu_custom_call" | custom-call | flops 393216 | bytes 1984 | tf_op jit(solution)/shard_map/partial/pallas_call | solution.py:403
  207.6 1.3 collective-permute-start.19
  208.9 1.9 collective-permute-done.21.rest_0_
  210.9 3.3 %add_shares.11.rest_1_ = bf16[1024,1536]{1,0:T(8,128)(2,1)} custom-call(s32[25]{0:T(128)} %dynamic-slice_bitcast_fusion.table_ref, f32[1024,384]{1,0:T(8,128)} %get-tuple-element.86.kept_ref, bf16[1024,384]{1,0:T(8,128)(2,1)} %collective-permute-done.21.rest_0_, bf16[1024,1536]{1,0:T(8,128)(2,1)} %add_shares.10.rest_1_), custom_call_target="tpu_custom_call", output_to_operand_aliasing={{}: (3, {})} | custom-call | flops 192 | bytes 960 | tf_op jit(solution)/shard_map/add_shares/pallas_call | solution.py:437
  214.2 5.2 %collective-permute-done.20.rest_0_ = bf16[1024,384]{1,0:T(8,128)(2,1)} collective-permute-done((bf16[1024,384]{1,0:T(8,128)(2,1)}, bf16[1024,384]{1,0:T(8,128)(2,1)}, u32[]{:S(2)}, u32[]{:S(2)}) %collective-permute-start.20) | collective-permute-done | bytes 786464 | tf_op jit(solution)/shard_map/ppermute | solution.py:423
  219.4 3.3 %add_shares.12.rest_1_ = bf16[1024,1536]{1,0:T(8,128)(2,1)} custom-call(s32[25]{0:T(128)} %dynamic-slice_bitcast_fusion.table_ref, f32[1024,384]{1,0:T(8,128)} %get-tuple-element.84.kept_ref, bf16[1024,384]{1,0:T(8,128)(2,1)} %collective-permute-done.20.rest_0_, bf16[1024,1536]{1,0:T(8,128)(2,1)} %add_shares.11.rest_1_), custom_call_target="tpu_custom_call", output_to_operand_aliasing={{}: (3, {})} | custom-call | flops 192 | bytes 960 | tf_op jit(solution)/shard_map/add_shares/pallas_call | solution.py:437
  222.7 5.1 %collective-permute-done.19.rest_0_ = bf16[1024,384]{1,0:T(8,128)(2,1)} collective-permute-done((bf16[1024,384]{1,0:T(8,128)(2,1)}, bf16[1024,384]{1,0:T(8,128)(2,1)}, u32[]{:S(2)}, u32[]{:S(2)}) %collective-permute-start.19) | collective-permute-done | bytes 786464 | tf_op jit(solution)/shard_map/ppermute | solution.py:423
  227.8 3.3 %add_shares.13 = bf16[1024,1536]{1,0:T(8,128)(2,1)} custom-call(s32[25]{0:T(128)} %dynamic-slice_bitcast_fusion.table_ref, f32[1024,384]{1,0:T(8,128)} %get-tuple-element.82.kept_ref, bf16[1024,384]{1,0:T(8,128)(2,1)} %collective-permute-done.19.rest_0_, bf16[1024,1536]{1,0:T(8,128)(2,1)} %add_shares.12.rest_1_), custom_call_target="tpu_custom_call", output_to_operand_aliasing={{}: (3, {})} | custom-call | flops 192 | bytes 960 | tf_op jit(solution)/shard_map/add_shares/pallas_call | solution.py:437
  (18 shorter events, 7.0 us)
Async XLA Ops:
  0.0 8.2 %collective-permute-start = (bf16[1024,768]{1,0:T(8,128)(2,1)}, bf16[1024,768]{1,0:T(8,128)(2,1)}, u32[]{:S(2)}, u32[]{:S(2)}) collective-permute-start(bf16[1024,768]{1,0:T(8,128)(2,1)} %mine_ref.1), channel_id=1, source_target_pairs={{1,0},{3,2},{5,4},{7,6},{8,9},{10,11},{12,13},{14,15},{17,16},{19,... | collective-permute-start | bytes 4718600 | tf_op jit(solution)/shard_map/ppermute | solution.py:326
  7.6 6.7 %collective-permute-start.1 = (bf16[8,128,128]{2,1,0:T(8,128)(2,1)}, bf16[8,128,128]{2,1,0:T(8,128)(2,1)}, u32[]{:S(2)}, u32[]{:S(2)}) collective-permute-start(bf16[8,128,128]{2,1,0:T(8,128)(2,1)} %summary.1.own_ref), channel_id=1, source_target_pairs={{0,4},{4,0},{8,12},{12,8},{16,20},{20,16},{24,28},{28,24},{1,5},{5... | collective-permute-start | bytes 786440 | tf_op jit(solution)/shard_map/ppermute | solution.py:335
  16.3 17.5 %collective-permute-start.3 = (bf16[8,128,128]{2,1,0:T(8,128)(2,1)}, bf16[8,128,128]{2,1,0:T(8,128)(2,1)}, u32[]{:S(2)}, u32[]{:S(2)}) collective-permute-start(bf16[8,128,128]{2,1,0:T(8,128)(2,1)} %pair_state.1), channel_id=1, source_target_pairs={{0,16},{4,20},{8,24},{12,28},{1,17},{5,21},{9,25},{13,29},{2,18},{... | collective-permute-start | bytes 786440 | tf_op jit(solution)/shard_map/ppermute | solution.py:361
  17.6 16.2 %collective-permute-start.2 = (bf16[8,128,128]{2,1,0:T(8,128)(2,1)}, bf16[8,128,128]{2,1,0:T(8,128)(2,1)}, u32[]{:S(2)}, u32[]{:S(2)}) collective-permute-start(bf16[8,128,128]{2,1,0:T(8,128)(2,1)} %pair_state.1), channel_id=1, source_target_pairs={{0,8},{4,12},{8,16},{12,20},{16,24},{20,28},{1,9},{5,13},{9,17},{1... | collective-permute-start | bytes 786440 | tf_op jit(solution)/shard_map/ppermute | solution.py:361
  33.9 18.1 %collective-permute-start.5 = (bf16[2,2048,384]{2,1,0:T(8,128)(2,1)}, bf16[2,2048,384]{2,1,0:T(8,128)(2,1)}, u32[]{:S(2)}, u32[]{:S(2)}) collective-permute-start(bf16[2,2048,384]{2,1,0:T(8,128)(2,1)} %merge.1.rest_0_), channel_id=1, source_target_pairs={{0,8},{2,10},{4,0},{6,2},{9,17},{11,19},{13,5},{15,7},{16,24},{18,... | collective-permute-start | bytes 9437192 | tf_op jit(solution)/shard_map/ppermute | solution.py:321
  36.2 41.0 %collective-permute-start.6 = (bf16[2,2048,384]{2,1,0:T(8,128)(2,1)}, bf16[2,2048,384]{2,1,0:T(8,128)(2,1)}, u32[]{:S(2)}, u32[]{:S(2)}) collective-permute-start(bf16[2,2048,384]{2,1,0:T(8,128)(2,1)} %merge.1.rest_0_), channel_id=1, source_target_pairs={{0,4},{2,6},{4,12},{6,14},{9,1},{11,3},{13,21},{15,23},{16,8},{18,... | collective-permute-start | bytes 9437192 | tf_op jit(solution)/shard_map/ppermute | solution.py:321
  51.9 59.5 %collective-permute-start.7 = (bf16[2,2048,384]{2,1,0:T(8,128)(2,1)}, bf16[2,2048,384]{2,1,0:T(8,128)(2,1)}, u32[]{:S(2)}, u32[]{:S(2)}) collective-permute-start(bf16[2,2048,384]{2,1,0:T(8,128)(2,1)} %collective-permute-done.5.rest_0_), channel_id=1, source_target_pairs={{0,8},{2,10},{5,1},{7,3},{8,16},{10,18},{12,4},{14,6},{17,25},{19,... | collective-permute-start | bytes 9437192 | tf_op jit(solution)/shard_map/ppermute | solution.py:321
  77.2 37.4 %collective-permute-start.8 = (bf16[2,2048,384]{2,1,0:T(8,128)(2,1)}, bf16[2,2048,384]{2,1,0:T(8,128)(2,1)}, u32[]{:S(2)}, u32[]{:S(2)}) collective-permute-start(bf16[2,2048,384]{2,1,0:T(8,128)(2,1)} %collective-permute-done.6.rest_1_), channel_id=1, source_target_pairs={{1,5},{3,7},{4,12},{6,14},{8,0},{10,2},{12,20},{14,22},{17,9},{19,... | collective-permute-start | bytes 9437192 | tf_op jit(solution)/shard_map/ppermute | solution.py:321
  90.0 4.5 %collective-permute-start.4 = (bf16[1024,1024]{1,0:T(8,128)(2,1)}, bf16[1024,1024]{1,0:T(8,128)(2,1)}, u32[]{:S(2)}, u32[]{:S(2)}) collective-permute-start(bf16[1024,1024]{1,0:T(8,128)(2,1)} %finish.1.own_ref), channel_id=1, source_target_pairs={{0,1},{1,0},{2,3},{3,2},{4,5},{5,4},{6,7},{7,6},{8,9},{9,8},{10,11... | collective-permute-start | bytes 6291464 | tf_op jit(solution)/shard_map/ppermute | solution.py:391
  98.2 43.8 %collective-permute-start.9 = (bf16[1024,768]{1,0:T(8,128)(2,1)}, bf16[1024,768]{1,0:T(8,128)(2,1)}, u32[]{:S(2)}, u32[]{:S(2)}) collective-permute-start(bf16[1024,768]{1,0:T(8,128)(2,1)} %get-tuple-element.51), channel_id=1, source_target_pairs={{2,0},{6,4},{11,9},{15,13},{16,18},{20,22},{25,27},{29,31}} | collective-permute-start | bytes 4718600 | tf_op jit(solution)/shard_map/ppermute | solution.py:423
  120.6 30.5 %collective-permute-start.10 = (bf16[1,2048,384]{2,1,0:T(8,128)(2,1)}, bf16[1,2048,384]{2,1,0:T(8,128)(2,1)}, u32[]{:S(2)}, u32[]{:S(2)}) collective-permute-start(bf16[1,2048,384]{2,1,0:T(8,128)(2,1)} %get-tuple-element.64), channel_id=1, source_target_pairs={{1,9},{3,11},{4,0},{6,2},{8,16},{10,18},{13,5},{15,7},{16,24},{18,... | collective-permute-start | bytes 4718600 | tf_op jit(solution)/shard_map/ppermute | solution.py:321
  125.8 27.8 %collective-permute-start.11 = (bf16[1,2048,384]{2,1,0:T(8,128)(2,1)}, bf16[1,2048,384]{2,1,0:T(8,128)(2,1)}, u32[]{:S(2)}, u32[]{:S(2)}) collective-permute-start(bf16[1,2048,384]{2,1,0:T(8,128)(2,1)} %get-tuple-element.65), channel_id=1, source_target_pairs={{0,4},{2,6},{5,13},{7,15},{9,1},{11,3},{12,20},{14,22},{17,9},{19,... | collective-permute-start | bytes 4718600 | tf_op jit(solution)/shard_map/ppermute | solution.py:321
  127.1 38.1 %collective-permute-start.12 = (bf16[1024,768]{1,0:T(8,128)(2,1)}, bf16[1024,768]{1,0:T(8,128)(2,1)}, u32[]{:S(2)}, u32[]{:S(2)}) collective-permute-start(bf16[1024,768]{1,0:T(8,128)(2,1)} %get-tuple-element.54), channel_id=1, source_target_pairs={{2,0},{3,1},{7,5},{6,4},{10,8},{8,10},{12,14},{14,12},{19,17},{17,... | collective-permute-start | bytes 4718600 | tf_op jit(solution)/shard_map/ppermute | solution.py:423
  131.7 37.1 %collective-permute-start.14 = (bf16[1,2048,384]{2,1,0:T(8,128)(2,1)}, bf16[1,2048,384]{2,1,0:T(8,128)(2,1)}, u32[]{:S(2)}, u32[]{:S(2)}) collective-permute-start(bf16[1,2048,384]{2,1,0:T(8,128)(2,1)} %get-tuple-element.71), channel_id=1, source_target_pairs={{0,4},{2,6},{5,13},{7,15},{9,1},{11,3},{12,20},{14,22},{17,9},{19,... | collective-permute-start | bytes 4718600 | tf_op jit(solution)/shard_map/ppermute | solution.py:321
  142.0 35.5 %collective-permute-start.13 = (bf16[1,2048,384]{2,1,0:T(8,128)(2,1)}, bf16[1,2048,384]{2,1,0:T(8,128)(2,1)}, u32[]{:S(2)}, u32[]{:S(2)}) collective-permute-start(bf16[1,2048,384]{2,1,0:T(8,128)(2,1)} %get-tuple-element.70), channel_id=1, source_target_pairs={{1,9},{3,11},{4,0},{6,2},{8,16},{10,18},{13,5},{15,7},{16,24},{18,... | collective-permute-start | bytes 4718600 | tf_op jit(solution)/shard_map/ppermute | solution.py:321
  151.1 34.6 %collective-permute-start.15 = (bf16[1024,768]{1,0:T(8,128)(2,1)}, bf16[1024,768]{1,0:T(8,128)(2,1)}, u32[]{:S(2)}, u32[]{:S(2)}) collective-permute-start(bf16[1024,768]{1,0:T(8,128)(2,1)} %get-tuple-element.58), channel_id=1, source_target_pairs={{3,1},{0,2},{4,6},{7,5},{10,8},{9,11},{13,15},{14,12},{18,16},{17,... | collective-permute-start | bytes 4718600 | tf_op jit(solution)/shard_map/ppermute | solution.py:423
  153.6 35.8 %collective-permute-start.16 = (bf16[1,2048,384]{2,1,0:T(8,128)(2,1)}, bf16[1,2048,384]{2,1,0:T(8,128)(2,1)}, u32[]{:S(2)}, u32[]{:S(2)}) collective-permute-start(bf16[1,2048,384]{2,1,0:T(8,128)(2,1)} %collective-permute-done.10.rest_0_), channel_id=1, source_target_pairs={{0,8},{2,10},{5,1},{7,3},{9,17},{11,19},{13,5},{15,7},{16,24},{18,... | collective-permute-start | bytes 4718600 | tf_op jit(solution)/shard_map/ppermute | solution.py:321
  168.8 32.0 %collective-permute-start.18 = (bf16[1,2048,384]{2,1,0:T(8,128)(2,1)}, bf16[1,2048,384]{2,1,0:T(8,128)(2,1)}, u32[]{:S(2)}, u32[]{:S(2)}) collective-permute-start(bf16[1,2048,384]{2,1,0:T(8,128)(2,1)} %collective-permute-done.14.rest_1_), channel_id=1, source_target_pairs={{1,5},{3,7},{4,12},{6,14},{9,1},{11,3},{13,21},{15,23},{16,8},{18,... | collective-permute-start | bytes 4718600 | tf_op jit(solution)/shard_map/ppermute | solution.py:321
  170.7 26.7 %collective-permute-start.17 = (bf16[1024,384]{1,0:T(8,128)(2,1)}, bf16[1024,384]{1,0:T(8,128)(2,1)}, u32[]{:S(2)}, u32[]{:S(2)}) collective-permute-start(bf16[1024,384]{1,0:T(8,128)(2,1)} %get-tuple-element.66), channel_id=1, source_target_pairs={{0,2},{1,3},{5,7},{4,6},{11,9},{9,11},{13,15},{15,13},{18,16},{16,... | collective-permute-start | bytes 2359304 | tf_op jit(solution)/shard_map/ppermute | solution.py:423
  184.4 26.4 %collective-permute-start.21 = (bf16[1024,384]{1,0:T(8,128)(2,1)}, bf16[1024,384]{1,0:T(8,128)(2,1)}, u32[]{:S(2)}, u32[]{:S(2)}) collective-permute-start(bf16[1024,384]{1,0:T(8,128)(2,1)} %get-tuple-element.72), channel_id=1, source_target_pairs={{0,2},{1,3},{5,7},{4,6},{11,9},{9,11},{13,15},{15,13},{18,16},{16,... | collective-permute-start | bytes 2359304 | tf_op jit(solution)/shard_map/ppermute | solution.py:423
  196.1 23.3 %collective-permute-start.20 = (bf16[1024,384]{1,0:T(8,128)(2,1)}, bf16[1024,384]{1,0:T(8,128)(2,1)}, u32[]{:S(2)}, u32[]{:S(2)}) collective-permute-start(bf16[1024,384]{1,0:T(8,128)(2,1)} %get-tuple-element.77), channel_id=1, source_target_pairs={{1,3},{5,7},{8,10},{12,14},{19,17},{23,21},{26,24},{30,28}} | collective-permute-start | bytes 2359304 | tf_op jit(solution)/shard_map/ppermute | solution.py:423
  207.6 20.2 %collective-permute-start.19 = (bf16[1024,384]{1,0:T(8,128)(2,1)}, bf16[1024,384]{1,0:T(8,128)(2,1)}, u32[]{:S(2)}, u32[]{:S(2)}) collective-permute-start(bf16[1024,384]{1,0:T(8,128)(2,1)} %get-tuple-element.83), channel_id=1, source_target_pairs={{1,3},{5,7},{8,10},{12,14},{19,17},{23,21},{26,24},{30,28}} | collective-permute-start | bytes 2359304 | tf_op jit(solution)/shard_map/ppermute | solution.py:423

commit v2 on v1

--- a/solution.py
+++ b/solution.py
@@ -144,7 +144,6 @@
 
 def partial_kernel(table_ref, own_ref, other_ref, *rest, slots, at):
     weights, (sent_ref, kept_ref, buffer_ref, sems) = rest[:slots], rest[slots:]
-    width = own_ref.shape[1]
     pieces, _, columns = weights[0].shape
 
     def copies(slot):
@@ -176,8 +175,8 @@
 
         @pl.when(role != 0)
         def _():
-            total = jnp.dot(own_ref[...], buffer_ref[slot, :width, :], preferred_element_type=F32)
-            total += jnp.dot(other_ref[...], buffer_ref[slot, width:, :], preferred_element_type=F32)
+            features = jnp.concatenate([own_ref[...], other_ref[...]], axis=1)
+            total = jnp.dot(features, buffer_ref[slot], preferred_element_type=F32)
 
             @pl.when(role == 1)
             def _():
@@ -188,19 +187,43 @@
                 sent_ref[...] = total.astype(BF16)
 
 
-def add_kernel(table_ref, kept_ref, *rest, at, shares):
-    received, out_ref = rest[:shares], rest[-1]
+def add_kernel(table_ref, kept_ref, *rest, at, shares, tile):
+    received, (out_ref, kept_buffer, buffers, sum_buffer, sems) = rest[:shares], rest[-5:]
+    rows, wide = kept_ref.shape
+    tiles = rows // tile
+    column = table_ref[at + 1]
+
+    def copies_in(t):
+        here = pl.ds(t * tile, tile)
+        return [pltpu.make_async_copy(kept_ref.at[here, :], kept_buffer.at[here, :], sems.at[t, 0])] + [
+            pltpu.make_async_copy(ref.at[here, :], buffers.at[i, here, :], sems.at[t, 1 + i])
+            for i, ref in enumerate(received)
+        ]
+
+    def copy_out(t):
+        here = pl.ds(t * tile, tile)
+        if len(out_ref.shape) == 2:
+            place = out_ref.at[here, pl.ds(pl.multiple_of(column * wide, 128), wide)]
+        else:
+            place = out_ref.at[column, here, :]
+        return pltpu.make_async_copy(sum_buffer.at[here, :], place, sems.at[t, 1 + shares])
 
     @pl.when(table_ref[at] == 1)
     def _():
-        total = kept_ref[...]
-        for ref in received:
-            total = total + ref[...].astype(F32)
-        out_ref[...] = total.astype(BF16).reshape(out_ref.shape)
-
-    @pl.when(table_ref[at] != 1)
-    def _():
-        out_ref[...] = rest[shares][...] if len(rest) > shares + 1 else jnp.zeros_like(out_ref)
+        for t in range(tiles):
+            for copy in copies_in(t):
+                copy.start()
+        for t in range(tiles):
+            for copy in copies_in(t):
+                copy.wait()
+            here = pl.ds(t * tile, tile)
+            total = kept_buffer[here, :]
+            for i in range(shares):
+                total = total + buffers[i, here, :].astype(F32)
+            sum_buffer[here, :] = total.astype(BF16)
+            copy_out(t).start()
+        for t in range(tiles):
+            copy_out(t).wait()
 
 
 def plan(n, heads, pieces):
@@ -333,6 +356,7 @@
         arrived[0, None] = merged
 
         other_state = lax.ppermute(summary, "seq", [(s, s ^ 1) for s in range(n)])
+        send_on(1, None, other_state)
 
         def intra_of(first, count, *before):
             block_at = pl.BlockSpec((rows, HS), lambda h: (0, first + h))
@@ -362,9 +386,8 @@
         ]
         intra_low = intra_of(0, count, pair_state)
         intra_high = intra_of(count, count, intra_low)
-        send_on(1, None, *earlier)
         for k in range(2, min(3, half - 1)):
-            send_on(k, None, intra_high)
+            send_on(k, None, intra_high, *earlier)
 
         low = pl.BlockSpec((rows, HS), lambda h: (0, jnp.minimum(h, count - 1)))
         high = pl.BlockSpec((rows, HS), lambda h: (0, jnp.maximum(h - count, 0)))
@@ -428,29 +451,30 @@
             (slots, chosen), at = groups[g], places[g]
             kept, received, _ = shares
             wide = part * len(chosen)
-            tiles = pl.BlockSpec((tile, wide), lambda i, t: (i * t[at], 0))
-            if by_columns:
-                target = pl.BlockSpec((tile, wide), lambda i, t: (i * t[at], t[at + 1]))
-            else:
-                target = pl.BlockSpec((1, tile, wide), lambda i, t: (t[at + 1], i * t[at], 0))
+            few = min(rows, 256)
             out = [
                 call(
-                    functools.partial(add_kernel, at=at, shares=len(received)),
+                    functools.partial(add_kernel, at=at, shares=len(received), tile=few),
                     "add_shares",
-                    grid_spec=pltpu.PrefetchScalarGridSpec(
-                        num_scalar_prefetch=1,
-                        grid=(rows // tile,),
-                        in_specs=[tiles] * (1 + len(received)) + [target] * len(out),
-                        out_specs=target,
-                    ),
+                    in_specs=[smem] + [anywhere] * (1 + len(received) + len(out)),
+                    out_specs=anywhere,
                     out_shape=jax.ShapeDtypeStruct(out_dims, BF16),
                     input_output_aliases={2 + len(received): 0} if out else {},
+                    scratch_shapes=[
+                        pltpu.VMEM((rows, wide), F32),
+                        pltpu.VMEM((len(received), rows, wide), BF16),
+                        pltpu.VMEM((rows, wide), BF16),
+                        pltpu.SemaphoreType.DMA((rows // few, 2 + len(received))),
+                    ],
                     cost_estimate=cost(2 * rows * wide, 10 * rows * wide),
                 )(tie(table, *before), kept, *received, *out)
             ]
 
         waiting, last = [], [head_out]
-        for g, (slots, chosen) in enumerate(groups):
+        near = [g for g, (slots, _) in enumerate(groups) if abs(slots[0]) == 1]
+        order = near + [g for g in range(len(groups)) if g not in near]
+        for g in order:
+            slots, chosen = groups[g]
             k, i = abs(slots[0]), chosen[0]
             arrival = []
             if k == 2 and slots[0] < 0:

time: 234 us -> 225 us (0.962)
  starting transfers between devices: 45.8 us -> 60 us
  waiting for transfers between devices: 71.4 us -> 58.9 us
  Pallas kernels: 112 us -> 103 us
    ppermute x10, waiting for transfers between devices: 35.1 us -> 5.75 us  [send_on(): lax.ppermute(here, BOTH, along(source, step))]
    ppermute x2, waiting for transfers between devices: 14.9 us -> 25.2 us  [shards(): lax.ppermute(pair_state, 'seq', [(s, s + 2 * d) for s in range(n - 2 * d)])]
    pallas_call x7, Pallas kernels: 23.9 us -> 14.7 us  [add(): call(functools.partial(add_kernel, at=at, shares=len(received), tile=few)...]
    ppermute x1, starting transfers between devices: 0.01 us -> 8.77 us  [shards(): lax.ppermute(head_out, 'head', [(h, h ^ 1) for h in range(heads)])]
    ppermute x7, waiting for transfers between devices: 15.7 us -> 22.7 us  [share(): received.append(lax.ppermute(sent, BOTH, to_owner))]
    ppermute x7, starting transfers between devices: 14 us -> 20.4 us  [share(): received.append(lax.ppermute(sent, BOTH, to_owner))]
  transfers between devices with their start and end apart: 22 -> 22, of which waited for: 11 -> 9; matrix products, arithmetic and copies ran while one was open for 1% -> 1% of each run, Pallas kernels for 46% -> 45%
where the time goes in v2:
time: 225 us; the launch traced here: 224 us
  Pallas kernels  103 us (46%)
  starting transfers between devices  60 us (27%)
  waiting for transfers between devices  58.9 us (26%)
    pallas_call x7, Pallas kernels, share(): call(functools.partial(partial_kernel, slots=len(slots), at=at + 2), 'par...  48.8 us
    ppermute x2, waiting for transfers between devices, shards(): lax.ppermute(pair_state, 'seq', [(s, s + 2 * d) for s in range(n - 2 * d)])  25.2 us
    ppermute x10, starting transfers between devices, send_on(): lax.ppermute(here, BOTH, along(source, step))  24.8 us
    ppermute x7, waiting for transfers between devices, share(): received.append(lax.ppermute(sent, BOTH, to_owner))  22.7 us
    ppermute x7, starting transfers between devices, share(): received.append(lax.ppermute(sent, BOTH, to_owner))  20.4 us
    pallas_call x7, Pallas kernels, add(): call(functools.partial(add_kernel, at=at, shares=len(received), tile=few)...  14.7 us
    pallas_call x2, Pallas kernels, intra_of(): call(functools.partial(intra_kernel, tile=256), 'intra', grid=(count,), i...  14.5 us
    pallas_call x1, Pallas kernels, shards(): call(functools.partial(finish_kernel, rows=rows, heads_low=count), 'finis...  8.83 us
  transfers between devices with their start and end apart: 22, of which 9 were waited for; matrix products, arithmetic and copies ran while one was open for 1% of the time, Pallas kernels for 45%

profile of v2, /device:TPU:26, one launch (start us, length us, event | category | flops | bytes accessed | tf_op | source)
XLA Modules:
  0.0 224.0 jit_solution(17597194805610455492)
XLA Ops:
  0.0 2.9 %collective-permute-start = (bf16[1024,768]{1,0:T(8,128)(2,1)}, bf16[1024,768]{1,0:T(8,128)(2,1)}, u32[]{:S(2)}, u32[]{:S(2)}) collective-permute-start(bf16[1024,768]{1,0:T(8,128)(2,1)} %mine_ref.1), channel_id=1, source_target_pairs={{1,0},{3,2},{5,4},{7,6},{8,9},{10,11},{12,13},{14,15},{17,16},{19,... | collective-permute-start | bytes 4718600 | tf_op jit(solution)/shard_map/ppermute | solution.py:349
  2.9 4.7 %summary.1.own_ref = bf16[8,128,128]{2,1,0:T(8,128)(2,1)} custom-call(s32[16]{0:T(128)} %lengths_ref.7, bf16[1024,1024]{1,0:T(8,128)(2,1)} %key_ref.5, bf16[1024,1024]{1,0:T(8,128)(2,1)} %value_ref.5), custom_call_target="tpu_custom_call" | custom-call | flops 65536 | bytes 1024 | tf_op jit(solution)/shard_map/summary/pallas_call | solution.py:299
  8.2 3.8 %merge.1.rest_0_ = bf16[2,2048,384]{2,1,0:T(8,128)(2,1)} custom-call(bf16[1024,768]{1,0:T(8,128)(2,1)} %mine_ref.1, bf16[1024,768]{1,0:T(8,128)(2,1)} %collective-permute-done.gathered_ref), custom_call_target="tpu_custom_call" | custom-call | flops 96 | bytes 1536 | tf_op jit(solution)/shard_map/merge/pallas_call | solution.py:350
  12.0 2.4 %collective-permute-done.1.other_ref = bf16[8,128,128]{2,1,0:T(8,128)(2,1)} collective-permute-done((bf16[8,128,128]{2,1,0:T(8,128)(2,1)}, bf16[8,128,128]{2,1,0:T(8,128)(2,1)}, u32[]{:S(2)}, u32[]{:S(2)}) %collective-permute-start.1) | collective-permute-done | bytes 262176 | tf_op jit(solution)/shard_map/ppermute | solution.py:358
  14.4 1.3 collective-permute-start.6
  15.7 2.3 %collective-permute-start.5 = (bf16[2,2048,384]{2,1,0:T(8,128)(2,1)}, bf16[2,2048,384]{2,1,0:T(8,128)(2,1)}, u32[]{:S(2)}, u32[]{:S(2)}) collective-permute-start(bf16[2,2048,384]{2,1,0:T(8,128)(2,1)} %merge.1.rest_0_), channel_id=1, source_target_pairs={{0,8},{2,10},{4,0},{6,2},{9,17},{11,19},{13,5},{15,7},{16,24},{18,... | collective-permute-start | bytes 9437192 | tf_op jit(solution)/shard_map/ppermute | solution.py:344
  18.0 2.0 pair_state.1
  19.9 1.3 collective-permute-start.3
  21.2 1.3 collective-permute-start.2
  22.5 7.3 %intra.2.low_ref = f32[1024,512]{1,0:T(8,128)} custom-call(s32[16]{0:T(128)} %lengths_ref.7, bf16[1024,1024]{1,0:T(8,128)(2,1)} %query_ref.5, bf16[1024,1024]{1,0:T(8,128)(2,1)} %key_ref.5, bf16[1024,1024]{1,0:T(8,128)(2,1)} %value_ref.5), custom_call_target="tpu_custom_call" | custom-call | flops 524288 | bytes 1280 | tf_op jit(solution)/shard_map/intra/pallas_call | solution.py:363
  29.8 7.3 %intra.3.high_ref = f32[1024,512]{1,0:T(8,128)} custom-call(s32[16]{0:T(128)} %lengths_ref.7, bf16[1024,1024]{1,0:T(8,128)(2,1)} %query_ref.5, bf16[1024,1024]{1,0:T(8,128)(2,1)} %key_ref.5, bf16[1024,1024]{1,0:T(8,128)(2,1)} %value_ref.5), custom_call_target="tpu_custom_call" | custom-call | flops 524288 | bytes 1280 | tf_op jit(solution)/shard_map/intra/pallas_call | solution.py:363
  37.0 25.2 %collective-permute-done.2.rest_0_ = bf16[8,128,128]{2,1,0:T(8,128)(2,1)} collective-permute-done((bf16[8,128,128]{2,1,0:T(8,128)(2,1)}, bf16[8,128,128]{2,1,0:T(8,128)(2,1)}, u32[]{:S(2)}, u32[]{:S(2)}) %collective-permute-start.2) | collective-permute-done | bytes 262176 | tf_op jit(solution)/shard_map/ppermute | solution.py:385
  62.3 6.4 %collective-permute-start.8 = (bf16[2,2048,384]{2,1,0:T(8,128)(2,1)}, bf16[2,2048,384]{2,1,0:T(8,128)(2,1)}, u32[]{:S(2)}, u32[]{:S(2)}) collective-permute-start(bf16[2,2048,384]{2,1,0:T(8,128)(2,1)} %collective-permute-done.6.rest_1_), channel_id=1, source_target_pairs={{1,5},{3,7},{4,12},{6,14},{8,0},{10,2},{12,20},{14,22},{17,9},{19,... | collective-permute-start | bytes 9437192 | tf_op jit(solution)/shard_map/ppermute | solution.py:344
  68.7 1.3 collective-permute-start.7
  70.0 8.8 %finish.1.own_ref = bf16[1024,1024]{1,0:T(8,128)(2,1)} custom-call(s32[16]{0:T(128)} %lengths_ref.7, bf16[1024,1024]{1,0:T(8,128)(2,1)} %query_ref.5, f32[1024,512]{1,0:T(8,128)} %intra.2.low_ref, f32[1024,512]{1,0:T(8,128)} %intra.3.high_ref, bf16[1024,1024]{1,0:T(8,128)(2,1)} %gate_ref.1, f32[1,1024]{1,0:T(1,128)} %bitcast.3, ...), custom_call_target="tpu_custom_call" | custom-call | flops 65536 | bytes 3072 | tf_op jit(solution)/shard_map/finish/pallas_call | solution.py:394
  78.8 8.8 %collective-permute-start.4 = (bf16[1024,1024]{1,0:T(8,128)(2,1)}, bf16[1024,1024]{1,0:T(8,128)(2,1)}, u32[]{:S(2)}, u32[]{:S(2)}) collective-permute-start(bf16[1024,1024]{1,0:T(8,128)(2,1)} %finish.1.own_ref), channel_id=1, source_target_pairs={{0,1},{1,0},{2,3},{3,2},{4,5},{5,4},{6,7},{7,6},{8,9},{9,8},{10,11... | collective-permute-start | bytes 6291464 | tf_op jit(solution)/shard_map/ppermute | solution.py:414
  87.6 1.3 dynamic-slice_bitcast_fusion.table_ref
  88.9 2.8 %collective-permute-done.4.other_ref = bf16[1024,1024]{1,0:T(8,128)(2,1)} collective-permute-done((bf16[1024,1024]{1,0:T(8,128)(2,1)}, bf16[1024,1024]{1,0:T(8,128)(2,1)}, u32[]{:S(2)}, u32[]{:S(2)}) %collective-permute-start.4) | collective-permute-done | bytes 2097184 | tf_op jit(solution)/shard_map/ppermute | solution.py:414
  91.7 8.9 %partial.7 = (bf16[1024,768]{1,0:T(8,128)(2,1)}, f32[1024,768]{1,0:T(8,128)}) custom-call(s32[25]{0:T(128)} %dynamic-slice_bitcast_fusion.table_ref, bf16[1024,1024]{1,0:T(8,128)(2,1)} %finish.1.own_ref, bf16[1024,1024]{1,0:T(8,128)(2,1)} %collective-permute-done.4.other_ref, bf16[2,2048,384]{2,1,0:T(8,128)(2,1)} %collective-permute-done.5.rest_0_, ...), custom_call_target="tpu_custom_call" | custom-call | flops 786432 | bytes 2944 | tf_op jit(solution)/shard_map/partial/pallas_call | solution.py:426
  100.6 4.6 %collective-permute-start.9 = (bf16[1024,768]{1,0:T(8,128)(2,1)}, bf16[1024,768]{1,0:T(8,128)(2,1)}, u32[]{:S(2)}, u32[]{:S(2)}) collective-permute-start(bf16[1024,768]{1,0:T(8,128)(2,1)} %get-tuple-element.52), channel_id=1, source_target_pairs={{2,0},{3,1},{7,5},{6,4},{10,8},{8,10},{12,14},{14,12},{19,17},{17,... | collective-permute-start | bytes 4718600 | tf_op jit(solution)/shard_map/ppermute | solution.py:446
  105.2 3.8 %partial.8 = (bf16[1024,768]{1,0:T(8,128)(2,1)}, f32[1024,768]{1,0:T(8,128)}) custom-call(s32[25]{0:T(128)} %dynamic-slice_bitcast_fusion.table_ref, bf16[1024,1024]{1,0:T(8,128)(2,1)} %finish.1.own_ref, bf16[1024,1024]{1,0:T(8,128)(2,1)} %collective-permute-done.4.other_ref, bf16[2,2048,384]{2,1,0:T(8,128)(2,1)} %merge.1.rest_0_), custom_call_target="tpu_custom_call" | custom-call | flops 786432 | bytes 2944 | tf_op jit(solution)/shard_map/partial/pallas_call | solution.py:426
  109.0 6.0 %split.1 = (bf16[1,2048,384]{2,1,0:T(8,128)(2,1)}, bf16[1,2048,384]{2,1,0:T(8,128)(2,1)}, bf16[1,2048,384]{2,1,0:T(8,128)(2,1)}, bf16[1,2048,384]{2,1,0:T(8,128)(2,1)}) custom-call(bf16[2,2048,384]{2,1,0:T(8,128)(2,1)} %collective-permute-done.8.rest_1_.refs_0_, bf16[2,2048,384]{2,1,0:T(8,128)(2,1)} %collective-permute-done.7.rest_0_.refs_1_), custom_call_target="tpu_custom_call" | custom-call | flops 192 | bytes 3072 | tf_op jit(solution)/shard_map/split/pallas_call | solution.py:334
  115.0 2.5 %collective-permute-start.10 = (bf16[1,2048,384]{2,1,0:T(8,128)(2,1)}, bf16[1,2048,384]{2,1,0:T(8,128)(2,1)}, u32[]{:S(2)}, u32[]{:S(2)}) collective-permute-start(bf16[1,2048,384]{2,1,0:T(8,128)(2,1)} %get-tuple-element.64), channel_id=1, source_target_pairs={{1,9},{3,11},{4,0},{6,2},{8,16},{10,18},{13,5},{15,7},{16,24},{18,... | collective-permute-start | bytes 4718600 | tf_op jit(solution)/shard_map/ppermute | solution.py:344
  117.5 1.3 collective-permute-start.11
  118.8 1.8 collective-permute-start.12
  120.6 1.5 collective-permute-start.14
  122.1 8.9 %partial.9 = (bf16[1024,768]{1,0:T(8,128)(2,1)}, f32[1024,768]{1,0:T(8,128)}) custom-call(s32[25]{0:T(128)} %dynamic-slice_bitcast_fusion.table_ref, bf16[1024,1024]{1,0:T(8,128)(2,1)} %finish.1.own_ref, bf16[1024,1024]{1,0:T(8,128)(2,1)} %collective-permute-done.4.other_ref, bf16[2,2048,384]{2,1,0:T(8,128)(2,1)} %collective-permute-done.7.rest_0_.refs_1_, ...), custom_call_target="tpu_custom_call" | custom-call | flops 786432 | bytes 2944 | tf_op jit(solution)/shard_map/partial/pallas_call | solution.py:426
  131.0 8.1 %collective-permute-done.9.rest_0_ = bf16[1024,768]{1,0:T(8,128)(2,1)} collective-permute-done((bf16[1024,768]{1,0:T(8,128)(2,1)}, bf16[1024,768]{1,0:T(8,128)(2,1)}, u32[]{:S(2)}, u32[]{:S(2)}) %collective-permute-start.9) | collective-permute-done | bytes 1572896 | tf_op jit(solution)/shard_map/ppermute | solution.py:446
  139.1 2.5 %collective-permute-start.13 = (bf16[1,2048,384]{2,1,0:T(8,128)(2,1)}, bf16[1,2048,384]{2,1,0:T(8,128)(2,1)}, u32[]{:S(2)}, u32[]{:S(2)}) collective-permute-start(bf16[1,2048,384]{2,1,0:T(8,128)(2,1)} %get-tuple-element.70), channel_id=1, source_target_pairs={{1,9},{3,11},{4,0},{6,2},{8,16},{10,18},{13,5},{15,7},{16,24},{18,... | collective-permute-start | bytes 4718600 | tf_op jit(solution)/shard_map/ppermute | solution.py:344
  142.3 8.8 %collective-permute-start.15 = (bf16[1024,768]{1,0:T(8,128)(2,1)}, bf16[1024,768]{1,0:T(8,128)(2,1)}, u32[]{:S(2)}, u32[]{:S(2)}) collective-permute-start(bf16[1024,768]{1,0:T(8,128)(2,1)} %get-tuple-element.58), channel_id=1, source_target_pairs={{3,1},{0,2},{4,6},{7,5},{10,8},{9,11},{13,15},{14,12},{18,16},{17,... | collective-permute-start | bytes 4718600 | tf_op jit(solution)/shard_map/ppermute | solution.py:446
  151.1 1.3 collective-permute-start.16
  152.4 6.9 %partial.10 = (bf16[1024,384]{1,0:T(8,128)(2,1)}, f32[1024,384]{1,0:T(8,128)}) custom-call(s32[25]{0:T(128)} %dynamic-slice_bitcast_fusion.table_ref, bf16[1024,1024]{1,0:T(8,128)(2,1)} %finish.1.own_ref, bf16[1024,1024]{1,0:T(8,128)(2,1)} %collective-permute-done.4.other_ref, bf16[1,2048,384]{2,1,0:T(8,128)(2,1)} %collective-permute-done.10.rest_0_, ...), custom_call_target="tpu_custom_call" | custom-call | flops 393216 | bytes 1984 | tf_op jit(solution)/shard_map/partial/pallas_call | solution.py:426
  160.1 4.6 %collective-permute-start.18 = (bf16[1,2048,384]{2,1,0:T(8,128)(2,1)}, bf16[1,2048,384]{2,1,0:T(8,128)(2,1)}, u32[]{:S(2)}, u32[]{:S(2)}) collective-permute-start(bf16[1,2048,384]{2,1,0:T(8,128)(2,1)} %collective-permute-done.14.rest_1_), channel_id=1, source_target_pairs={{1,5},{3,7},{4,12},{6,14},{9,1},{11,3},{13,21},{15,23},{16,8},{18,... | collective-permute-start | bytes 4718600 | tf_op jit(solution)/shard_map/ppermute | solution.py:344
  164.7 1.3 collective-permute-start.17
  166.3 6.9 %partial.11 = (bf16[1024,384]{1,0:T(8,128)(2,1)}, f32[1024,384]{1,0:T(8,128)}) custom-call(s32[25]{0:T(128)} %dynamic-slice_bitcast_fusion.table_ref, bf16[1024,1024]{1,0:T(8,128)(2,1)} %finish.1.own_ref, bf16[1024,1024]{1,0:T(8,128)(2,1)} %collective-permute-done.4.other_ref, bf16[1,2048,384]{2,1,0:T(8,128)(2,1)} %collective-permute-done.13.rest_0_, ...), custom_call_target="tpu_custom_call" | custom-call | flops 393216 | bytes 1984 | tf_op jit(solution)/shard_map/partial/pallas_call | solution.py:426
  173.2 1.3 collective-permute-start.21
  175.3 5.4 %collective-permute-done.16.rest_0_ = bf16[1,2048,384]{2,1,0:T(8,128)(2,1)} collective-permute-done((bf16[1,2048,384]{2,1,0:T(8,128)(2,1)}, bf16[1,2048,384]{2,1,0:T(8,128)(2,1)}, u32[]{:S(2)}, u32[]{:S(2)}) %collective-permute-start.16) | collective-permute-done | bytes 1572896 | tf_op jit(solution)/shard_map/ppermute | solution.py:344
  180.7 6.8 %partial.12 = (bf16[1024,384]{1,0:T(8,128)(2,1)}, f32[1024,384]{1,0:T(8,128)}) custom-call(s32[25]{0:T(128)} %dynamic-slice_bitcast_fusion.table_ref, bf16[1024,1024]{1,0:T(8,128)(2,1)} %finish.1.own_ref, bf16[1024,1024]{1,0:T(8,128)(2,1)} %collective-permute-done.4.other_ref, bf16[1,2048,384]{2,1,0:T(8,128)(2,1)} %collective-permute-done.16.rest_0_), custom_call_target="tpu_custom_call" | custom-call | flops 393216 | bytes 1984 | tf_op jit(solution)/shard_map/partial/pallas_call | solution.py:426
  187.4 1.3 collective-permute-start.20
  188.8 3.1 %add_shares.10.rest_1_ = bf16[1024,1536]{1,0:T(8,128)(2,1)} custom-call(s32[25]{0:T(128)} %dynamic-slice_bitcast_fusion.table_ref, f32[1024,384]{1,0:T(8,128)} %get-tuple-element.79.kept_ref, bf16[1024,384]{1,0:T(8,128)(2,1)} %collective-permute-done.17.rest_0_, bf16[1024,1536]{1,0:T(8,128)(2,1)} %add_shares.9.rest_1_), custom_call_target="tpu_custom_call", output_to_operand_aliasing={{}: (3, {})} | custom-call | flops 192 | bytes 960 | tf_op jit(solution)/shard_map/add_shares/pallas_call | solution.py:456
  191.9 6.8 %partial.13 = (bf16[1024,384]{1,0:T(8,128)(2,1)}, f32[1024,384]{1,0:T(8,128)}) custom-call(s32[25]{0:T(128)} %dynamic-slice_bitcast_fusion.table_ref, bf16[1024,1024]{1,0:T(8,128)(2,1)} %finish.1.own_ref, bf16[1024,1024]{1,0:T(8,128)(2,1)} %collective-permute-done.4.other_ref, bf16[1,2048,384]{2,1,0:T(8,128)(2,1)} %collective-permute-done.18.rest_0_), custom_call_target="tpu_custom_call" | custom-call | flops 393216 | bytes 1984 | tf_op jit(solution)/shard_map/partial/pallas_call | solution.py:426
  198.7 1.3 collective-permute-start.19
  200.0 3.9 %collective-permute-done.21.rest_0_ = bf16[1024,384]{1,0:T(8,128)(2,1)} collective-permute-done((bf16[1024,384]{1,0:T(8,128)(2,1)}, bf16[1024,384]{1,0:T(8,128)(2,1)}, u32[]{:S(2)}, u32[]{:S(2)}) %collective-permute-start.21) | collective-permute-done | bytes 786464 | tf_op jit(solution)/shard_map/ppermute | solution.py:446
  203.9 3.1 %add_shares.11.rest_1_ = bf16[1024,1536]{1,0:T(8,128)(2,1)} custom-call(s32[25]{0:T(128)} %dynamic-slice_bitcast_fusion.table_ref, f32[1024,384]{1,0:T(8,128)} %get-tuple-element.86.kept_ref, bf16[1024,384]{1,0:T(8,128)(2,1)} %collective-permute-done.21.rest_0_, bf16[1024,1536]{1,0:T(8,128)(2,1)} %add_shares.10.rest_1_), custom_call_target="tpu_custom_call", output_to_operand_aliasing={{}: (3, {})} | custom-call | flops 192 | bytes 960 | tf_op jit(solution)/shard_map/add_shares/pallas_call | solution.py:456
  207.0 5.3 %collective-permute-done.20.rest_0_ = bf16[1024,384]{1,0:T(8,128)(2,1)} collective-permute-done((bf16[1024,384]{1,0:T(8,128)(2,1)}, bf16[1024,384]{1,0:T(8,128)(2,1)}, u32[]{:S(2)}, u32[]{:S(2)}) %collective-permute-start.20) | collective-permute-done | bytes 786464 | tf_op jit(solution)/shard_map/ppermute | solution.py:446
  212.4 3.1 %add_shares.12.rest_1_ = bf16[1024,1536]{1,0:T(8,128)(2,1)} custom-call(s32[25]{0:T(128)} %dynamic-slice_bitcast_fusion.table_ref, f32[1024,384]{1,0:T(8,128)} %get-tuple-element.84.kept_ref, bf16[1024,384]{1,0:T(8,128)(2,1)} %collective-permute-done.20.rest_0_, bf16[1024,1536]{1,0:T(8,128)(2,1)} %add_shares.11.rest_1_), custom_call_target="tpu_custom_call", output_to_operand_aliasing={{}: (3, {})} | custom-call | flops 192 | bytes 960 | tf_op jit(solution)/shard_map/add_shares/pallas_call | solution.py:456
  215.5 5.3 %collective-permute-done.19.rest_0_ = bf16[1024,384]{1,0:T(8,128)(2,1)} collective-permute-done((bf16[1024,384]{1,0:T(8,128)(2,1)}, bf16[1024,384]{1,0:T(8,128)(2,1)}, u32[]{:S(2)}, u32[]{:S(2)}) %collective-permute-start.19) | collective-permute-done | bytes 786464 | tf_op jit(solution)/shard_map/ppermute | solution.py:446
  220.8 3.1 %add_shares.13 = bf16[1024,1536]{1,0:T(8,128)(2,1)} custom-call(s32[25]{0:T(128)} %dynamic-slice_bitcast_fusion.table_ref, f32[1024,384]{1,0:T(8,128)} %get-tuple-element.82.kept_ref, bf16[1024,384]{1,0:T(8,128)(2,1)} %collective-permute-done.19.rest_0_, bf16[1024,1536]{1,0:T(8,128)(2,1)} %add_shares.12.rest_1_), custom_call_target="tpu_custom_call", output_to_operand_aliasing={{}: (3, {})} | custom-call | flops 192 | bytes 960 | tf_op jit(solution)/shard_map/add_shares/pallas_call | solution.py:456
  (18 shorter events, 3.3 us)
Async XLA Ops:
  0.0 8.2 %collective-permute-start = (bf16[1024,768]{1,0:T(8,128)(2,1)}, bf16[1024,768]{1,0:T(8,128)(2,1)}, u32[]{:S(2)}, u32[]{:S(2)}) collective-permute-start(bf16[1024,768]{1,0:T(8,128)(2,1)} %mine_ref.1), channel_id=1, source_target_pairs={{1,0},{3,2},{5,4},{7,6},{8,9},{10,11},{12,13},{14,15},{17,16},{19,... | collective-permute-start | bytes 4718600 | tf_op jit(solution)/shard_map/ppermute | solution.py:349
  7.6 6.7 %collective-permute-start.1 = (bf16[8,128,128]{2,1,0:T(8,128)(2,1)}, bf16[8,128,128]{2,1,0:T(8,128)(2,1)}, u32[]{:S(2)}, u32[]{:S(2)}) collective-permute-start(bf16[8,128,128]{2,1,0:T(8,128)(2,1)} %summary.1.own_ref), channel_id=1, source_target_pairs={{0,4},{4,0},{8,12},{12,8},{16,20},{20,16},{24,28},{28,24},{1,5},{5... | collective-permute-start | bytes 786440 | tf_op jit(solution)/shard_map/ppermute | solution.py:358
  14.4 47.9 %collective-permute-start.6 = (bf16[2,2048,384]{2,1,0:T(8,128)(2,1)}, bf16[2,2048,384]{2,1,0:T(8,128)(2,1)}, u32[]{:S(2)}, u32[]{:S(2)}) collective-permute-start(bf16[2,2048,384]{2,1,0:T(8,128)(2,1)} %merge.1.rest_0_), channel_id=1, source_target_pairs={{0,4},{2,6},{4,12},{6,14},{9,1},{11,3},{13,21},{15,23},{16,8},{18,... | collective-permute-start | bytes 9437192 | tf_op jit(solution)/shard_map/ppermute | solution.py:344
  15.7 53.0 %collective-permute-start.5 = (bf16[2,2048,384]{2,1,0:T(8,128)(2,1)}, bf16[2,2048,384]{2,1,0:T(8,128)(2,1)}, u32[]{:S(2)}, u32[]{:S(2)}) collective-permute-start(bf16[2,2048,384]{2,1,0:T(8,128)(2,1)} %merge.1.rest_0_), channel_id=1, source_target_pairs={{0,8},{2,10},{4,0},{6,2},{9,17},{11,19},{13,5},{15,7},{16,24},{18,... | collective-permute-start | bytes 9437192 | tf_op jit(solution)/shard_map/ppermute | solution.py:344
  19.9 17.1 %collective-permute-start.3 = (bf16[8,128,128]{2,1,0:T(8,128)(2,1)}, bf16[8,128,128]{2,1,0:T(8,128)(2,1)}, u32[]{:S(2)}, u32[]{:S(2)}) collective-permute-start(bf16[8,128,128]{2,1,0:T(8,128)(2,1)} %pair_state.1), channel_id=1, source_target_pairs={{0,16},{4,20},{8,24},{12,28},{1,17},{5,21},{9,25},{13,29},{2,18},{... | collective-permute-start | bytes 786440 | tf_op jit(solution)/shard_map/ppermute | solution.py:385
  21.2 41.0 %collective-permute-start.2 = (bf16[8,128,128]{2,1,0:T(8,128)(2,1)}, bf16[8,128,128]{2,1,0:T(8,128)(2,1)}, u32[]{:S(2)}, u32[]{:S(2)}) collective-permute-start(bf16[8,128,128]{2,1,0:T(8,128)(2,1)} %pair_state.1), channel_id=1, source_target_pairs={{0,8},{4,12},{8,16},{12,20},{16,24},{20,28},{1,9},{5,13},{9,17},{1... | collective-permute-start | bytes 786440 | tf_op jit(solution)/shard_map/ppermute | solution.py:385
  62.3 46.7 %collective-permute-start.8 = (bf16[2,2048,384]{2,1,0:T(8,128)(2,1)}, bf16[2,2048,384]{2,1,0:T(8,128)(2,1)}, u32[]{:S(2)}, u32[]{:S(2)}) collective-permute-start(bf16[2,2048,384]{2,1,0:T(8,128)(2,1)} %collective-permute-done.6.rest_1_), channel_id=1, source_target_pairs={{1,5},{3,7},{4,12},{6,14},{8,0},{10,2},{12,20},{14,22},{17,9},{19,... | collective-permute-start | bytes 9437192 | tf_op jit(solution)/shard_map/ppermute | solution.py:344
  68.7 40.3 %collective-permute-start.7 = (bf16[2,2048,384]{2,1,0:T(8,128)(2,1)}, bf16[2,2048,384]{2,1,0:T(8,128)(2,1)}, u32[]{:S(2)}, u32[]{:S(2)}) collective-permute-start(bf16[2,2048,384]{2,1,0:T(8,128)(2,1)} %collective-permute-done.5.rest_0_), channel_id=1, source_target_pairs={{0,8},{2,10},{5,1},{7,3},{8,16},{10,18},{12,4},{14,6},{17,25},{19,... | collective-permute-start | bytes 9437192 | tf_op jit(solution)/shard_map/ppermute | solution.py:344
  78.8 12.9 %collective-permute-start.4 = (bf16[1024,1024]{1,0:T(8,128)(2,1)}, bf16[1024,1024]{1,0:T(8,128)(2,1)}, u32[]{:S(2)}, u32[]{:S(2)}) collective-permute-start(bf16[1024,1024]{1,0:T(8,128)(2,1)} %finish.1.own_ref), channel_id=1, source_target_pairs={{0,1},{1,0},{2,3},{3,2},{4,5},{5,4},{6,7},{7,6},{8,9},{9,8},{10,11... | collective-permute-start | bytes 6291464 | tf_op jit(solution)/shard_map/ppermute | solution.py:414
  100.6 38.5 %collective-permute-start.9 = (bf16[1024,768]{1,0:T(8,128)(2,1)}, bf16[1024,768]{1,0:T(8,128)(2,1)}, u32[]{:S(2)}, u32[]{:S(2)}) collective-permute-start(bf16[1024,768]{1,0:T(8,128)(2,1)} %get-tuple-element.52), channel_id=1, source_target_pairs={{2,0},{3,1},{7,5},{6,4},{10,8},{8,10},{12,14},{14,12},{19,17},{17,... | collective-permute-start | bytes 4718600 | tf_op jit(solution)/shard_map/ppermute | solution.py:446
  115.0 27.3 %collective-permute-start.10 = (bf16[1,2048,384]{2,1,0:T(8,128)(2,1)}, bf16[1,2048,384]{2,1,0:T(8,128)(2,1)}, u32[]{:S(2)}, u32[]{:S(2)}) collective-permute-start(bf16[1,2048,384]{2,1,0:T(8,128)(2,1)} %get-tuple-element.64), channel_id=1, source_target_pairs={{1,9},{3,11},{4,0},{6,2},{8,16},{10,18},{13,5},{15,7},{16,24},{18,... | collective-permute-start | bytes 4718600 | tf_op jit(solution)/shard_map/ppermute | solution.py:344
  117.5 33.6 %collective-permute-start.11 = (bf16[1,2048,384]{2,1,0:T(8,128)(2,1)}, bf16[1,2048,384]{2,1,0:T(8,128)(2,1)}, u32[]{:S(2)}, u32[]{:S(2)}) collective-permute-start(bf16[1,2048,384]{2,1,0:T(8,128)(2,1)} %get-tuple-element.65), channel_id=1, source_target_pairs={{0,4},{2,6},{5,13},{7,15},{9,1},{11,3},{12,20},{14,22},{17,9},{19,... | collective-permute-start | bytes 4718600 | tf_op jit(solution)/shard_map/ppermute | solution.py:344
  118.8 40.5 %collective-permute-start.12 = (bf16[1024,768]{1,0:T(8,128)(2,1)}, bf16[1024,768]{1,0:T(8,128)(2,1)}, u32[]{:S(2)}, u32[]{:S(2)}) collective-permute-start(bf16[1024,768]{1,0:T(8,128)(2,1)} %get-tuple-element.54), channel_id=1, source_target_pairs={{2,0},{6,4},{11,9},{15,13},{16,18},{20,22},{25,27},{29,31}} | collective-permute-start | bytes 4718600 | tf_op jit(solution)/shard_map/ppermute | solution.py:446
  120.6 39.5 %collective-permute-start.14 = (bf16[1,2048,384]{2,1,0:T(8,128)(2,1)}, bf16[1,2048,384]{2,1,0:T(8,128)(2,1)}, u32[]{:S(2)}, u32[]{:S(2)}) collective-permute-start(bf16[1,2048,384]{2,1,0:T(8,128)(2,1)} %get-tuple-element.71), channel_id=1, source_target_pairs={{0,4},{2,6},{5,13},{7,15},{9,1},{11,3},{12,20},{14,22},{17,9},{19,... | collective-permute-start | bytes 4718600 | tf_op jit(solution)/shard_map/ppermute | solution.py:344
  139.1 27.2 %collective-permute-start.13 = (bf16[1,2048,384]{2,1,0:T(8,128)(2,1)}, bf16[1,2048,384]{2,1,0:T(8,128)(2,1)}, u32[]{:S(2)}, u32[]{:S(2)}) collective-permute-start(bf16[1,2048,384]{2,1,0:T(8,128)(2,1)} %get-tuple-element.70), channel_id=1, source_target_pairs={{1,9},{3,11},{4,0},{6,2},{8,16},{10,18},{13,5},{15,7},{16,24},{18,... | collective-permute-start | bytes 4718600 | tf_op jit(solution)/shard_map/ppermute | solution.py:344
  142.3 32.1 %collective-permute-start.15 = (bf16[1024,768]{1,0:T(8,128)(2,1)}, bf16[1024,768]{1,0:T(8,128)(2,1)}, u32[]{:S(2)}, u32[]{:S(2)}) collective-permute-start(bf16[1024,768]{1,0:T(8,128)(2,1)} %get-tuple-element.58), channel_id=1, source_target_pairs={{3,1},{0,2},{4,6},{7,5},{10,8},{9,11},{13,15},{14,12},{18,16},{17,... | collective-permute-start | bytes 4718600 | tf_op jit(solution)/shard_map/ppermute | solution.py:446
  151.1 29.5 %collective-permute-start.16 = (bf16[1,2048,384]{2,1,0:T(8,128)(2,1)}, bf16[1,2048,384]{2,1,0:T(8,128)(2,1)}, u32[]{:S(2)}, u32[]{:S(2)}) collective-permute-start(bf16[1,2048,384]{2,1,0:T(8,128)(2,1)} %collective-permute-done.10.rest_0_), channel_id=1, source_target_pairs={{0,8},{2,10},{5,1},{7,3},{9,17},{11,19},{13,5},{15,7},{16,24},{18,... | collective-permute-start | bytes 4718600 | tf_op jit(solution)/shard_map/ppermute | solution.py:344
  160.1 31.8 %collective-permute-start.18 = (bf16[1,2048,384]{2,1,0:T(8,128)(2,1)}, bf16[1,2048,384]{2,1,0:T(8,128)(2,1)}, u32[]{:S(2)}, u32[]{:S(2)}) collective-permute-start(bf16[1,2048,384]{2,1,0:T(8,128)(2,1)} %collective-permute-done.14.rest_1_), channel_id=1, source_target_pairs={{1,5},{3,7},{4,12},{6,14},{9,1},{11,3},{13,21},{15,23},{16,8},{18,... | collective-permute-start | bytes 4718600 | tf_op jit(solution)/shard_map/ppermute | solution.py:344
  164.7 24.1 %collective-permute-start.17 = (bf16[1024,384]{1,0:T(8,128)(2,1)}, bf16[1024,384]{1,0:T(8,128)(2,1)}, u32[]{:S(2)}, u32[]{:S(2)}) collective-permute-start(bf16[1024,384]{1,0:T(8,128)(2,1)} %get-tuple-element.66), channel_id=1, source_target_pairs={{0,2},{1,3},{5,7},{4,6},{11,9},{9,11},{13,15},{15,13},{18,16},{16,... | collective-permute-start | bytes 2359304 | tf_op jit(solution)/shard_map/ppermute | solution.py:446
  173.2 30.7 %collective-permute-start.21 = (bf16[1024,384]{1,0:T(8,128)(2,1)}, bf16[1024,384]{1,0:T(8,128)(2,1)}, u32[]{:S(2)}, u32[]{:S(2)}) collective-permute-start(bf16[1024,384]{1,0:T(8,128)(2,1)} %get-tuple-element.72), channel_id=1, source_target_pairs={{0,2},{1,3},{5,7},{4,6},{11,9},{9,11},{13,15},{15,13},{18,16},{16,... | collective-permute-start | bytes 2359304 | tf_op jit(solution)/shard_map/ppermute | solution.py:446
  187.4 24.9 %collective-permute-start.20 = (bf16[1024,384]{1,0:T(8,128)(2,1)}, bf16[1024,384]{1,0:T(8,128)(2,1)}, u32[]{:S(2)}, u32[]{:S(2)}) collective-permute-start(bf16[1024,384]{1,0:T(8,128)(2,1)} %get-tuple-element.77), channel_id=1, source_target_pairs={{1,3},{5,7},{8,10},{12,14},{19,17},{23,21},{26,24},{30,28}} | collective-permute-start | bytes 2359304 | tf_op jit(solution)/shard_map/ppermute | solution.py:446
  198.7 22.1 %collective-permute-start.19 = (bf16[1024,384]{1,0:T(8,128)(2,1)}, bf16[1024,384]{1,0:T(8,128)(2,1)}, u32[]{:S(2)}, u32[]{:S(2)}) collective-permute-start(bf16[1024,384]{1,0:T(8,128)(2,1)} %get-tuple-element.83), channel_id=1, source_target_pairs={{1,3},{5,7},{8,10},{12,14},{19,17},{23,21},{26,24},{30,28}} | collective-permute-start | bytes 2359304 | tf_op jit(solution)/shard_map/ppermute | solution.py:446

commit v3 on v2

--- a/solution.py
+++ b/solution.py
@@ -113,18 +113,20 @@
         scalars_ref[1] = end
 
     before, end = scalars_ref[0], scalars_ref[1]
-    incoming = odd.astype(F32) * other_ref[0].astype(F32)
-    for j, pair_ref in enumerate(pair_refs):
-        live = (before < pair_first - j * 2 * rows).astype(F32)
-        incoming = incoming + live * pair_ref[0].astype(F32)
-    carried = incoming.astype(BF16)
-    inter = jnp.dot(query_ref[...], carried, preferred_element_type=F32)
     inside = lax.broadcasted_iota(jnp.int32, (rows, HS), 0) < end - first_pos
-    intra = jnp.where(pl.program_id(0) < heads_low, low_ref[...], high_ref[...])
-    a = intra + jnp.where(inside, inter, 0.0)
-    scale = lax.rsqrt(jnp.mean(a * a, axis=-1, keepdims=True) + EPS)
-    gate = jax.nn.sigmoid(gate_ref[...].astype(F32))
-    out_ref[...] = (a * scale * gain_ref[...] * gate).astype(BF16)
+    is_low = pl.program_id(0) < heads_low
+    for h in range(other_ref.shape[0]):
+        at = slice(h * HS, (h + 1) * HS)
+        incoming = odd.astype(F32) * other_ref[h].astype(F32)
+        for j, pair_ref in enumerate(pair_refs):
+            live = (before < pair_first - j * 2 * rows).astype(F32)
+            incoming = incoming + live * pair_ref[h].astype(F32)
+        inter = jnp.dot(query_ref[:, at], incoming.astype(BF16), preferred_element_type=F32)
+        intra = jnp.where(is_low, low_ref[:, at], high_ref[:, at])
+        a = intra + jnp.where(inside, inter, 0.0)
+        scale = lax.rsqrt(jnp.mean(a * a, axis=-1, keepdims=True) + EPS)
+        gate = jax.nn.sigmoid(gate_ref[:, at].astype(F32))
+        out_ref[:, at] = (a * scale * gain_ref[:, at] * gate).astype(BF16)
 
 
 def merge_kernel(mine_ref, gathered_ref, out_ref):
@@ -384,20 +386,21 @@
         earlier = [
             lax.ppermute(pair_state, "seq", [(s, s + 2 * d) for s in range(n - 2 * d)]) for d in range(1, n // 4 + 1)
         ]
-        intra_low = intra_of(0, count, pair_state)
+        intra_low = intra_of(0, count, pair_state, table)
         intra_high = intra_of(count, count, intra_low)
         for k in range(2, min(3, half - 1)):
             send_on(k, None, intra_high, *earlier)
 
-        low = pl.BlockSpec((rows, HS), lambda h: (0, jnp.minimum(h, count - 1)))
-        high = pl.BlockSpec((rows, HS), lambda h: (0, jnp.maximum(h - count, 0)))
+        low = pl.BlockSpec((rows, 2 * HS), lambda h: (0, jnp.minimum(h, count // 2 - 1)))
+        high = pl.BlockSpec((rows, 2 * HS), lambda h: (0, jnp.maximum(h - count // 2, 0)))
+        two_states = pl.BlockSpec((2, HS, HS), lambda h: (h, 0, 0))
         head_out = call(
-            functools.partial(finish_kernel, rows=rows, heads_low=count),
+            functools.partial(finish_kernel, rows=rows, heads_low=count // 2),
             "finish",
-            grid=(heads_here,),
-            in_specs=[smem, head_block, low, high, head_block, pl.BlockSpec((1, HS), lambda h: (0, h)), state_block]
-            + [state_block] * len(earlier),
-            out_specs=head_block,
+            grid=(heads_here // 2,),
+            in_specs=[smem, two_heads, low, high, two_heads, pl.BlockSpec((1, 2 * HS), lambda h: (0, h)), two_states]
+            + [two_states] * len(earlier),
+            out_specs=two_heads,
             out_shape=jax.ShapeDtypeStruct((rows, width), BF16),
             scratch_shapes=[pltpu.SMEM((2,), jnp.int32)],
             cost_estimate=cost(2 * rows * width * HS, 12 * rows * width),

time: 225 us -> 224 us (level)
    ppermute x7, waiting for transfers between devices: 22.7 us -> 19.8 us  [share(): received.append(lax.ppermute(sent, BOTH, to_owner))]
    ppermute x10, waiting for transfers between devices: 5.75 us -> 8.64 us  [send_on(): lax.ppermute(here, BOTH, along(source, step))]
  transfers between devices with their start and end apart: 22 -> 22, of which waited for: 9 -> 9; matrix products, arithmetic and copies ran while one was open for 1% -> 1% of each run, Pallas kernels for 45% -> 44%
where the time goes in v3:
time: 224 us; the launch traced here: 222 us
  Pallas kernels  101 us (45%)
  starting transfers between devices  60.1 us (27%)
  waiting for transfers between devices  58.9 us (26%)
    pallas_call x7, Pallas kernels, share(): call(functools.partial(partial_kernel, slots=len(slots), at=at + 2), 'par...  48.8 us
    ppermute x10, starting transfers between devices, send_on(): lax.ppermute(here, BOTH, along(source, step))  24.8 us
    ppermute x2, waiting for transfers between devices, shards(): lax.ppermute(pair_state, 'seq', [(s, s + 2 * d) for s in range(n - 2 * d)])  24 us
    ppermute x7, starting transfers between devices, share(): received.append(lax.ppermute(sent, BOTH, to_owner))  20.5 us
    ppermute x7, waiting for transfers between devices, share(): received.append(lax.ppermute(sent, BOTH, to_owner))  19.8 us
    pallas_call x7, Pallas kernels, add(): call(functools.partial(add_kernel, at=at, shares=len(received), tile=few)...  14.7 us
    pallas_call x2, Pallas kernels, intra_of(): call(functools.partial(intra_kernel, tile=256), 'intra', grid=(count,), i...  14.5 us
    ppermute x1, starting transfers between devices, shards(): lax.ppermute(head_out, 'head', [(h, h ^ 1) for h in range(heads)])  8.81 us
  transfers between devices with their start and end apart: 22, of which 9 were waited for; matrix products, arithmetic and copies ran while one was open for 1% of the time, Pallas kernels for 44%

profile of v3, /device:TPU:26, one launch (start us, length us, event | category | flops | bytes accessed | tf_op | source)
XLA Modules:
  0.0 222.2 jit_solution(12767486410056237152)
XLA Ops:
  0.0 2.9 %collective-permute-start = (bf16[1024,768]{1,0:T(8,128)(2,1)}, bf16[1024,768]{1,0:T(8,128)(2,1)}, u32[]{:S(2)}, u32[]{:S(2)}) collective-permute-start(bf16[1024,768]{1,0:T(8,128)(2,1)} %mine_ref.1), channel_id=1, source_target_pairs={{1,0},{3,2},{5,4},{7,6},{8,9},{10,11},{12,13},{14,15},{17,16},{19,... | collective-permute-start | bytes 4718600 | tf_op jit(solution)/shard_map/ppermute | solution.py:351
  2.9 4.7 %summary.1.own_ref = bf16[8,128,128]{2,1,0:T(8,128)(2,1)} custom-call(s32[16]{0:T(128)} %lengths_ref.7, bf16[1024,1024]{1,0:T(8,128)(2,1)} %key_ref.5, bf16[1024,1024]{1,0:T(8,128)(2,1)} %value_ref.5), custom_call_target="tpu_custom_call" | custom-call | flops 65536 | bytes 1024 | tf_op jit(solution)/shard_map/summary/pallas_call | solution.py:301
  8.2 3.8 %merge.1.rest_0_ = bf16[2,2048,384]{2,1,0:T(8,128)(2,1)} custom-call(bf16[1024,768]{1,0:T(8,128)(2,1)} %mine_ref.1, bf16[1024,768]{1,0:T(8,128)(2,1)} %collective-permute-done.gathered_ref), custom_call_target="tpu_custom_call" | custom-call | flops 96 | bytes 1536 | tf_op jit(solution)/shard_map/merge/pallas_call | solution.py:352
  12.0 2.4 %collective-permute-done.1.other_ref = bf16[8,128,128]{2,1,0:T(8,128)(2,1)} collective-permute-done((bf16[8,128,128]{2,1,0:T(8,128)(2,1)}, bf16[8,128,128]{2,1,0:T(8,128)(2,1)}, u32[]{:S(2)}, u32[]{:S(2)}) %collective-permute-start.1) | collective-permute-done | bytes 262176 | tf_op jit(solution)/shard_map/ppermute | solution.py:360
  14.4 1.3 collective-permute-start.6
  15.7 2.3 %collective-permute-start.5 = (bf16[2,2048,384]{2,1,0:T(8,128)(2,1)}, bf16[2,2048,384]{2,1,0:T(8,128)(2,1)}, u32[]{:S(2)}, u32[]{:S(2)}) collective-permute-start(bf16[2,2048,384]{2,1,0:T(8,128)(2,1)} %merge.1.rest_0_), channel_id=1, source_target_pairs={{0,8},{2,10},{4,0},{6,2},{9,17},{11,19},{13,5},{15,7},{16,24},{18,... | collective-permute-start | bytes 9437192 | tf_op jit(solution)/shard_map/ppermute | solution.py:346
  18.0 2.0 pair_state.1
  19.9 1.3 collective-permute-start.3
  21.2 1.3 collective-permute-start.2
  22.5 1.3 dynamic-slice_bitcast_fusion.table_ref
  23.8 7.2 %intra.2.low_ref = f32[1024,512]{1,0:T(8,128)} custom-call(s32[16]{0:T(128)} %lengths_ref.7, bf16[1024,1024]{1,0:T(8,128)(2,1)} %query_ref.5, bf16[1024,1024]{1,0:T(8,128)(2,1)} %key_ref.5, bf16[1024,1024]{1,0:T(8,128)(2,1)} %value_ref.5), custom_call_target="tpu_custom_call" | custom-call | flops 524288 | bytes 1280 | tf_op jit(solution)/shard_map/intra/pallas_call | solution.py:365
  31.0 7.3 %intra.3.high_ref = f32[1024,512]{1,0:T(8,128)} custom-call(s32[16]{0:T(128)} %lengths_ref.7, bf16[1024,1024]{1,0:T(8,128)(2,1)} %query_ref.5, bf16[1024,1024]{1,0:T(8,128)(2,1)} %key_ref.5, bf16[1024,1024]{1,0:T(8,128)(2,1)} %value_ref.5), custom_call_target="tpu_custom_call" | custom-call | flops 524288 | bytes 1280 | tf_op jit(solution)/shard_map/intra/pallas_call | solution.py:365
  38.3 24.0 %collective-permute-done.2.rest_0_ = bf16[8,128,128]{2,1,0:T(8,128)(2,1)} collective-permute-done((bf16[8,128,128]{2,1,0:T(8,128)(2,1)}, bf16[8,128,128]{2,1,0:T(8,128)(2,1)}, u32[]{:S(2)}, u32[]{:S(2)}) %collective-permute-start.2) | collective-permute-done | bytes 262176 | tf_op jit(solution)/shard_map/ppermute | solution.py:387
  62.3 6.4 %collective-permute-start.8 = (bf16[2,2048,384]{2,1,0:T(8,128)(2,1)}, bf16[2,2048,384]{2,1,0:T(8,128)(2,1)}, u32[]{:S(2)}, u32[]{:S(2)}) collective-permute-start(bf16[2,2048,384]{2,1,0:T(8,128)(2,1)} %collective-permute-done.6.rest_1_), channel_id=1, source_target_pairs={{1,5},{3,7},{4,12},{6,14},{8,0},{10,2},{12,20},{14,22},{17,9},{19,... | collective-permute-start | bytes 9437192 | tf_op jit(solution)/shard_map/ppermute | solution.py:346
  68.7 1.3 collective-permute-start.7
  70.0 6.9 %finish.1.own_ref = bf16[1024,1024]{1,0:T(8,128)(2,1)} custom-call(s32[16]{0:T(128)} %lengths_ref.7, bf16[1024,1024]{1,0:T(8,128)(2,1)} %query_ref.5, f32[1024,512]{1,0:T(8,128)} %intra.2.low_ref, f32[1024,512]{1,0:T(8,128)} %intra.3.high_ref, bf16[1024,1024]{1,0:T(8,128)(2,1)} %gate_ref.1, f32[1,1024]{1,0:T(1,128)} %bitcast.3, ...), custom_call_target="tpu_custom_call" | custom-call | flops 65536 | bytes 3072 | tf_op jit(solution)/shard_map/finish/pallas_call | solution.py:397
  76.9 8.8 %collective-permute-start.4 = (bf16[1024,1024]{1,0:T(8,128)(2,1)}, bf16[1024,1024]{1,0:T(8,128)(2,1)}, u32[]{:S(2)}, u32[]{:S(2)}) collective-permute-start(bf16[1024,1024]{1,0:T(8,128)(2,1)} %finish.1.own_ref), channel_id=1, source_target_pairs={{0,1},{1,0},{2,3},{3,2},{4,5},{5,4},{6,7},{7,6},{8,9},{9,8},{10,11... | collective-permute-start | bytes 6291464 | tf_op jit(solution)/shard_map/ppermute | solution.py:417
  85.7 4.1 %collective-permute-done.4.other_ref = bf16[1024,1024]{1,0:T(8,128)(2,1)} collective-permute-done((bf16[1024,1024]{1,0:T(8,128)(2,1)}, bf16[1024,1024]{1,0:T(8,128)(2,1)}, u32[]{:S(2)}, u32[]{:S(2)}) %collective-permute-start.4) | collective-permute-done | bytes 2097184 | tf_op jit(solution)/shard_map/ppermute | solution.py:417
  89.9 8.9 %partial.7 = (bf16[1024,768]{1,0:T(8,128)(2,1)}, f32[1024,768]{1,0:T(8,128)}) custom-call(s32[25]{0:T(128)} %dynamic-slice_bitcast_fusion.table_ref, bf16[1024,1024]{1,0:T(8,128)(2,1)} %finish.1.own_ref, bf16[1024,1024]{1,0:T(8,128)(2,1)} %collective-permute-done.4.other_ref, bf16[2,2048,384]{2,1,0:T(8,128)(2,1)} %collective-permute-done.5.rest_0_, ...), custom_call_target="tpu_custom_call" | custom-call | flops 786432 | bytes 2944 | tf_op jit(solution)/shard_map/partial/pallas_call | solution.py:429
  98.7 4.6 %collective-permute-start.9 = (bf16[1024,768]{1,0:T(8,128)(2,1)}, bf16[1024,768]{1,0:T(8,128)(2,1)}, u32[]{:S(2)}, u32[]{:S(2)}) collective-permute-start(bf16[1024,768]{1,0:T(8,128)(2,1)} %get-tuple-element.52), channel_id=1, source_target_pairs={{2,0},{3,1},{7,5},{6,4},{10,8},{8,10},{12,14},{14,12},{19,17},{17,... | collective-permute-start | bytes 4718600 | tf_op jit(solution)/shard_map/ppermute | solution.py:449
  103.4 3.7 %partial.8 = (bf16[1024,768]{1,0:T(8,128)(2,1)}, f32[1024,768]{1,0:T(8,128)}) custom-call(s32[25]{0:T(128)} %dynamic-slice_bitcast_fusion.table_ref, bf16[1024,1024]{1,0:T(8,128)(2,1)} %finish.1.own_ref, bf16[1024,1024]{1,0:T(8,128)(2,1)} %collective-permute-done.4.other_ref, bf16[2,2048,384]{2,1,0:T(8,128)(2,1)} %merge.1.rest_0_), custom_call_target="tpu_custom_call" | custom-call | flops 786432 | bytes 2944 | tf_op jit(solution)/shard_map/partial/pallas_call | solution.py:429
  108.2 6.0 %split.1 = (bf16[1,2048,384]{2,1,0:T(8,128)(2,1)}, bf16[1,2048,384]{2,1,0:T(8,128)(2,1)}, bf16[1,2048,384]{2,1,0:T(8,128)(2,1)}, bf16[1,2048,384]{2,1,0:T(8,128)(2,1)}) custom-call(bf16[2,2048,384]{2,1,0:T(8,128)(2,1)} %collective-permute-done.8.rest_1_.refs_0_, bf16[2,2048,384]{2,1,0:T(8,128)(2,1)} %collective-permute-done.7.rest_0_.refs_1_), custom_call_target="tpu_custom_call" | custom-call | flops 192 | bytes 3072 | tf_op jit(solution)/shard_map/split/pallas_call | solution.py:336
  114.2 2.5 %collective-permute-start.10 = (bf16[1,2048,384]{2,1,0:T(8,128)(2,1)}, bf16[1,2048,384]{2,1,0:T(8,128)(2,1)}, u32[]{:S(2)}, u32[]{:S(2)}) collective-permute-start(bf16[1,2048,384]{2,1,0:T(8,128)(2,1)} %get-tuple-element.64), channel_id=1, source_target_pairs={{1,9},{3,11},{4,0},{6,2},{8,16},{10,18},{13,5},{15,7},{16,24},{18,... | collective-permute-start | bytes 4718600 | tf_op jit(solution)/shard_map/ppermute | solution.py:346
  116.7 1.3 collective-permute-start.11
  118.0 1.8 collective-permute-start.12
  119.8 1.5 collective-permute-start.14
  121.3 8.9 %partial.9 = (bf16[1024,768]{1,0:T(8,128)(2,1)}, f32[1024,768]{1,0:T(8,128)}) custom-call(s32[25]{0:T(128)} %dynamic-slice_bitcast_fusion.table_ref, bf16[1024,1024]{1,0:T(8,128)(2,1)} %finish.1.own_ref, bf16[1024,1024]{1,0:T(8,128)(2,1)} %collective-permute-done.4.other_ref, bf16[2,2048,384]{2,1,0:T(8,128)(2,1)} %collective-permute-done.7.rest_0_.refs_1_, ...), custom_call_target="tpu_custom_call" | custom-call | flops 786432 | bytes 2944 | tf_op jit(solution)/shard_map/partial/pallas_call | solution.py:429
  130.2 7.1 %collective-permute-done.9.rest_0_ = bf16[1024,768]{1,0:T(8,128)(2,1)} collective-permute-done((bf16[1024,768]{1,0:T(8,128)(2,1)}, bf16[1024,768]{1,0:T(8,128)(2,1)}, u32[]{:S(2)}, u32[]{:S(2)}) %collective-permute-start.9) | collective-permute-done | bytes 1572896 | tf_op jit(solution)/shard_map/ppermute | solution.py:449
  137.2 2.5 %collective-permute-start.13 = (bf16[1,2048,384]{2,1,0:T(8,128)(2,1)}, bf16[1,2048,384]{2,1,0:T(8,128)(2,1)}, u32[]{:S(2)}, u32[]{:S(2)}) collective-permute-start(bf16[1,2048,384]{2,1,0:T(8,128)(2,1)} %get-tuple-element.70), channel_id=1, source_target_pairs={{1,9},{3,11},{4,0},{6,2},{8,16},{10,18},{13,5},{15,7},{16,24},{18,... | collective-permute-start | bytes 4718600 | tf_op jit(solution)/shard_map/ppermute | solution.py:346
  140.5 8.8 %collective-permute-start.15 = (bf16[1024,768]{1,0:T(8,128)(2,1)}, bf16[1024,768]{1,0:T(8,128)(2,1)}, u32[]{:S(2)}, u32[]{:S(2)}) collective-permute-start(bf16[1024,768]{1,0:T(8,128)(2,1)} %get-tuple-element.58), channel_id=1, source_target_pairs={{3,1},{0,2},{4,6},{7,5},{10,8},{9,11},{13,15},{14,12},{18,16},{17,... | collective-permute-start | bytes 4718600 | tf_op jit(solution)/shard_map/ppermute | solution.py:449
  149.3 1.3 collective-permute-start.16
  150.6 6.8 %partial.10 = (bf16[1024,384]{1,0:T(8,128)(2,1)}, f32[1024,384]{1,0:T(8,128)}) custom-call(s32[25]{0:T(128)} %dynamic-slice_bitcast_fusion.table_ref, bf16[1024,1024]{1,0:T(8,128)(2,1)} %finish.1.own_ref, bf16[1024,1024]{1,0:T(8,128)(2,1)} %collective-permute-done.4.other_ref, bf16[1,2048,384]{2,1,0:T(8,128)(2,1)} %collective-permute-done.10.rest_0_, ...), custom_call_target="tpu_custom_call" | custom-call | flops 393216 | bytes 1984 | tf_op jit(solution)/shard_map/partial/pallas_call | solution.py:429
  158.3 4.6 %collective-permute-start.18 = (bf16[1,2048,384]{2,1,0:T(8,128)(2,1)}, bf16[1,2048,384]{2,1,0:T(8,128)(2,1)}, u32[]{:S(2)}, u32[]{:S(2)}) collective-permute-start(bf16[1,2048,384]{2,1,0:T(8,128)(2,1)} %collective-permute-done.14.rest_1_), channel_id=1, source_target_pairs={{1,5},{3,7},{4,12},{6,14},{9,1},{11,3},{13,21},{15,23},{16,8},{18,... | collective-permute-start | bytes 4718600 | tf_op jit(solution)/shard_map/ppermute | solution.py:346
  162.9 1.3 collective-permute-start.17
  164.2 6.8 %partial.11 = (bf16[1024,384]{1,0:T(8,128)(2,1)}, f32[1024,384]{1,0:T(8,128)}) custom-call(s32[25]{0:T(128)} %dynamic-slice_bitcast_fusion.table_ref, bf16[1024,1024]{1,0:T(8,128)(2,1)} %finish.1.own_ref, bf16[1024,1024]{1,0:T(8,128)(2,1)} %collective-permute-done.4.other_ref, bf16[1,2048,384]{2,1,0:T(8,128)(2,1)} %collective-permute-done.13.rest_0_, ...), custom_call_target="tpu_custom_call" | custom-call | flops 393216 | bytes 1984 | tf_op jit(solution)/shard_map/partial/pallas_call | solution.py:429
  171.0 1.3 collective-permute-start.21
  173.1 7.6 %collective-permute-done.16.rest_0_ = bf16[1,2048,384]{2,1,0:T(8,128)(2,1)} collective-permute-done((bf16[1,2048,384]{2,1,0:T(8,128)(2,1)}, bf16[1,2048,384]{2,1,0:T(8,128)(2,1)}, u32[]{:S(2)}, u32[]{:S(2)}) %collective-permute-start.16) | collective-permute-done | bytes 1572896 | tf_op jit(solution)/shard_map/ppermute | solution.py:346
  180.7 6.8 %partial.12 = (bf16[1024,384]{1,0:T(8,128)(2,1)}, f32[1024,384]{1,0:T(8,128)}) custom-call(s32[25]{0:T(128)} %dynamic-slice_bitcast_fusion.table_ref, bf16[1024,1024]{1,0:T(8,128)(2,1)} %finish.1.own_ref, bf16[1024,1024]{1,0:T(8,128)(2,1)} %collective-permute-done.4.other_ref, bf16[1,2048,384]{2,1,0:T(8,128)(2,1)} %collective-permute-done.16.rest_0_), custom_call_target="tpu_custom_call" | custom-call | flops 393216 | bytes 1984 | tf_op jit(solution)/shard_map/partial/pallas_call | solution.py:429
  187.5 1.3 collective-permute-start.20
  188.8 3.1 %add_shares.10.rest_1_ = bf16[1024,1536]{1,0:T(8,128)(2,1)} custom-call(s32[25]{0:T(128)} %dynamic-slice_bitcast_fusion.table_ref, f32[1024,384]{1,0:T(8,128)} %get-tuple-element.79.kept_ref, bf16[1024,384]{1,0:T(8,128)(2,1)} %collective-permute-done.17.rest_0_, bf16[1024,1536]{1,0:T(8,128)(2,1)} %add_shares.9.rest_1_), custom_call_target="tpu_custom_call", output_to_operand_aliasing={{}: (3, {})} | custom-call | flops 192 | bytes 960 | tf_op jit(solution)/shard_map/add_shares/pallas_call | solution.py:459
  191.9 6.8 %partial.13 = (bf16[1024,384]{1,0:T(8,128)(2,1)}, f32[1024,384]{1,0:T(8,128)}) custom-call(s32[25]{0:T(128)} %dynamic-slice_bitcast_fusion.table_ref, bf16[1024,1024]{1,0:T(8,128)(2,1)} %finish.1.own_ref, bf16[1024,1024]{1,0:T(8,128)(2,1)} %collective-permute-done.4.other_ref, bf16[1,2048,384]{2,1,0:T(8,128)(2,1)} %collective-permute-done.18.rest_0_), custom_call_target="tpu_custom_call" | custom-call | flops 393216 | bytes 1984 | tf_op jit(solution)/shard_map/partial/pallas_call | solution.py:429
  198.8 1.3 collective-permute-start.19
  200.1 2.1 collective-permute-done.21.rest_0_
  202.1 3.1 %add_shares.11.rest_1_ = bf16[1024,1536]{1,0:T(8,128)(2,1)} custom-call(s32[25]{0:T(128)} %dynamic-slice_bitcast_fusion.table_ref, f32[1024,384]{1,0:T(8,128)} %get-tuple-element.86.kept_ref, bf16[1024,384]{1,0:T(8,128)(2,1)} %collective-permute-done.21.rest_0_, bf16[1024,1536]{1,0:T(8,128)(2,1)} %add_shares.10.rest_1_), custom_call_target="tpu_custom_call", output_to_operand_aliasing={{}: (3, {})} | custom-call | flops 192 | bytes 960 | tf_op jit(solution)/shard_map/add_shares/pallas_call | solution.py:459
  205.2 5.3 %collective-permute-done.20.rest_0_ = bf16[1024,384]{1,0:T(8,128)(2,1)} collective-permute-done((bf16[1024,384]{1,0:T(8,128)(2,1)}, bf16[1024,384]{1,0:T(8,128)(2,1)}, u32[]{:S(2)}, u32[]{:S(2)}) %collective-permute-start.20) | collective-permute-done | bytes 786464 | tf_op jit(solution)/shard_map/ppermute | solution.py:449
  210.5 3.1 %add_shares.12.rest_1_ = bf16[1024,1536]{1,0:T(8,128)(2,1)} custom-call(s32[25]{0:T(128)} %dynamic-slice_bitcast_fusion.table_ref, f32[1024,384]{1,0:T(8,128)} %get-tuple-element.84.kept_ref, bf16[1024,384]{1,0:T(8,128)(2,1)} %collective-permute-done.20.rest_0_, bf16[1024,1536]{1,0:T(8,128)(2,1)} %add_shares.11.rest_1_), custom_call_target="tpu_custom_call", output_to_operand_aliasing={{}: (3, {})} | custom-call | flops 192 | bytes 960 | tf_op jit(solution)/shard_map/add_shares/pallas_call | solution.py:459
  213.6 5.3 %collective-permute-done.19.rest_0_ = bf16[1024,384]{1,0:T(8,128)(2,1)} collective-permute-done((bf16[1024,384]{1,0:T(8,128)(2,1)}, bf16[1024,384]{1,0:T(8,128)(2,1)}, u32[]{:S(2)}, u32[]{:S(2)}) %collective-permute-start.19) | collective-permute-done | bytes 786464 | tf_op jit(solution)/shard_map/ppermute | solution.py:449
  219.0 3.1 %add_shares.13 = bf16[1024,1536]{1,0:T(8,128)(2,1)} custom-call(s32[25]{0:T(128)} %dynamic-slice_bitcast_fusion.table_ref, f32[1024,384]{1,0:T(8,128)} %get-tuple-element.82.kept_ref, bf16[1024,384]{1,0:T(8,128)(2,1)} %collective-permute-done.19.rest_0_, bf16[1024,1536]{1,0:T(8,128)(2,1)} %add_shares.12.rest_1_), custom_call_target="tpu_custom_call", output_to_operand_aliasing={{}: (3, {})} | custom-call | flops 192 | bytes 960 | tf_op jit(solution)/shard_map/add_shares/pallas_call | solution.py:459
  (18 shorter events, 4.0 us)
Async XLA Ops:
  0.0 8.2 %collective-permute-start = (bf16[1024,768]{1,0:T(8,128)(2,1)}, bf16[1024,768]{1,0:T(8,128)(2,1)}, u32[]{:S(2)}, u32[]{:S(2)}) collective-permute-start(bf16[1024,768]{1,0:T(8,128)(2,1)} %mine_ref.1), channel_id=1, source_target_pairs={{1,0},{3,2},{5,4},{7,6},{8,9},{10,11},{12,13},{14,15},{17,16},{19,... | collective-permute-start | bytes 4718600 | tf_op jit(solution)/shard_map/ppermute | solution.py:351
  7.6 6.7 %collective-permute-start.1 = (bf16[8,128,128]{2,1,0:T(8,128)(2,1)}, bf16[8,128,128]{2,1,0:T(8,128)(2,1)}, u32[]{:S(2)}, u32[]{:S(2)}) collective-permute-start(bf16[8,128,128]{2,1,0:T(8,128)(2,1)} %summary.1.own_ref), channel_id=1, source_target_pairs={{0,4},{4,0},{8,12},{12,8},{16,20},{20,16},{24,28},{28,24},{1,5},{5... | collective-permute-start | bytes 786440 | tf_op jit(solution)/shard_map/ppermute | solution.py:360
  14.4 47.9 %collective-permute-start.6 = (bf16[2,2048,384]{2,1,0:T(8,128)(2,1)}, bf16[2,2048,384]{2,1,0:T(8,128)(2,1)}, u32[]{:S(2)}, u32[]{:S(2)}) collective-permute-start(bf16[2,2048,384]{2,1,0:T(8,128)(2,1)} %merge.1.rest_0_), channel_id=1, source_target_pairs={{0,4},{2,6},{4,12},{6,14},{9,1},{11,3},{13,21},{15,23},{16,8},{18,... | collective-permute-start | bytes 9437192 | tf_op jit(solution)/shard_map/ppermute | solution.py:346
  15.7 53.1 %collective-permute-start.5 = (bf16[2,2048,384]{2,1,0:T(8,128)(2,1)}, bf16[2,2048,384]{2,1,0:T(8,128)(2,1)}, u32[]{:S(2)}, u32[]{:S(2)}) collective-permute-start(bf16[2,2048,384]{2,1,0:T(8,128)(2,1)} %merge.1.rest_0_), channel_id=1, source_target_pairs={{0,8},{2,10},{4,0},{6,2},{9,17},{11,19},{13,5},{15,7},{16,24},{18,... | collective-permute-start | bytes 9437192 | tf_op jit(solution)/shard_map/ppermute | solution.py:346
  19.9 18.4 %collective-permute-start.3 = (bf16[8,128,128]{2,1,0:T(8,128)(2,1)}, bf16[8,128,128]{2,1,0:T(8,128)(2,1)}, u32[]{:S(2)}, u32[]{:S(2)}) collective-permute-start(bf16[8,128,128]{2,1,0:T(8,128)(2,1)} %pair_state.1), channel_id=1, source_target_pairs={{0,16},{4,20},{8,24},{12,28},{1,17},{5,21},{9,25},{13,29},{2,18},{... | collective-permute-start | bytes 786440 | tf_op jit(solution)/shard_map/ppermute | solution.py:387
  21.2 41.1 %collective-permute-start.2 = (bf16[8,128,128]{2,1,0:T(8,128)(2,1)}, bf16[8,128,128]{2,1,0:T(8,128)(2,1)}, u32[]{:S(2)}, u32[]{:S(2)}) collective-permute-start(bf16[8,128,128]{2,1,0:T(8,128)(2,1)} %pair_state.1), channel_id=1, source_target_pairs={{0,8},{4,12},{8,16},{12,20},{16,24},{20,28},{1,9},{5,13},{9,17},{1... | collective-permute-start | bytes 786440 | tf_op jit(solution)/shard_map/ppermute | solution.py:387
  62.3 44.8 %collective-permute-start.8 = (bf16[2,2048,384]{2,1,0:T(8,128)(2,1)}, bf16[2,2048,384]{2,1,0:T(8,128)(2,1)}, u32[]{:S(2)}, u32[]{:S(2)}) collective-permute-start(bf16[2,2048,384]{2,1,0:T(8,128)(2,1)} %collective-permute-done.6.rest_1_), channel_id=1, source_target_pairs={{1,5},{3,7},{4,12},{6,14},{8,0},{10,2},{12,20},{14,22},{17,9},{19,... | collective-permute-start | bytes 9437192 | tf_op jit(solution)/shard_map/ppermute | solution.py:346
  68.7 39.5 %collective-permute-start.7 = (bf16[2,2048,384]{2,1,0:T(8,128)(2,1)}, bf16[2,2048,384]{2,1,0:T(8,128)(2,1)}, u32[]{:S(2)}, u32[]{:S(2)}) collective-permute-start(bf16[2,2048,384]{2,1,0:T(8,128)(2,1)} %collective-permute-done.5.rest_0_), channel_id=1, source_target_pairs={{0,8},{2,10},{5,1},{7,3},{8,16},{10,18},{12,4},{14,6},{17,25},{19,... | collective-permute-start | bytes 9437192 | tf_op jit(solution)/shard_map/ppermute | solution.py:346
  76.9 12.9 %collective-permute-start.4 = (bf16[1024,1024]{1,0:T(8,128)(2,1)}, bf16[1024,1024]{1,0:T(8,128)(2,1)}, u32[]{:S(2)}, u32[]{:S(2)}) collective-permute-start(bf16[1024,1024]{1,0:T(8,128)(2,1)} %finish.1.own_ref), channel_id=1, source_target_pairs={{0,1},{1,0},{2,3},{3,2},{4,5},{5,4},{6,7},{7,6},{8,9},{9,8},{10,11... | collective-permute-start | bytes 6291464 | tf_op jit(solution)/shard_map/ppermute | solution.py:417
  98.7 38.5 %collective-permute-start.9 = (bf16[1024,768]{1,0:T(8,128)(2,1)}, bf16[1024,768]{1,0:T(8,128)(2,1)}, u32[]{:S(2)}, u32[]{:S(2)}) collective-permute-start(bf16[1024,768]{1,0:T(8,128)(2,1)} %get-tuple-element.52), channel_id=1, source_target_pairs={{2,0},{3,1},{7,5},{6,4},{10,8},{8,10},{12,14},{14,12},{19,17},{17,... | collective-permute-start | bytes 4718600 | tf_op jit(solution)/shard_map/ppermute | solution.py:449
  114.2 26.3 %collective-permute-start.10 = (bf16[1,2048,384]{2,1,0:T(8,128)(2,1)}, bf16[1,2048,384]{2,1,0:T(8,128)(2,1)}, u32[]{:S(2)}, u32[]{:S(2)}) collective-permute-start(bf16[1,2048,384]{2,1,0:T(8,128)(2,1)} %get-tuple-element.64), channel_id=1, source_target_pairs={{1,9},{3,11},{4,0},{6,2},{8,16},{10,18},{13,5},{15,7},{16,24},{18,... | collective-permute-start | bytes 4718600 | tf_op jit(solution)/shard_map/ppermute | solution.py:346
  116.7 32.7 %collective-permute-start.11 = (bf16[1,2048,384]{2,1,0:T(8,128)(2,1)}, bf16[1,2048,384]{2,1,0:T(8,128)(2,1)}, u32[]{:S(2)}, u32[]{:S(2)}) collective-permute-start(bf16[1,2048,384]{2,1,0:T(8,128)(2,1)} %get-tuple-element.65), channel_id=1, source_target_pairs={{0,4},{2,6},{5,13},{7,15},{9,1},{11,3},{12,20},{14,22},{17,9},{19,... | collective-permute-start | bytes 4718600 | tf_op jit(solution)/shard_map/ppermute | solution.py:346
  118.0 39.5 %collective-permute-start.12 = (bf16[1024,768]{1,0:T(8,128)(2,1)}, bf16[1024,768]{1,0:T(8,128)(2,1)}, u32[]{:S(2)}, u32[]{:S(2)}) collective-permute-start(bf16[1024,768]{1,0:T(8,128)(2,1)} %get-tuple-element.54), channel_id=1, source_target_pairs={{2,0},{6,4},{11,9},{15,13},{16,18},{20,22},{25,27},{29,31}} | collective-permute-start | bytes 4718600 | tf_op jit(solution)/shard_map/ppermute | solution.py:449
  119.8 38.5 %collective-permute-start.14 = (bf16[1,2048,384]{2,1,0:T(8,128)(2,1)}, bf16[1,2048,384]{2,1,0:T(8,128)(2,1)}, u32[]{:S(2)}, u32[]{:S(2)}) collective-permute-start(bf16[1,2048,384]{2,1,0:T(8,128)(2,1)} %get-tuple-element.71), channel_id=1, source_target_pairs={{0,4},{2,6},{5,13},{7,15},{9,1},{11,3},{12,20},{14,22},{17,9},{19,... | collective-permute-start | bytes 4718600 | tf_op jit(solution)/shard_map/ppermute | solution.py:346
  137.2 26.9 %collective-permute-start.13 = (bf16[1,2048,384]{2,1,0:T(8,128)(2,1)}, bf16[1,2048,384]{2,1,0:T(8,128)(2,1)}, u32[]{:S(2)}, u32[]{:S(2)}) collective-permute-start(bf16[1,2048,384]{2,1,0:T(8,128)(2,1)} %get-tuple-element.70), channel_id=1, source_target_pairs={{1,9},{3,11},{4,0},{6,2},{8,16},{10,18},{13,5},{15,7},{16,24},{18,... | collective-permute-start | bytes 4718600 | tf_op jit(solution)/shard_map/ppermute | solution.py:346
  140.5 31.8 %collective-permute-start.15 = (bf16[1024,768]{1,0:T(8,128)(2,1)}, bf16[1024,768]{1,0:T(8,128)(2,1)}, u32[]{:S(2)}, u32[]{:S(2)}) collective-permute-start(bf16[1024,768]{1,0:T(8,128)(2,1)} %get-tuple-element.58), channel_id=1, source_target_pairs={{3,1},{0,2},{4,6},{7,5},{10,8},{9,11},{13,15},{14,12},{18,16},{17,... | collective-permute-start | bytes 4718600 | tf_op jit(solution)/shard_map/ppermute | solution.py:449
  149.3 31.4 %collective-permute-start.16 = (bf16[1,2048,384]{2,1,0:T(8,128)(2,1)}, bf16[1,2048,384]{2,1,0:T(8,128)(2,1)}, u32[]{:S(2)}, u32[]{:S(2)}) collective-permute-start(bf16[1,2048,384]{2,1,0:T(8,128)(2,1)} %collective-permute-done.10.rest_0_), channel_id=1, source_target_pairs={{0,8},{2,10},{5,1},{7,3},{9,17},{11,19},{13,5},{15,7},{16,24},{18,... | collective-permute-start | bytes 4718600 | tf_op jit(solution)/shard_map/ppermute | solution.py:346
  158.3 33.6 %collective-permute-start.18 = (bf16[1,2048,384]{2,1,0:T(8,128)(2,1)}, bf16[1,2048,384]{2,1,0:T(8,128)(2,1)}, u32[]{:S(2)}, u32[]{:S(2)}) collective-permute-start(bf16[1,2048,384]{2,1,0:T(8,128)(2,1)} %collective-permute-done.14.rest_1_), channel_id=1, source_target_pairs={{1,5},{3,7},{4,12},{6,14},{9,1},{11,3},{13,21},{15,23},{16,8},{18,... | collective-permute-start | bytes 4718600 | tf_op jit(solution)/shard_map/ppermute | solution.py:346
  162.9 26.0 %collective-permute-start.17 = (bf16[1024,384]{1,0:T(8,128)(2,1)}, bf16[1024,384]{1,0:T(8,128)(2,1)}, u32[]{:S(2)}, u32[]{:S(2)}) collective-permute-start(bf16[1024,384]{1,0:T(8,128)(2,1)} %get-tuple-element.66), channel_id=1, source_target_pairs={{0,2},{1,3},{5,7},{4,6},{11,9},{9,11},{13,15},{15,13},{18,16},{16,... | collective-permute-start | bytes 2359304 | tf_op jit(solution)/shard_map/ppermute | solution.py:449
  171.0 31.1 %collective-permute-start.21 = (bf16[1024,384]{1,0:T(8,128)(2,1)}, bf16[1024,384]{1,0:T(8,128)(2,1)}, u32[]{:S(2)}, u32[]{:S(2)}) collective-permute-start(bf16[1024,384]{1,0:T(8,128)(2,1)} %get-tuple-element.72), channel_id=1, source_target_pairs={{0,2},{1,3},{5,7},{4,6},{11,9},{9,11},{13,15},{15,13},{18,16},{16,... | collective-permute-start | bytes 2359304 | tf_op jit(solution)/shard_map/ppermute | solution.py:449
  187.5 23.0 %collective-permute-start.20 = (bf16[1024,384]{1,0:T(8,128)(2,1)}, bf16[1024,384]{1,0:T(8,128)(2,1)}, u32[]{:S(2)}, u32[]{:S(2)}) collective-permute-start(bf16[1024,384]{1,0:T(8,128)(2,1)} %get-tuple-element.77), channel_id=1, source_target_pairs={{1,3},{5,7},{8,10},{12,14},{19,17},{23,21},{26,24},{30,28}} | collective-permute-start | bytes 2359304 | tf_op jit(solution)/shard_map/ppermute | solution.py:449
  198.8 20.2 %collective-permute-start.19 = (bf16[1024,384]{1,0:T(8,128)(2,1)}, bf16[1024,384]{1,0:T(8,128)(2,1)}, u32[]{:S(2)}, u32[]{:S(2)}) collective-permute-start(bf16[1024,384]{1,0:T(8,128)(2,1)} %get-tuple-element.83), channel_id=1, source_target_pairs={{1,3},{5,7},{8,10},{12,14},{19,17},{23,21},{26,24},{30,28}} | collective-permute-start | bytes 2359304 | tf_op jit(solution)/shard_map/ppermute | solution.py:449

commit v4 on v3

--- a/solution.py
+++ b/solution.py
@@ -48,10 +48,19 @@
     return found
 
 
-def summary_kernel(lengths_ref, key_ref, value_ref, out_ref):
+def summary_kernel(lengths_ref, key_ref, value_ref, out_ref, scalar_ref):
     rows = key_ref.shape[0]
     first_pos = lax.axis_index("seq") * rows
-    last_start = doc_start_of(lengths_ref, first_pos + rows - 1) - first_pos
+
+    @pl.when(pl.program_id(0) == 0)
+    def _():
+        start, found = jnp.int32(0), jnp.int32(0)
+        for c in range(lengths_ref.shape[0]):
+            found = jnp.where(start <= first_pos + rows - 1, start, found)
+            start = start + lengths_ref[c]
+        scalar_ref[0] = found - first_pos
+
+    last_start = scalar_ref[0]
     mask = lax.broadcasted_iota(jnp.int32, (rows, HS), 0) >= last_start
     for h in range(out_ref.shape[0]):
         at = slice(h * HS, (h + 1) * HS)
@@ -305,6 +314,7 @@
             in_specs=[smem, two_heads, two_heads],
             out_specs=pl.BlockSpec((2, HS, HS), lambda h: (h, 0, 0)),
             out_shape=jax.ShapeDtypeStruct((heads_here, HS, HS), BF16),
+            scratch_shapes=[pltpu.SMEM((1,), jnp.int32)],
             cost_estimate=cost(2 * rows * width * HS, 4 * rows * width),
         )(doc_lengths, key_rows, value_rows)
 

time: 224 us -> 224 us (level)
  no operation moved by 1% of the time
where the time goes in v4:
time: 224 us; the launch traced here: 222 us
  Pallas kernels  101 us (45%)
  starting transfers between devices  60.1 us (27%)
  waiting for transfers between devices  58.9 us (26%)
    pallas_call x7, Pallas kernels, share(): call(functools.partial(partial_kernel, slots=len(slots), at=at + 2), 'par...  48.8 us
    ppermute x10, starting transfers between devices, send_on(): lax.ppermute(here, BOTH, along(source, step))  24.8 us
    ppermute x2, waiting for transfers between devices, shards(): lax.ppermute(pair_state, 'seq', [(s, s + 2 * d) for s in range(n - 2 * d)])  24 us
    ppermute x7, starting transfers between devices, share(): received.append(lax.ppermute(sent, BOTH, to_owner))  20.5 us
    ppermute x7, waiting for transfers between devices, share(): received.append(lax.ppermute(sent, BOTH, to_owner))  19.8 us
    pallas_call x7, Pallas kernels, add(): call(functools.partial(add_kernel, at=at, shares=len(received), tile=few)...  14.7 us
    pallas_call x2, Pallas kernels, intra_of(): call(functools.partial(intra_kernel, tile=256), 'intra', grid=(count,), i...  14.5 us
    ppermute x1, starting transfers between devices, shards(): lax.ppermute(head_out, 'head', [(h, h ^ 1) for h in range(heads)])  8.81 us
  transfers between devices with their start and end apart: 22, of which 9 were waited for; matrix products, arithmetic and copies ran while one was open for 1% of the time, Pallas kernels for 44%

profile of v4, /device:TPU:26, one launch (start us, length us, event | category | flops | bytes accessed | tf_op | source)
XLA Modules:
  0.0 222.1 jit_solution(7220525150865798592)
XLA Ops:
  0.0 2.9 %collective-permute-start = (bf16[1024,768]{1,0:T(8,128)(2,1)}, bf16[1024,768]{1,0:T(8,128)(2,1)}, u32[]{:S(2)}, u32[]{:S(2)}) collective-permute-start(bf16[1024,768]{1,0:T(8,128)(2,1)} %mine_ref.1), channel_id=1, source_target_pairs={{1,0},{3,2},{5,4},{7,6},{8,9},{10,11},{12,13},{14,15},{17,16},{19,... | collective-permute-start | bytes 4718600 | tf_op jit(solution)/shard_map/ppermute | solution.py:361
  2.9 4.6 %summary.1.own_ref = bf16[8,128,128]{2,1,0:T(8,128)(2,1)} custom-call(s32[16]{0:T(128)} %lengths_ref.7, bf16[1024,1024]{1,0:T(8,128)(2,1)} %key_ref.5, bf16[1024,1024]{1,0:T(8,128)(2,1)} %value_ref.5), custom_call_target="tpu_custom_call" | custom-call | flops 65536 | bytes 1024 | tf_op jit(solution)/shard_map/summary/pallas_call | solution.py:310
  8.0 3.8 %merge.1.rest_0_ = bf16[2,2048,384]{2,1,0:T(8,128)(2,1)} custom-call(bf16[1024,768]{1,0:T(8,128)(2,1)} %mine_ref.1, bf16[1024,768]{1,0:T(8,128)(2,1)} %collective-permute-done.gathered_ref), custom_call_target="tpu_custom_call" | custom-call | flops 96 | bytes 1536 | tf_op jit(solution)/shard_map/merge/pallas_call | solution.py:362
  11.8 2.4 %collective-permute-done.1.other_ref = bf16[8,128,128]{2,1,0:T(8,128)(2,1)} collective-permute-done((bf16[8,128,128]{2,1,0:T(8,128)(2,1)}, bf16[8,128,128]{2,1,0:T(8,128)(2,1)}, u32[]{:S(2)}, u32[]{:S(2)}) %collective-permute-start.1) | collective-permute-done | bytes 262176 | tf_op jit(solution)/shard_map/ppermute | solution.py:370
  14.2 1.3 collective-permute-start.6
  15.5 2.3 %collective-permute-start.5 = (bf16[2,2048,384]{2,1,0:T(8,128)(2,1)}, bf16[2,2048,384]{2,1,0:T(8,128)(2,1)}, u32[]{:S(2)}, u32[]{:S(2)}) collective-permute-start(bf16[2,2048,384]{2,1,0:T(8,128)(2,1)} %merge.1.rest_0_), channel_id=1, source_target_pairs={{0,8},{2,10},{4,0},{6,2},{9,17},{11,19},{13,5},{15,7},{16,24},{18,... | collective-permute-start | bytes 9437192 | tf_op jit(solution)/shard_map/ppermute | solution.py:356
  17.8 2.0 pair_state.1
  19.8 1.3 collective-permute-start.3
  21.1 1.3 collective-permute-start.2
  22.4 1.3 dynamic-slice_bitcast_fusion.table_ref
  23.7 7.2 %intra.2.low_ref = f32[1024,512]{1,0:T(8,128)} custom-call(s32[16]{0:T(128)} %lengths_ref.7, bf16[1024,1024]{1,0:T(8,128)(2,1)} %query_ref.5, bf16[1024,1024]{1,0:T(8,128)(2,1)} %key_ref.5, bf16[1024,1024]{1,0:T(8,128)(2,1)} %value_ref.5), custom_call_target="tpu_custom_call" | custom-call | flops 524288 | bytes 1280 | tf_op jit(solution)/shard_map/intra/pallas_call | solution.py:375
  30.9 7.3 %intra.3.high_ref = f32[1024,512]{1,0:T(8,128)} custom-call(s32[16]{0:T(128)} %lengths_ref.7, bf16[1024,1024]{1,0:T(8,128)(2,1)} %query_ref.5, bf16[1024,1024]{1,0:T(8,128)(2,1)} %key_ref.5, bf16[1024,1024]{1,0:T(8,128)(2,1)} %value_ref.5), custom_call_target="tpu_custom_call" | custom-call | flops 524288 | bytes 1280 | tf_op jit(solution)/shard_map/intra/pallas_call | solution.py:375
  38.2 24.0 %collective-permute-done.2.rest_0_ = bf16[8,128,128]{2,1,0:T(8,128)(2,1)} collective-permute-done((bf16[8,128,128]{2,1,0:T(8,128)(2,1)}, bf16[8,128,128]{2,1,0:T(8,128)(2,1)}, u32[]{:S(2)}, u32[]{:S(2)}) %collective-permute-start.2) | collective-permute-done | bytes 262176 | tf_op jit(solution)/shard_map/ppermute | solution.py:397
  62.1 6.4 %collective-permute-start.8 = (bf16[2,2048,384]{2,1,0:T(8,128)(2,1)}, bf16[2,2048,384]{2,1,0:T(8,128)(2,1)}, u32[]{:S(2)}, u32[]{:S(2)}) collective-permute-start(bf16[2,2048,384]{2,1,0:T(8,128)(2,1)} %collective-permute-done.6.rest_1_), channel_id=1, source_target_pairs={{1,5},{3,7},{4,12},{6,14},{8,0},{10,2},{12,20},{14,22},{17,9},{19,... | collective-permute-start | bytes 9437192 | tf_op jit(solution)/shard_map/ppermute | solution.py:356
  68.6 1.3 collective-permute-start.7
  69.9 6.9 %finish.1.own_ref = bf16[1024,1024]{1,0:T(8,128)(2,1)} custom-call(s32[16]{0:T(128)} %lengths_ref.7, bf16[1024,1024]{1,0:T(8,128)(2,1)} %query_ref.5, f32[1024,512]{1,0:T(8,128)} %intra.2.low_ref, f32[1024,512]{1,0:T(8,128)} %intra.3.high_ref, bf16[1024,1024]{1,0:T(8,128)(2,1)} %gate_ref.1, f32[1,1024]{1,0:T(1,128)} %bitcast.3, ...), custom_call_target="tpu_custom_call" | custom-call | flops 65536 | bytes 3072 | tf_op jit(solution)/shard_map/finish/pallas_call | solution.py:407
  76.8 8.8 %collective-permute-start.4 = (bf16[1024,1024]{1,0:T(8,128)(2,1)}, bf16[1024,1024]{1,0:T(8,128)(2,1)}, u32[]{:S(2)}, u32[]{:S(2)}) collective-permute-start(bf16[1024,1024]{1,0:T(8,128)(2,1)} %finish.1.own_ref), channel_id=1, source_target_pairs={{0,1},{1,0},{2,3},{3,2},{4,5},{5,4},{6,7},{7,6},{8,9},{9,8},{10,11... | collective-permute-start | bytes 6291464 | tf_op jit(solution)/shard_map/ppermute | solution.py:427
  85.6 4.1 %collective-permute-done.4.other_ref = bf16[1024,1024]{1,0:T(8,128)(2,1)} collective-permute-done((bf16[1024,1024]{1,0:T(8,128)(2,1)}, bf16[1024,1024]{1,0:T(8,128)(2,1)}, u32[]{:S(2)}, u32[]{:S(2)}) %collective-permute-start.4) | collective-permute-done | bytes 2097184 | tf_op jit(solution)/shard_map/ppermute | solution.py:427
  89.7 8.9 %partial.7 = (bf16[1024,768]{1,0:T(8,128)(2,1)}, f32[1024,768]{1,0:T(8,128)}) custom-call(s32[25]{0:T(128)} %dynamic-slice_bitcast_fusion.table_ref, bf16[1024,1024]{1,0:T(8,128)(2,1)} %finish.1.own_ref, bf16[1024,1024]{1,0:T(8,128)(2,1)} %collective-permute-done.4.other_ref, bf16[2,2048,384]{2,1,0:T(8,128)(2,1)} %collective-permute-done.5.rest_0_, ...), custom_call_target="tpu_custom_call" | custom-call | flops 786432 | bytes 2944 | tf_op jit(solution)/shard_map/partial/pallas_call | solution.py:439
  98.6 4.6 %collective-permute-start.9 = (bf16[1024,768]{1,0:T(8,128)(2,1)}, bf16[1024,768]{1,0:T(8,128)(2,1)}, u32[]{:S(2)}, u32[]{:S(2)}) collective-permute-start(bf16[1024,768]{1,0:T(8,128)(2,1)} %get-tuple-element.52), channel_id=1, source_target_pairs={{2,0},{3,1},{7,5},{6,4},{10,8},{8,10},{12,14},{14,12},{19,17},{17,... | collective-permute-start | bytes 4718600 | tf_op jit(solution)/shard_map/ppermute | solution.py:459
  103.2 3.7 %partial.8 = (bf16[1024,768]{1,0:T(8,128)(2,1)}, f32[1024,768]{1,0:T(8,128)}) custom-call(s32[25]{0:T(128)} %dynamic-slice_bitcast_fusion.table_ref, bf16[1024,1024]{1,0:T(8,128)(2,1)} %finish.1.own_ref, bf16[1024,1024]{1,0:T(8,128)(2,1)} %collective-permute-done.4.other_ref, bf16[2,2048,384]{2,1,0:T(8,128)(2,1)} %merge.1.rest_0_), custom_call_target="tpu_custom_call" | custom-call | flops 786432 | bytes 2944 | tf_op jit(solution)/shard_map/partial/pallas_call | solution.py:439
  108.1 6.0 %split.1 = (bf16[1,2048,384]{2,1,0:T(8,128)(2,1)}, bf16[1,2048,384]{2,1,0:T(8,128)(2,1)}, bf16[1,2048,384]{2,1,0:T(8,128)(2,1)}, bf16[1,2048,384]{2,1,0:T(8,128)(2,1)}) custom-call(bf16[2,2048,384]{2,1,0:T(8,128)(2,1)} %collective-permute-done.8.rest_1_.refs_0_, bf16[2,2048,384]{2,1,0:T(8,128)(2,1)} %collective-permute-done.7.rest_0_.refs_1_), custom_call_target="tpu_custom_call" | custom-call | flops 192 | bytes 3072 | tf_op jit(solution)/shard_map/split/pallas_call | solution.py:346
  114.1 2.5 %collective-permute-start.10 = (bf16[1,2048,384]{2,1,0:T(8,128)(2,1)}, bf16[1,2048,384]{2,1,0:T(8,128)(2,1)}, u32[]{:S(2)}, u32[]{:S(2)}) collective-permute-start(bf16[1,2048,384]{2,1,0:T(8,128)(2,1)} %get-tuple-element.64), channel_id=1, source_target_pairs={{1,9},{3,11},{4,0},{6,2},{8,16},{10,18},{13,5},{15,7},{16,24},{18,... | collective-permute-start | bytes 4718600 | tf_op jit(solution)/shard_map/ppermute | solution.py:356
  116.5 1.3 collective-permute-start.11
  117.8 1.8 collective-permute-start.12
  119.7 1.5 collective-permute-start.14
  121.1 8.9 %partial.9 = (bf16[1024,768]{1,0:T(8,128)(2,1)}, f32[1024,768]{1,0:T(8,128)}) custom-call(s32[25]{0:T(128)} %dynamic-slice_bitcast_fusion.table_ref, bf16[1024,1024]{1,0:T(8,128)(2,1)} %finish.1.own_ref, bf16[1024,1024]{1,0:T(8,128)(2,1)} %collective-permute-done.4.other_ref, bf16[2,2048,384]{2,1,0:T(8,128)(2,1)} %collective-permute-done.7.rest_0_.refs_1_, ...), custom_call_target="tpu_custom_call" | custom-call | flops 786432 | bytes 2944 | tf_op jit(solution)/shard_map/partial/pallas_call | solution.py:439
  130.0 7.1 %collective-permute-done.9.rest_0_ = bf16[1024,768]{1,0:T(8,128)(2,1)} collective-permute-done((bf16[1024,768]{1,0:T(8,128)(2,1)}, bf16[1024,768]{1,0:T(8,128)(2,1)}, u32[]{:S(2)}, u32[]{:S(2)}) %collective-permute-start.9) | collective-permute-done | bytes 1572896 | tf_op jit(solution)/shard_map/ppermute | solution.py:459
  137.1 2.5 %collective-permute-start.13 = (bf16[1,2048,384]{2,1,0:T(8,128)(2,1)}, bf16[1,2048,384]{2,1,0:T(8,128)(2,1)}, u32[]{:S(2)}, u32[]{:S(2)}) collective-permute-start(bf16[1,2048,384]{2,1,0:T(8,128)(2,1)} %get-tuple-element.70), channel_id=1, source_target_pairs={{1,9},{3,11},{4,0},{6,2},{8,16},{10,18},{13,5},{15,7},{16,24},{18,... | collective-permute-start | bytes 4718600 | tf_op jit(solution)/shard_map/ppermute | solution.py:356
  140.3 8.8 %collective-permute-start.15 = (bf16[1024,768]{1,0:T(8,128)(2,1)}, bf16[1024,768]{1,0:T(8,128)(2,1)}, u32[]{:S(2)}, u32[]{:S(2)}) collective-permute-start(bf16[1024,768]{1,0:T(8,128)(2,1)} %get-tuple-element.58), channel_id=1, source_target_pairs={{3,1},{0,2},{4,6},{7,5},{10,8},{9,11},{13,15},{14,12},{18,16},{17,... | collective-permute-start | bytes 4718600 | tf_op jit(solution)/shard_map/ppermute | solution.py:459
  149.2 1.3 collective-permute-start.16
  150.5 6.8 %partial.10 = (bf16[1024,384]{1,0:T(8,128)(2,1)}, f32[1024,384]{1,0:T(8,128)}) custom-call(s32[25]{0:T(128)} %dynamic-slice_bitcast_fusion.table_ref, bf16[1024,1024]{1,0:T(8,128)(2,1)} %finish.1.own_ref, bf16[1024,1024]{1,0:T(8,128)(2,1)} %collective-permute-done.4.other_ref, bf16[1,2048,384]{2,1,0:T(8,128)(2,1)} %collective-permute-done.10.rest_0_, ...), custom_call_target="tpu_custom_call" | custom-call | flops 393216 | bytes 1984 | tf_op jit(solution)/shard_map/partial/pallas_call | solution.py:439
  158.1 4.6 %collective-permute-start.18 = (bf16[1,2048,384]{2,1,0:T(8,128)(2,1)}, bf16[1,2048,384]{2,1,0:T(8,128)(2,1)}, u32[]{:S(2)}, u32[]{:S(2)}) collective-permute-start(bf16[1,2048,384]{2,1,0:T(8,128)(2,1)} %collective-permute-done.14.rest_1_), channel_id=1, source_target_pairs={{1,5},{3,7},{4,12},{6,14},{9,1},{11,3},{13,21},{15,23},{16,8},{18,... | collective-permute-start | bytes 4718600 | tf_op jit(solution)/shard_map/ppermute | solution.py:356
  162.7 1.3 collective-permute-start.17
  164.0 6.8 %partial.11 = (bf16[1024,384]{1,0:T(8,128)(2,1)}, f32[1024,384]{1,0:T(8,128)}) custom-call(s32[25]{0:T(128)} %dynamic-slice_bitcast_fusion.table_ref, bf16[1024,1024]{1,0:T(8,128)(2,1)} %finish.1.own_ref, bf16[1024,1024]{1,0:T(8,128)(2,1)} %collective-permute-done.4.other_ref, bf16[1,2048,384]{2,1,0:T(8,128)(2,1)} %collective-permute-done.13.rest_0_, ...), custom_call_target="tpu_custom_call" | custom-call | flops 393216 | bytes 1984 | tf_op jit(solution)/shard_map/partial/pallas_call | solution.py:439
  170.9 1.3 collective-permute-start.21
  173.0 7.6 %collective-permute-done.16.rest_0_ = bf16[1,2048,384]{2,1,0:T(8,128)(2,1)} collective-permute-done((bf16[1,2048,384]{2,1,0:T(8,128)(2,1)}, bf16[1,2048,384]{2,1,0:T(8,128)(2,1)}, u32[]{:S(2)}, u32[]{:S(2)}) %collective-permute-start.16) | collective-permute-done | bytes 1572896 | tf_op jit(solution)/shard_map/ppermute | solution.py:356
  180.6 6.8 %partial.12 = (bf16[1024,384]{1,0:T(8,128)(2,1)}, f32[1024,384]{1,0:T(8,128)}) custom-call(s32[25]{0:T(128)} %dynamic-slice_bitcast_fusion.table_ref, bf16[1024,1024]{1,0:T(8,128)(2,1)} %finish.1.own_ref, bf16[1024,1024]{1,0:T(8,128)(2,1)} %collective-permute-done.4.other_ref, bf16[1,2048,384]{2,1,0:T(8,128)(2,1)} %collective-permute-done.16.rest_0_), custom_call_target="tpu_custom_call" | custom-call | flops 393216 | bytes 1984 | tf_op jit(solution)/shard_map/partial/pallas_call | solution.py:439
  187.4 1.3 collective-permute-start.20
  188.7 3.1 %add_shares.10.rest_1_ = bf16[1024,1536]{1,0:T(8,128)(2,1)} custom-call(s32[25]{0:T(128)} %dynamic-slice_bitcast_fusion.table_ref, f32[1024,384]{1,0:T(8,128)} %get-tuple-element.79.kept_ref, bf16[1024,384]{1,0:T(8,128)(2,1)} %collective-permute-done.17.rest_0_, bf16[1024,1536]{1,0:T(8,128)(2,1)} %add_shares.9.rest_1_), custom_call_target="tpu_custom_call", output_to_operand_aliasing={{}: (3, {})} | custom-call | flops 192 | bytes 960 | tf_op jit(solution)/shard_map/add_shares/pallas_call | solution.py:469
  191.8 6.8 %partial.13 = (bf16[1024,384]{1,0:T(8,128)(2,1)}, f32[1024,384]{1,0:T(8,128)}) custom-call(s32[25]{0:T(128)} %dynamic-slice_bitcast_fusion.table_ref, bf16[1024,1024]{1,0:T(8,128)(2,1)} %finish.1.own_ref, bf16[1024,1024]{1,0:T(8,128)(2,1)} %collective-permute-done.4.other_ref, bf16[1,2048,384]{2,1,0:T(8,128)(2,1)} %collective-permute-done.18.rest_0_), custom_call_target="tpu_custom_call" | custom-call | flops 393216 | bytes 1984 | tf_op jit(solution)/shard_map/partial/pallas_call | solution.py:439
  198.6 1.3 collective-permute-start.19
  199.9 2.0 collective-permute-done.21.rest_0_
  202.0 3.1 %add_shares.11.rest_1_ = bf16[1024,1536]{1,0:T(8,128)(2,1)} custom-call(s32[25]{0:T(128)} %dynamic-slice_bitcast_fusion.table_ref, f32[1024,384]{1,0:T(8,128)} %get-tuple-element.86.kept_ref, bf16[1024,384]{1,0:T(8,128)(2,1)} %collective-permute-done.21.rest_0_, bf16[1024,1536]{1,0:T(8,128)(2,1)} %add_shares.10.rest_1_), custom_call_target="tpu_custom_call", output_to_operand_aliasing={{}: (3, {})} | custom-call | flops 192 | bytes 960 | tf_op jit(solution)/shard_map/add_shares/pallas_call | solution.py:469
  205.1 5.3 %collective-permute-done.20.rest_0_ = bf16[1024,384]{1,0:T(8,128)(2,1)} collective-permute-done((bf16[1024,384]{1,0:T(8,128)(2,1)}, bf16[1024,384]{1,0:T(8,128)(2,1)}, u32[]{:S(2)}, u32[]{:S(2)}) %collective-permute-start.20) | collective-permute-done | bytes 786464 | tf_op jit(solution)/shard_map/ppermute | solution.py:459
  210.4 3.1 %add_shares.12.rest_1_ = bf16[1024,1536]{1,0:T(8,128)(2,1)} custom-call(s32[25]{0:T(128)} %dynamic-slice_bitcast_fusion.table_ref, f32[1024,384]{1,0:T(8,128)} %get-tuple-element.84.kept_ref, bf16[1024,384]{1,0:T(8,128)(2,1)} %collective-permute-done.20.rest_0_, bf16[1024,1536]{1,0:T(8,128)(2,1)} %add_shares.11.rest_1_), custom_call_target="tpu_custom_call", output_to_operand_aliasing={{}: (3, {})} | custom-call | flops 192 | bytes 960 | tf_op jit(solution)/shard_map/add_shares/pallas_call | solution.py:469
  213.5 5.3 %collective-permute-done.19.rest_0_ = bf16[1024,384]{1,0:T(8,128)(2,1)} collective-permute-done((bf16[1024,384]{1,0:T(8,128)(2,1)}, bf16[1024,384]{1,0:T(8,128)(2,1)}, u32[]{:S(2)}, u32[]{:S(2)}) %collective-permute-start.19) | collective-permute-done | bytes 786464 | tf_op jit(solution)/shard_map/ppermute | solution.py:459
  218.8 3.1 %add_shares.13 = bf16[1024,1536]{1,0:T(8,128)(2,1)} custom-call(s32[25]{0:T(128)} %dynamic-slice_bitcast_fusion.table_ref, f32[1024,384]{1,0:T(8,128)} %get-tuple-element.82.kept_ref, bf16[1024,384]{1,0:T(8,128)(2,1)} %collective-permute-done.19.rest_0_, bf16[1024,1536]{1,0:T(8,128)(2,1)} %add_shares.12.rest_1_), custom_call_target="tpu_custom_call", output_to_operand_aliasing={{}: (3, {})} | custom-call | flops 192 | bytes 960 | tf_op jit(solution)/shard_map/add_shares/pallas_call | solution.py:469
  (18 shorter events, 4.0 us)
Async XLA Ops:
  0.0 8.0 %collective-permute-start = (bf16[1024,768]{1,0:T(8,128)(2,1)}, bf16[1024,768]{1,0:T(8,128)(2,1)}, u32[]{:S(2)}, u32[]{:S(2)}) collective-permute-start(bf16[1024,768]{1,0:T(8,128)(2,1)} %mine_ref.1), channel_id=1, source_target_pairs={{1,0},{3,2},{5,4},{7,6},{8,9},{10,11},{12,13},{14,15},{17,16},{19,... | collective-permute-start | bytes 4718600 | tf_op jit(solution)/shard_map/ppermute | solution.py:361
  7.5 6.7 %collective-permute-start.1 = (bf16[8,128,128]{2,1,0:T(8,128)(2,1)}, bf16[8,128,128]{2,1,0:T(8,128)(2,1)}, u32[]{:S(2)}, u32[]{:S(2)}) collective-permute-start(bf16[8,128,128]{2,1,0:T(8,128)(2,1)} %summary.1.own_ref), channel_id=1, source_target_pairs={{0,4},{4,0},{8,12},{12,8},{16,20},{20,16},{24,28},{28,24},{1,5},{5... | collective-permute-start | bytes 786440 | tf_op jit(solution)/shard_map/ppermute | solution.py:370
  14.2 47.9 %collective-permute-start.6 = (bf16[2,2048,384]{2,1,0:T(8,128)(2,1)}, bf16[2,2048,384]{2,1,0:T(8,128)(2,1)}, u32[]{:S(2)}, u32[]{:S(2)}) collective-permute-start(bf16[2,2048,384]{2,1,0:T(8,128)(2,1)} %merge.1.rest_0_), channel_id=1, source_target_pairs={{0,4},{2,6},{4,12},{6,14},{9,1},{11,3},{13,21},{15,23},{16,8},{18,... | collective-permute-start | bytes 9437192 | tf_op jit(solution)/shard_map/ppermute | solution.py:356
  15.5 53.1 %collective-permute-start.5 = (bf16[2,2048,384]{2,1,0:T(8,128)(2,1)}, bf16[2,2048,384]{2,1,0:T(8,128)(2,1)}, u32[]{:S(2)}, u32[]{:S(2)}) collective-permute-start(bf16[2,2048,384]{2,1,0:T(8,128)(2,1)} %merge.1.rest_0_), channel_id=1, source_target_pairs={{0,8},{2,10},{4,0},{6,2},{9,17},{11,19},{13,5},{15,7},{16,24},{18,... | collective-permute-start | bytes 9437192 | tf_op jit(solution)/shard_map/ppermute | solution.py:356
  19.8 18.4 %collective-permute-start.3 = (bf16[8,128,128]{2,1,0:T(8,128)(2,1)}, bf16[8,128,128]{2,1,0:T(8,128)(2,1)}, u32[]{:S(2)}, u32[]{:S(2)}) collective-permute-start(bf16[8,128,128]{2,1,0:T(8,128)(2,1)} %pair_state.1), channel_id=1, source_target_pairs={{0,16},{4,20},{8,24},{12,28},{1,17},{5,21},{9,25},{13,29},{2,18},{... | collective-permute-start | bytes 786440 | tf_op jit(solution)/shard_map/ppermute | solution.py:397
  21.1 41.1 %collective-permute-start.2 = (bf16[8,128,128]{2,1,0:T(8,128)(2,1)}, bf16[8,128,128]{2,1,0:T(8,128)(2,1)}, u32[]{:S(2)}, u32[]{:S(2)}) collective-permute-start(bf16[8,128,128]{2,1,0:T(8,128)(2,1)} %pair_state.1), channel_id=1, source_target_pairs={{0,8},{4,12},{8,16},{12,20},{16,24},{20,28},{1,9},{5,13},{9,17},{1... | collective-permute-start | bytes 786440 | tf_op jit(solution)/shard_map/ppermute | solution.py:397
  62.1 44.8 %collective-permute-start.8 = (bf16[2,2048,384]{2,1,0:T(8,128)(2,1)}, bf16[2,2048,384]{2,1,0:T(8,128)(2,1)}, u32[]{:S(2)}, u32[]{:S(2)}) collective-permute-start(bf16[2,2048,384]{2,1,0:T(8,128)(2,1)} %collective-permute-done.6.rest_1_), channel_id=1, source_target_pairs={{1,5},{3,7},{4,12},{6,14},{8,0},{10,2},{12,20},{14,22},{17,9},{19,... | collective-permute-start | bytes 9437192 | tf_op jit(solution)/shard_map/ppermute | solution.py:356
  68.6 39.5 %collective-permute-start.7 = (bf16[2,2048,384]{2,1,0:T(8,128)(2,1)}, bf16[2,2048,384]{2,1,0:T(8,128)(2,1)}, u32[]{:S(2)}, u32[]{:S(2)}) collective-permute-start(bf16[2,2048,384]{2,1,0:T(8,128)(2,1)} %collective-permute-done.5.rest_0_), channel_id=1, source_target_pairs={{0,8},{2,10},{5,1},{7,3},{8,16},{10,18},{12,4},{14,6},{17,25},{19,... | collective-permute-start | bytes 9437192 | tf_op jit(solution)/shard_map/ppermute | solution.py:356
  76.8 12.9 %collective-permute-start.4 = (bf16[1024,1024]{1,0:T(8,128)(2,1)}, bf16[1024,1024]{1,0:T(8,128)(2,1)}, u32[]{:S(2)}, u32[]{:S(2)}) collective-permute-start(bf16[1024,1024]{1,0:T(8,128)(2,1)} %finish.1.own_ref), channel_id=1, source_target_pairs={{0,1},{1,0},{2,3},{3,2},{4,5},{5,4},{6,7},{7,6},{8,9},{9,8},{10,11... | collective-permute-start | bytes 6291464 | tf_op jit(solution)/shard_map/ppermute | solution.py:427
  98.6 38.5 %collective-permute-start.9 = (bf16[1024,768]{1,0:T(8,128)(2,1)}, bf16[1024,768]{1,0:T(8,128)(2,1)}, u32[]{:S(2)}, u32[]{:S(2)}) collective-permute-start(bf16[1024,768]{1,0:T(8,128)(2,1)} %get-tuple-element.52), channel_id=1, source_target_pairs={{2,0},{3,1},{7,5},{6,4},{10,8},{8,10},{12,14},{14,12},{19,17},{17,... | collective-permute-start | bytes 4718600 | tf_op jit(solution)/shard_map/ppermute | solution.py:459
  114.1 26.3 %collective-permute-start.10 = (bf16[1,2048,384]{2,1,0:T(8,128)(2,1)}, bf16[1,2048,384]{2,1,0:T(8,128)(2,1)}, u32[]{:S(2)}, u32[]{:S(2)}) collective-permute-start(bf16[1,2048,384]{2,1,0:T(8,128)(2,1)} %get-tuple-element.64), channel_id=1, source_target_pairs={{1,9},{3,11},{4,0},{6,2},{8,16},{10,18},{13,5},{15,7},{16,24},{18,... | collective-permute-start | bytes 4718600 | tf_op jit(solution)/shard_map/ppermute | solution.py:356
  116.5 32.7 %collective-permute-start.11 = (bf16[1,2048,384]{2,1,0:T(8,128)(2,1)}, bf16[1,2048,384]{2,1,0:T(8,128)(2,1)}, u32[]{:S(2)}, u32[]{:S(2)}) collective-permute-start(bf16[1,2048,384]{2,1,0:T(8,128)(2,1)} %get-tuple-element.65), channel_id=1, source_target_pairs={{0,4},{2,6},{5,13},{7,15},{9,1},{11,3},{12,20},{14,22},{17,9},{19,... | collective-permute-start | bytes 4718600 | tf_op jit(solution)/shard_map/ppermute | solution.py:356
  117.8 39.5 %collective-permute-start.12 = (bf16[1024,768]{1,0:T(8,128)(2,1)}, bf16[1024,768]{1,0:T(8,128)(2,1)}, u32[]{:S(2)}, u32[]{:S(2)}) collective-permute-start(bf16[1024,768]{1,0:T(8,128)(2,1)} %get-tuple-element.54), channel_id=1, source_target_pairs={{2,0},{6,4},{11,9},{15,13},{16,18},{20,22},{25,27},{29,31}} | collective-permute-start | bytes 4718600 | tf_op jit(solution)/shard_map/ppermute | solution.py:459
  119.7 38.5 %collective-permute-start.14 = (bf16[1,2048,384]{2,1,0:T(8,128)(2,1)}, bf16[1,2048,384]{2,1,0:T(8,128)(2,1)}, u32[]{:S(2)}, u32[]{:S(2)}) collective-permute-start(bf16[1,2048,384]{2,1,0:T(8,128)(2,1)} %get-tuple-element.71), channel_id=1, source_target_pairs={{0,4},{2,6},{5,13},{7,15},{9,1},{11,3},{12,20},{14,22},{17,9},{19,... | collective-permute-start | bytes 4718600 | tf_op jit(solution)/shard_map/ppermute | solution.py:356
  137.1 26.9 %collective-permute-start.13 = (bf16[1,2048,384]{2,1,0:T(8,128)(2,1)}, bf16[1,2048,384]{2,1,0:T(8,128)(2,1)}, u32[]{:S(2)}, u32[]{:S(2)}) collective-permute-start(bf16[1,2048,384]{2,1,0:T(8,128)(2,1)} %get-tuple-element.70), channel_id=1, source_target_pairs={{1,9},{3,11},{4,0},{6,2},{8,16},{10,18},{13,5},{15,7},{16,24},{18,... | collective-permute-start | bytes 4718600 | tf_op jit(solution)/shard_map/ppermute | solution.py:356
  140.3 31.8 %collective-permute-start.15 = (bf16[1024,768]{1,0:T(8,128)(2,1)}, bf16[1024,768]{1,0:T(8,128)(2,1)}, u32[]{:S(2)}, u32[]{:S(2)}) collective-permute-start(bf16[1024,768]{1,0:T(8,128)(2,1)} %get-tuple-element.58), channel_id=1, source_target_pairs={{3,1},{0,2},{4,6},{7,5},{10,8},{9,11},{13,15},{14,12},{18,16},{17,... | collective-permute-start | bytes 4718600 | tf_op jit(solution)/shard_map/ppermute | solution.py:459
  149.2 31.4 %collective-permute-start.16 = (bf16[1,2048,384]{2,1,0:T(8,128)(2,1)}, bf16[1,2048,384]{2,1,0:T(8,128)(2,1)}, u32[]{:S(2)}, u32[]{:S(2)}) collective-permute-start(bf16[1,2048,384]{2,1,0:T(8,128)(2,1)} %collective-permute-done.10.rest_0_), channel_id=1, source_target_pairs={{0,8},{2,10},{5,1},{7,3},{9,17},{11,19},{13,5},{15,7},{16,24},{18,... | collective-permute-start | bytes 4718600 | tf_op jit(solution)/shard_map/ppermute | solution.py:356
  158.1 33.6 %collective-permute-start.18 = (bf16[1,2048,384]{2,1,0:T(8,128)(2,1)}, bf16[1,2048,384]{2,1,0:T(8,128)(2,1)}, u32[]{:S(2)}, u32[]{:S(2)}) collective-permute-start(bf16[1,2048,384]{2,1,0:T(8,128)(2,1)} %collective-permute-done.14.rest_1_), channel_id=1, source_target_pairs={{1,5},{3,7},{4,12},{6,14},{9,1},{11,3},{13,21},{15,23},{16,8},{18,... | collective-permute-start | bytes 4718600 | tf_op jit(solution)/shard_map/ppermute | solution.py:356
  162.7 26.0 %collective-permute-start.17 = (bf16[1024,384]{1,0:T(8,128)(2,1)}, bf16[1024,384]{1,0:T(8,128)(2,1)}, u32[]{:S(2)}, u32[]{:S(2)}) collective-permute-start(bf16[1024,384]{1,0:T(8,128)(2,1)} %get-tuple-element.66), channel_id=1, source_target_pairs={{0,2},{1,3},{5,7},{4,6},{11,9},{9,11},{13,15},{15,13},{18,16},{16,... | collective-permute-start | bytes 2359304 | tf_op jit(solution)/shard_map/ppermute | solution.py:459
  170.9 31.1 %collective-permute-start.21 = (bf16[1024,384]{1,0:T(8,128)(2,1)}, bf16[1024,384]{1,0:T(8,128)(2,1)}, u32[]{:S(2)}, u32[]{:S(2)}) collective-permute-start(bf16[1024,384]{1,0:T(8,128)(2,1)} %get-tuple-element.72), channel_id=1, source_target_pairs={{0,2},{1,3},{5,7},{4,6},{11,9},{9,11},{13,15},{15,13},{18,16},{16,... | collective-permute-start | bytes 2359304 | tf_op jit(solution)/shard_map/ppermute | solution.py:459
  187.4 23.0 %collective-permute-start.20 = (bf16[1024,384]{1,0:T(8,128)(2,1)}, bf16[1024,384]{1,0:T(8,128)(2,1)}, u32[]{:S(2)}, u32[]{:S(2)}) collective-permute-start(bf16[1024,384]{1,0:T(8,128)(2,1)} %get-tuple-element.77), channel_id=1, source_target_pairs={{1,3},{5,7},{8,10},{12,14},{19,17},{23,21},{26,24},{30,28}} | collective-permute-start | bytes 2359304 | tf_op jit(solution)/shard_map/ppermute | solution.py:459
  198.6 20.2 %collective-permute-start.19 = (bf16[1024,384]{1,0:T(8,128)(2,1)}, bf16[1024,384]{1,0:T(8,128)(2,1)}, u32[]{:S(2)}, u32[]{:S(2)}) collective-permute-start(bf16[1024,384]{1,0:T(8,128)(2,1)} %get-tuple-element.83), channel_id=1, source_target_pairs={{1,3},{5,7},{8,10},{12,14},{19,17},{23,21},{26,24},{30,28}} | collective-permute-start | bytes 2359304 | tf_op jit(solution)/shard_map/ppermute | solution.py:459

commit v5 on v4

--- a/solution.py
+++ b/solution.py
@@ -310,9 +310,9 @@
         summary = call(
             summary_kernel,
             "summary",
-            grid=(heads_here // 2,),
-            in_specs=[smem, two_heads, two_heads],
-            out_specs=pl.BlockSpec((2, HS, HS), lambda h: (h, 0, 0)),
+            grid=(heads_here // 4,),
+            in_specs=[smem] + [pl.BlockSpec((rows, 4 * HS), lambda h: (0, h))] * 2,
+            out_specs=pl.BlockSpec((4, HS, HS), lambda h: (h, 0, 0)),
             out_shape=jax.ShapeDtypeStruct((heads_here, HS, HS), BF16),
             scratch_shapes=[pltpu.SMEM((1,), jnp.int32)],
             cost_estimate=cost(2 * rows * width * HS, 4 * rows * width),

time: 224 us -> 222 us (level)
  no operation moved by 1% of the time
where the time goes in v5:
time: 222 us; the launch traced here: 221 us
  Pallas kernels  100 us (45%)
  starting transfers between devices  60.1 us (27%)
  waiting for transfers between devices  58.9 us (27%)
    pallas_call x7, Pallas kernels, share(): call(functools.partial(partial_kernel, slots=len(slots), at=at + 2), 'par...  48.8 us
    ppermute x10, starting transfers between devices, send_on(): lax.ppermute(here, BOTH, along(source, step))  24.8 us
    ppermute x2, waiting for transfers between devices, shards(): lax.ppermute(pair_state, 'seq', [(s, s + 2 * d) for s in range(n - 2 * d)])  24 us
    ppermute x7, starting transfers between devices, share(): received.append(lax.ppermute(sent, BOTH, to_owner))  20.5 us
    ppermute x7, waiting for transfers between devices, share(): received.append(lax.ppermute(sent, BOTH, to_owner))  19.8 us
    pallas_call x7, Pallas kernels, add(): call(functools.partial(add_kernel, at=at, shares=len(received), tile=few)...  14.7 us
    pallas_call x2, Pallas kernels, intra_of(): call(functools.partial(intra_kernel, tile=256), 'intra', grid=(count,), i...  14.5 us
    ppermute x1, starting transfers between devices, shards(): lax.ppermute(head_out, 'head', [(h, h ^ 1) for h in range(heads)])  8.81 us
  transfers between devices with their start and end apart: 22, of which 9 were waited for; matrix products, arithmetic and copies ran while one was open for 1% of the time, Pallas kernels for 44%

profile of v5, /device:TPU:26, one launch (start us, length us, event | category | flops | bytes accessed | tf_op | source)
XLA Modules:
  0.0 220.9 jit_solution(12554111033150565552)
XLA Ops:
  0.0 2.9 %collective-permute-start = (bf16[1024,768]{1,0:T(8,128)(2,1)}, bf16[1024,768]{1,0:T(8,128)(2,1)}, u32[]{:S(2)}, u32[]{:S(2)}) collective-permute-start(bf16[1024,768]{1,0:T(8,128)(2,1)} %mine_ref.1), channel_id=1, source_target_pairs={{1,0},{3,2},{5,4},{7,6},{8,9},{10,11},{12,13},{14,15},{17,16},{19,... | collective-permute-start | bytes 4718600 | tf_op jit(solution)/shard_map/ppermute | solution.py:361
  2.9 3.4 %summary.1.own_ref = bf16[8,128,128]{2,1,0:T(8,128)(2,1)} custom-call(s32[16]{0:T(128)} %lengths_ref.7, bf16[1024,1024]{1,0:T(8,128)(2,1)} %key_ref.5, bf16[1024,1024]{1,0:T(8,128)(2,1)} %value_ref.5), custom_call_target="tpu_custom_call" | custom-call | flops 65536 | bytes 1024 | tf_op jit(solution)/shard_map/summary/pallas_call | solution.py:310
  6.8 3.8 %merge.1.rest_0_ = bf16[2,2048,384]{2,1,0:T(8,128)(2,1)} custom-call(bf16[1024,768]{1,0:T(8,128)(2,1)} %mine_ref.1, bf16[1024,768]{1,0:T(8,128)(2,1)} %collective-permute-done.gathered_ref), custom_call_target="tpu_custom_call" | custom-call | flops 96 | bytes 1536 | tf_op jit(solution)/shard_map/merge/pallas_call | solution.py:362
  10.7 2.4 %collective-permute-done.1.other_ref = bf16[8,128,128]{2,1,0:T(8,128)(2,1)} collective-permute-done((bf16[8,128,128]{2,1,0:T(8,128)(2,1)}, bf16[8,128,128]{2,1,0:T(8,128)(2,1)}, u32[]{:S(2)}, u32[]{:S(2)}) %collective-permute-start.1) | collective-permute-done | bytes 262176 | tf_op jit(solution)/shard_map/ppermute | solution.py:370
  13.1 1.3 collective-permute-start.6
  14.3 2.3 %collective-permute-start.5 = (bf16[2,2048,384]{2,1,0:T(8,128)(2,1)}, bf16[2,2048,384]{2,1,0:T(8,128)(2,1)}, u32[]{:S(2)}, u32[]{:S(2)}) collective-permute-start(bf16[2,2048,384]{2,1,0:T(8,128)(2,1)} %merge.1.rest_0_), channel_id=1, source_target_pairs={{0,8},{2,10},{4,0},{6,2},{9,17},{11,19},{13,5},{15,7},{16,24},{18,... | collective-permute-start | bytes 9437192 | tf_op jit(solution)/shard_map/ppermute | solution.py:356
  16.7 2.0 pair_state.1
  18.6 1.3 collective-permute-start.3
  19.9 1.3 collective-permute-start.2
  21.2 1.3 dynamic-slice_bitcast_fusion.table_ref
  22.5 7.2 %intra.2.low_ref = f32[1024,512]{1,0:T(8,128)} custom-call(s32[16]{0:T(128)} %lengths_ref.7, bf16[1024,1024]{1,0:T(8,128)(2,1)} %query_ref.5, bf16[1024,1024]{1,0:T(8,128)(2,1)} %key_ref.5, bf16[1024,1024]{1,0:T(8,128)(2,1)} %value_ref.5), custom_call_target="tpu_custom_call" | custom-call | flops 524288 | bytes 1280 | tf_op jit(solution)/shard_map/intra/pallas_call | solution.py:375
  29.7 7.3 %intra.3.high_ref = f32[1024,512]{1,0:T(8,128)} custom-call(s32[16]{0:T(128)} %lengths_ref.7, bf16[1024,1024]{1,0:T(8,128)(2,1)} %query_ref.5, bf16[1024,1024]{1,0:T(8,128)(2,1)} %key_ref.5, bf16[1024,1024]{1,0:T(8,128)(2,1)} %value_ref.5), custom_call_target="tpu_custom_call" | custom-call | flops 524288 | bytes 1280 | tf_op jit(solution)/shard_map/intra/pallas_call | solution.py:375
  37.0 24.0 %collective-permute-done.2.rest_0_ = bf16[8,128,128]{2,1,0:T(8,128)(2,1)} collective-permute-done((bf16[8,128,128]{2,1,0:T(8,128)(2,1)}, bf16[8,128,128]{2,1,0:T(8,128)(2,1)}, u32[]{:S(2)}, u32[]{:S(2)}) %collective-permute-start.2) | collective-permute-done | bytes 262176 | tf_op jit(solution)/shard_map/ppermute | solution.py:397
  61.0 6.4 %collective-permute-start.8 = (bf16[2,2048,384]{2,1,0:T(8,128)(2,1)}, bf16[2,2048,384]{2,1,0:T(8,128)(2,1)}, u32[]{:S(2)}, u32[]{:S(2)}) collective-permute-start(bf16[2,2048,384]{2,1,0:T(8,128)(2,1)} %collective-permute-done.6.rest_1_), channel_id=1, source_target_pairs={{1,5},{3,7},{4,12},{6,14},{8,0},{10,2},{12,20},{14,22},{17,9},{19,... | collective-permute-start | bytes 9437192 | tf_op jit(solution)/shard_map/ppermute | solution.py:356
  67.4 1.3 collective-permute-start.7
  68.7 6.9 %finish.1.own_ref = bf16[1024,1024]{1,0:T(8,128)(2,1)} custom-call(s32[16]{0:T(128)} %lengths_ref.7, bf16[1024,1024]{1,0:T(8,128)(2,1)} %query_ref.5, f32[1024,512]{1,0:T(8,128)} %intra.2.low_ref, f32[1024,512]{1,0:T(8,128)} %intra.3.high_ref, bf16[1024,1024]{1,0:T(8,128)(2,1)} %gate_ref.1, f32[1,1024]{1,0:T(1,128)} %bitcast.3, ...), custom_call_target="tpu_custom_call" | custom-call | flops 65536 | bytes 3072 | tf_op jit(solution)/shard_map/finish/pallas_call | solution.py:407
  75.6 8.8 %collective-permute-start.4 = (bf16[1024,1024]{1,0:T(8,128)(2,1)}, bf16[1024,1024]{1,0:T(8,128)(2,1)}, u32[]{:S(2)}, u32[]{:S(2)}) collective-permute-start(bf16[1024,1024]{1,0:T(8,128)(2,1)} %finish.1.own_ref), channel_id=1, source_target_pairs={{0,1},{1,0},{2,3},{3,2},{4,5},{5,4},{6,7},{7,6},{8,9},{9,8},{10,11... | collective-permute-start | bytes 6291464 | tf_op jit(solution)/shard_map/ppermute | solution.py:427
  84.4 4.1 %collective-permute-done.4.other_ref = bf16[1024,1024]{1,0:T(8,128)(2,1)} collective-permute-done((bf16[1024,1024]{1,0:T(8,128)(2,1)}, bf16[1024,1024]{1,0:T(8,128)(2,1)}, u32[]{:S(2)}, u32[]{:S(2)}) %collective-permute-start.4) | collective-permute-done | bytes 2097184 | tf_op jit(solution)/shard_map/ppermute | solution.py:427
  88.5 8.9 %partial.7 = (bf16[1024,768]{1,0:T(8,128)(2,1)}, f32[1024,768]{1,0:T(8,128)}) custom-call(s32[25]{0:T(128)} %dynamic-slice_bitcast_fusion.table_ref, bf16[1024,1024]{1,0:T(8,128)(2,1)} %finish.1.own_ref, bf16[1024,1024]{1,0:T(8,128)(2,1)} %collective-permute-done.4.other_ref, bf16[2,2048,384]{2,1,0:T(8,128)(2,1)} %collective-permute-done.5.rest_0_, ...), custom_call_target="tpu_custom_call" | custom-call | flops 786432 | bytes 2944 | tf_op jit(solution)/shard_map/partial/pallas_call | solution.py:439
  97.4 4.6 %collective-permute-start.9 = (bf16[1024,768]{1,0:T(8,128)(2,1)}, bf16[1024,768]{1,0:T(8,128)(2,1)}, u32[]{:S(2)}, u32[]{:S(2)}) collective-permute-start(bf16[1024,768]{1,0:T(8,128)(2,1)} %get-tuple-element.52), channel_id=1, source_target_pairs={{2,0},{3,1},{7,5},{6,4},{10,8},{8,10},{12,14},{14,12},{19,17},{17,... | collective-permute-start | bytes 4718600 | tf_op jit(solution)/shard_map/ppermute | solution.py:459
  102.0 3.7 %partial.8 = (bf16[1024,768]{1,0:T(8,128)(2,1)}, f32[1024,768]{1,0:T(8,128)}) custom-call(s32[25]{0:T(128)} %dynamic-slice_bitcast_fusion.table_ref, bf16[1024,1024]{1,0:T(8,128)(2,1)} %finish.1.own_ref, bf16[1024,1024]{1,0:T(8,128)(2,1)} %collective-permute-done.4.other_ref, bf16[2,2048,384]{2,1,0:T(8,128)(2,1)} %merge.1.rest_0_), custom_call_target="tpu_custom_call" | custom-call | flops 786432 | bytes 2944 | tf_op jit(solution)/shard_map/partial/pallas_call | solution.py:439
  106.9 6.0 %split.1 = (bf16[1,2048,384]{2,1,0:T(8,128)(2,1)}, bf16[1,2048,384]{2,1,0:T(8,128)(2,1)}, bf16[1,2048,384]{2,1,0:T(8,128)(2,1)}, bf16[1,2048,384]{2,1,0:T(8,128)(2,1)}) custom-call(bf16[2,2048,384]{2,1,0:T(8,128)(2,1)} %collective-permute-done.8.rest_1_.refs_0_, bf16[2,2048,384]{2,1,0:T(8,128)(2,1)} %collective-permute-done.7.rest_0_.refs_1_), custom_call_target="tpu_custom_call" | custom-call | flops 192 | bytes 3072 | tf_op jit(solution)/shard_map/split/pallas_call | solution.py:346
  112.9 2.5 %collective-permute-start.10 = (bf16[1,2048,384]{2,1,0:T(8,128)(2,1)}, bf16[1,2048,384]{2,1,0:T(8,128)(2,1)}, u32[]{:S(2)}, u32[]{:S(2)}) collective-permute-start(bf16[1,2048,384]{2,1,0:T(8,128)(2,1)} %get-tuple-element.64), channel_id=1, source_target_pairs={{1,9},{3,11},{4,0},{6,2},{8,16},{10,18},{13,5},{15,7},{16,24},{18,... | collective-permute-start | bytes 4718600 | tf_op jit(solution)/shard_map/ppermute | solution.py:356
  115.4 1.3 collective-permute-start.11
  116.6 1.8 collective-permute-start.12
  118.5 1.5 collective-permute-start.14
  120.0 8.9 %partial.9 = (bf16[1024,768]{1,0:T(8,128)(2,1)}, f32[1024,768]{1,0:T(8,128)}) custom-call(s32[25]{0:T(128)} %dynamic-slice_bitcast_fusion.table_ref, bf16[1024,1024]{1,0:T(8,128)(2,1)} %finish.1.own_ref, bf16[1024,1024]{1,0:T(8,128)(2,1)} %collective-permute-done.4.other_ref, bf16[2,2048,384]{2,1,0:T(8,128)(2,1)} %collective-permute-done.7.rest_0_.refs_1_, ...), custom_call_target="tpu_custom_call" | custom-call | flops 786432 | bytes 2944 | tf_op jit(solution)/shard_map/partial/pallas_call | solution.py:439
  128.8 7.1 %collective-permute-done.9.rest_0_ = bf16[1024,768]{1,0:T(8,128)(2,1)} collective-permute-done((bf16[1024,768]{1,0:T(8,128)(2,1)}, bf16[1024,768]{1,0:T(8,128)(2,1)}, u32[]{:S(2)}, u32[]{:S(2)}) %collective-permute-start.9) | collective-permute-done | bytes 1572896 | tf_op jit(solution)/shard_map/ppermute | solution.py:459
  135.9 2.5 %collective-permute-start.13 = (bf16[1,2048,384]{2,1,0:T(8,128)(2,1)}, bf16[1,2048,384]{2,1,0:T(8,128)(2,1)}, u32[]{:S(2)}, u32[]{:S(2)}) collective-permute-start(bf16[1,2048,384]{2,1,0:T(8,128)(2,1)} %get-tuple-element.70), channel_id=1, source_target_pairs={{1,9},{3,11},{4,0},{6,2},{8,16},{10,18},{13,5},{15,7},{16,24},{18,... | collective-permute-start | bytes 4718600 | tf_op jit(solution)/shard_map/ppermute | solution.py:356
  139.2 8.8 %collective-permute-start.15 = (bf16[1024,768]{1,0:T(8,128)(2,1)}, bf16[1024,768]{1,0:T(8,128)(2,1)}, u32[]{:S(2)}, u32[]{:S(2)}) collective-permute-start(bf16[1024,768]{1,0:T(8,128)(2,1)} %get-tuple-element.58), channel_id=1, source_target_pairs={{3,1},{0,2},{4,6},{7,5},{10,8},{9,11},{13,15},{14,12},{18,16},{17,... | collective-permute-start | bytes 4718600 | tf_op jit(solution)/shard_map/ppermute | solution.py:459
  148.0 1.3 collective-permute-start.16
  149.3 6.9 %partial.10 = (bf16[1024,384]{1,0:T(8,128)(2,1)}, f32[1024,384]{1,0:T(8,128)}) custom-call(s32[25]{0:T(128)} %dynamic-slice_bitcast_fusion.table_ref, bf16[1024,1024]{1,0:T(8,128)(2,1)} %finish.1.own_ref, bf16[1024,1024]{1,0:T(8,128)(2,1)} %collective-permute-done.4.other_ref, bf16[1,2048,384]{2,1,0:T(8,128)(2,1)} %collective-permute-done.10.rest_0_, ...), custom_call_target="tpu_custom_call" | custom-call | flops 393216 | bytes 1984 | tf_op jit(solution)/shard_map/partial/pallas_call | solution.py:439
  157.0 4.6 %collective-permute-start.18 = (bf16[1,2048,384]{2,1,0:T(8,128)(2,1)}, bf16[1,2048,384]{2,1,0:T(8,128)(2,1)}, u32[]{:S(2)}, u32[]{:S(2)}) collective-permute-start(bf16[1,2048,384]{2,1,0:T(8,128)(2,1)} %collective-permute-done.14.rest_1_), channel_id=1, source_target_pairs={{1,5},{3,7},{4,12},{6,14},{9,1},{11,3},{13,21},{15,23},{16,8},{18,... | collective-permute-start | bytes 4718600 | tf_op jit(solution)/shard_map/ppermute | solution.py:356
  161.5 1.3 collective-permute-start.17
  162.9 6.8 %partial.11 = (bf16[1024,384]{1,0:T(8,128)(2,1)}, f32[1024,384]{1,0:T(8,128)}) custom-call(s32[25]{0:T(128)} %dynamic-slice_bitcast_fusion.table_ref, bf16[1024,1024]{1,0:T(8,128)(2,1)} %finish.1.own_ref, bf16[1024,1024]{1,0:T(8,128)(2,1)} %collective-permute-done.4.other_ref, bf16[1,2048,384]{2,1,0:T(8,128)(2,1)} %collective-permute-done.13.rest_0_, ...), custom_call_target="tpu_custom_call" | custom-call | flops 393216 | bytes 1984 | tf_op jit(solution)/shard_map/partial/pallas_call | solution.py:439
  169.7 1.3 collective-permute-start.21
  171.8 7.6 %collective-permute-done.16.rest_0_ = bf16[1,2048,384]{2,1,0:T(8,128)(2,1)} collective-permute-done((bf16[1,2048,384]{2,1,0:T(8,128)(2,1)}, bf16[1,2048,384]{2,1,0:T(8,128)(2,1)}, u32[]{:S(2)}, u32[]{:S(2)}) %collective-permute-start.16) | collective-permute-done | bytes 1572896 | tf_op jit(solution)/shard_map/ppermute | solution.py:356
  179.4 6.8 %partial.12 = (bf16[1024,384]{1,0:T(8,128)(2,1)}, f32[1024,384]{1,0:T(8,128)}) custom-call(s32[25]{0:T(128)} %dynamic-slice_bitcast_fusion.table_ref, bf16[1024,1024]{1,0:T(8,128)(2,1)} %finish.1.own_ref, bf16[1024,1024]{1,0:T(8,128)(2,1)} %collective-permute-done.4.other_ref, bf16[1,2048,384]{2,1,0:T(8,128)(2,1)} %collective-permute-done.16.rest_0_), custom_call_target="tpu_custom_call" | custom-call | flops 393216 | bytes 1984 | tf_op jit(solution)/shard_map/partial/pallas_call | solution.py:439
  186.2 1.3 collective-permute-start.20
  187.5 3.1 %add_shares.10.rest_1_ = bf16[1024,1536]{1,0:T(8,128)(2,1)} custom-call(s32[25]{0:T(128)} %dynamic-slice_bitcast_fusion.table_ref, f32[1024,384]{1,0:T(8,128)} %get-tuple-element.79.kept_ref, bf16[1024,384]{1,0:T(8,128)(2,1)} %collective-permute-done.17.rest_0_, bf16[1024,1536]{1,0:T(8,128)(2,1)} %add_shares.9.rest_1_), custom_call_target="tpu_custom_call", output_to_operand_aliasing={{}: (3, {})} | custom-call | flops 192 | bytes 960 | tf_op jit(solution)/shard_map/add_shares/pallas_call | solution.py:469
  190.6 6.8 %partial.13 = (bf16[1024,384]{1,0:T(8,128)(2,1)}, f32[1024,384]{1,0:T(8,128)}) custom-call(s32[25]{0:T(128)} %dynamic-slice_bitcast_fusion.table_ref, bf16[1024,1024]{1,0:T(8,128)(2,1)} %finish.1.own_ref, bf16[1024,1024]{1,0:T(8,128)(2,1)} %collective-permute-done.4.other_ref, bf16[1,2048,384]{2,1,0:T(8,128)(2,1)} %collective-permute-done.18.rest_0_), custom_call_target="tpu_custom_call" | custom-call | flops 393216 | bytes 1984 | tf_op jit(solution)/shard_map/partial/pallas_call | solution.py:439
  197.4 1.3 collective-permute-start.19
  198.7 2.1 collective-permute-done.21.rest_0_
  200.8 3.1 %add_shares.11.rest_1_ = bf16[1024,1536]{1,0:T(8,128)(2,1)} custom-call(s32[25]{0:T(128)} %dynamic-slice_bitcast_fusion.table_ref, f32[1024,384]{1,0:T(8,128)} %get-tuple-element.86.kept_ref, bf16[1024,384]{1,0:T(8,128)(2,1)} %collective-permute-done.21.rest_0_, bf16[1024,1536]{1,0:T(8,128)(2,1)} %add_shares.10.rest_1_), custom_call_target="tpu_custom_call", output_to_operand_aliasing={{}: (3, {})} | custom-call | flops 192 | bytes 960 | tf_op jit(solution)/shard_map/add_shares/pallas_call | solution.py:469
  203.9 5.3 %collective-permute-done.20.rest_0_ = bf16[1024,384]{1,0:T(8,128)(2,1)} collective-permute-done((bf16[1024,384]{1,0:T(8,128)(2,1)}, bf16[1024,384]{1,0:T(8,128)(2,1)}, u32[]{:S(2)}, u32[]{:S(2)}) %collective-permute-start.20) | collective-permute-done | bytes 786464 | tf_op jit(solution)/shard_map/ppermute | solution.py:459
  209.2 3.1 %add_shares.12.rest_1_ = bf16[1024,1536]{1,0:T(8,128)(2,1)} custom-call(s32[25]{0:T(128)} %dynamic-slice_bitcast_fusion.table_ref, f32[1024,384]{1,0:T(8,128)} %get-tuple-element.84.kept_ref, bf16[1024,384]{1,0:T(8,128)(2,1)} %collective-permute-done.20.rest_0_, bf16[1024,1536]{1,0:T(8,128)(2,1)} %add_shares.11.rest_1_), custom_call_target="tpu_custom_call", output_to_operand_aliasing={{}: (3, {})} | custom-call | flops 192 | bytes 960 | tf_op jit(solution)/shard_map/add_shares/pallas_call | solution.py:469
  212.3 5.3 %collective-permute-done.19.rest_0_ = bf16[1024,384]{1,0:T(8,128)(2,1)} collective-permute-done((bf16[1024,384]{1,0:T(8,128)(2,1)}, bf16[1024,384]{1,0:T(8,128)(2,1)}, u32[]{:S(2)}, u32[]{:S(2)}) %collective-permute-start.19) | collective-permute-done | bytes 786464 | tf_op jit(solution)/shard_map/ppermute | solution.py:459
  217.6 3.1 %add_shares.13 = bf16[1024,1536]{1,0:T(8,128)(2,1)} custom-call(s32[25]{0:T(128)} %dynamic-slice_bitcast_fusion.table_ref, f32[1024,384]{1,0:T(8,128)} %get-tuple-element.82.kept_ref, bf16[1024,384]{1,0:T(8,128)(2,1)} %collective-permute-done.19.rest_0_, bf16[1024,1536]{1,0:T(8,128)(2,1)} %add_shares.12.rest_1_), custom_call_target="tpu_custom_call", output_to_operand_aliasing={{}: (3, {})} | custom-call | flops 192 | bytes 960 | tf_op jit(solution)/shard_map/add_shares/pallas_call | solution.py:469
  (18 shorter events, 4.0 us)
Async XLA Ops:
  0.0 6.8 %collective-permute-start = (bf16[1024,768]{1,0:T(8,128)(2,1)}, bf16[1024,768]{1,0:T(8,128)(2,1)}, u32[]{:S(2)}, u32[]{:S(2)}) collective-permute-start(bf16[1024,768]{1,0:T(8,128)(2,1)} %mine_ref.1), channel_id=1, source_target_pairs={{1,0},{3,2},{5,4},{7,6},{8,9},{10,11},{12,13},{14,15},{17,16},{19,... | collective-permute-start | bytes 4718600 | tf_op jit(solution)/shard_map/ppermute | solution.py:361
  6.3 6.8 %collective-permute-start.1 = (bf16[8,128,128]{2,1,0:T(8,128)(2,1)}, bf16[8,128,128]{2,1,0:T(8,128)(2,1)}, u32[]{:S(2)}, u32[]{:S(2)}) collective-permute-start(bf16[8,128,128]{2,1,0:T(8,128)(2,1)} %summary.1.own_ref), channel_id=1, source_target_pairs={{0,4},{4,0},{8,12},{12,8},{16,20},{20,16},{24,28},{28,24},{1,5},{5... | collective-permute-start | bytes 786440 | tf_op jit(solution)/shard_map/ppermute | solution.py:370
  13.1 47.9 %collective-permute-start.6 = (bf16[2,2048,384]{2,1,0:T(8,128)(2,1)}, bf16[2,2048,384]{2,1,0:T(8,128)(2,1)}, u32[]{:S(2)}, u32[]{:S(2)}) collective-permute-start(bf16[2,2048,384]{2,1,0:T(8,128)(2,1)} %merge.1.rest_0_), channel_id=1, source_target_pairs={{0,4},{2,6},{4,12},{6,14},{9,1},{11,3},{13,21},{15,23},{16,8},{18,... | collective-permute-start | bytes 9437192 | tf_op jit(solution)/shard_map/ppermute | solution.py:356
  14.3 53.1 %collective-permute-start.5 = (bf16[2,2048,384]{2,1,0:T(8,128)(2,1)}, bf16[2,2048,384]{2,1,0:T(8,128)(2,1)}, u32[]{:S(2)}, u32[]{:S(2)}) collective-permute-start(bf16[2,2048,384]{2,1,0:T(8,128)(2,1)} %merge.1.rest_0_), channel_id=1, source_target_pairs={{0,8},{2,10},{4,0},{6,2},{9,17},{11,19},{13,5},{15,7},{16,24},{18,... | collective-permute-start | bytes 9437192 | tf_op jit(solution)/shard_map/ppermute | solution.py:356
  18.6 18.4 %collective-permute-start.3 = (bf16[8,128,128]{2,1,0:T(8,128)(2,1)}, bf16[8,128,128]{2,1,0:T(8,128)(2,1)}, u32[]{:S(2)}, u32[]{:S(2)}) collective-permute-start(bf16[8,128,128]{2,1,0:T(8,128)(2,1)} %pair_state.1), channel_id=1, source_target_pairs={{0,16},{4,20},{8,24},{12,28},{1,17},{5,21},{9,25},{13,29},{2,18},{... | collective-permute-start | bytes 786440 | tf_op jit(solution)/shard_map/ppermute | solution.py:397
  19.9 41.1 %collective-permute-start.2 = (bf16[8,128,128]{2,1,0:T(8,128)(2,1)}, bf16[8,128,128]{2,1,0:T(8,128)(2,1)}, u32[]{:S(2)}, u32[]{:S(2)}) collective-permute-start(bf16[8,128,128]{2,1,0:T(8,128)(2,1)} %pair_state.1), channel_id=1, source_target_pairs={{0,8},{4,12},{8,16},{12,20},{16,24},{20,28},{1,9},{5,13},{9,17},{1... | collective-permute-start | bytes 786440 | tf_op jit(solution)/shard_map/ppermute | solution.py:397
  61.0 44.8 %collective-permute-start.8 = (bf16[2,2048,384]{2,1,0:T(8,128)(2,1)}, bf16[2,2048,384]{2,1,0:T(8,128)(2,1)}, u32[]{:S(2)}, u32[]{:S(2)}) collective-permute-start(bf16[2,2048,384]{2,1,0:T(8,128)(2,1)} %collective-permute-done.6.rest_1_), channel_id=1, source_target_pairs={{1,5},{3,7},{4,12},{6,14},{8,0},{10,2},{12,20},{14,22},{17,9},{19,... | collective-permute-start | bytes 9437192 | tf_op jit(solution)/shard_map/ppermute | solution.py:356
  67.4 39.5 %collective-permute-start.7 = (bf16[2,2048,384]{2,1,0:T(8,128)(2,1)}, bf16[2,2048,384]{2,1,0:T(8,128)(2,1)}, u32[]{:S(2)}, u32[]{:S(2)}) collective-permute-start(bf16[2,2048,384]{2,1,0:T(8,128)(2,1)} %collective-permute-done.5.rest_0_), channel_id=1, source_target_pairs={{0,8},{2,10},{5,1},{7,3},{8,16},{10,18},{12,4},{14,6},{17,25},{19,... | collective-permute-start | bytes 9437192 | tf_op jit(solution)/shard_map/ppermute | solution.py:356
  75.6 12.9 %collective-permute-start.4 = (bf16[1024,1024]{1,0:T(8,128)(2,1)}, bf16[1024,1024]{1,0:T(8,128)(2,1)}, u32[]{:S(2)}, u32[]{:S(2)}) collective-permute-start(bf16[1024,1024]{1,0:T(8,128)(2,1)} %finish.1.own_ref), channel_id=1, source_target_pairs={{0,1},{1,0},{2,3},{3,2},{4,5},{5,4},{6,7},{7,6},{8,9},{9,8},{10,11... | collective-permute-start | bytes 6291464 | tf_op jit(solution)/shard_map/ppermute | solution.py:427
  97.4 38.5 %collective-permute-start.9 = (bf16[1024,768]{1,0:T(8,128)(2,1)}, bf16[1024,768]{1,0:T(8,128)(2,1)}, u32[]{:S(2)}, u32[]{:S(2)}) collective-permute-start(bf16[1024,768]{1,0:T(8,128)(2,1)} %get-tuple-element.52), channel_id=1, source_target_pairs={{2,0},{3,1},{7,5},{6,4},{10,8},{8,10},{12,14},{14,12},{19,17},{17,... | collective-permute-start | bytes 4718600 | tf_op jit(solution)/shard_map/ppermute | solution.py:459
  112.9 26.3 %collective-permute-start.10 = (bf16[1,2048,384]{2,1,0:T(8,128)(2,1)}, bf16[1,2048,384]{2,1,0:T(8,128)(2,1)}, u32[]{:S(2)}, u32[]{:S(2)}) collective-permute-start(bf16[1,2048,384]{2,1,0:T(8,128)(2,1)} %get-tuple-element.64), channel_id=1, source_target_pairs={{1,9},{3,11},{4,0},{6,2},{8,16},{10,18},{13,5},{15,7},{16,24},{18,... | collective-permute-start | bytes 4718600 | tf_op jit(solution)/shard_map/ppermute | solution.py:356
  115.4 32.7 %collective-permute-start.11 = (bf16[1,2048,384]{2,1,0:T(8,128)(2,1)}, bf16[1,2048,384]{2,1,0:T(8,128)(2,1)}, u32[]{:S(2)}, u32[]{:S(2)}) collective-permute-start(bf16[1,2048,384]{2,1,0:T(8,128)(2,1)} %get-tuple-element.65), channel_id=1, source_target_pairs={{0,4},{2,6},{5,13},{7,15},{9,1},{11,3},{12,20},{14,22},{17,9},{19,... | collective-permute-start | bytes 4718600 | tf_op jit(solution)/shard_map/ppermute | solution.py:356
  116.6 39.5 %collective-permute-start.12 = (bf16[1024,768]{1,0:T(8,128)(2,1)}, bf16[1024,768]{1,0:T(8,128)(2,1)}, u32[]{:S(2)}, u32[]{:S(2)}) collective-permute-start(bf16[1024,768]{1,0:T(8,128)(2,1)} %get-tuple-element.54), channel_id=1, source_target_pairs={{2,0},{6,4},{11,9},{15,13},{16,18},{20,22},{25,27},{29,31}} | collective-permute-start | bytes 4718600 | tf_op jit(solution)/shard_map/ppermute | solution.py:459
  118.5 38.5 %collective-permute-start.14 = (bf16[1,2048,384]{2,1,0:T(8,128)(2,1)}, bf16[1,2048,384]{2,1,0:T(8,128)(2,1)}, u32[]{:S(2)}, u32[]{:S(2)}) collective-permute-start(bf16[1,2048,384]{2,1,0:T(8,128)(2,1)} %get-tuple-element.71), channel_id=1, source_target_pairs={{0,4},{2,6},{5,13},{7,15},{9,1},{11,3},{12,20},{14,22},{17,9},{19,... | collective-permute-start | bytes 4718600 | tf_op jit(solution)/shard_map/ppermute | solution.py:356
  135.9 26.9 %collective-permute-start.13 = (bf16[1,2048,384]{2,1,0:T(8,128)(2,1)}, bf16[1,2048,384]{2,1,0:T(8,128)(2,1)}, u32[]{:S(2)}, u32[]{:S(2)}) collective-permute-start(bf16[1,2048,384]{2,1,0:T(8,128)(2,1)} %get-tuple-element.70), channel_id=1, source_target_pairs={{1,9},{3,11},{4,0},{6,2},{8,16},{10,18},{13,5},{15,7},{16,24},{18,... | collective-permute-start | bytes 4718600 | tf_op jit(solution)/shard_map/ppermute | solution.py:356
  139.2 31.8 %collective-permute-start.15 = (bf16[1024,768]{1,0:T(8,128)(2,1)}, bf16[1024,768]{1,0:T(8,128)(2,1)}, u32[]{:S(2)}, u32[]{:S(2)}) collective-permute-start(bf16[1024,768]{1,0:T(8,128)(2,1)} %get-tuple-element.58), channel_id=1, source_target_pairs={{3,1},{0,2},{4,6},{7,5},{10,8},{9,11},{13,15},{14,12},{18,16},{17,... | collective-permute-start | bytes 4718600 | tf_op jit(solution)/shard_map/ppermute | solution.py:459
  148.0 31.4 %collective-permute-start.16 = (bf16[1,2048,384]{2,1,0:T(8,128)(2,1)}, bf16[1,2048,384]{2,1,0:T(8,128)(2,1)}, u32[]{:S(2)}, u32[]{:S(2)}) collective-permute-start(bf16[1,2048,384]{2,1,0:T(8,128)(2,1)} %collective-permute-done.10.rest_0_), channel_id=1, source_target_pairs={{0,8},{2,10},{5,1},{7,3},{9,17},{11,19},{13,5},{15,7},{16,24},{18,... | collective-permute-start | bytes 4718600 | tf_op jit(solution)/shard_map/ppermute | solution.py:356
  157.0 33.6 %collective-permute-start.18 = (bf16[1,2048,384]{2,1,0:T(8,128)(2,1)}, bf16[1,2048,384]{2,1,0:T(8,128)(2,1)}, u32[]{:S(2)}, u32[]{:S(2)}) collective-permute-start(bf16[1,2048,384]{2,1,0:T(8,128)(2,1)} %collective-permute-done.14.rest_1_), channel_id=1, source_target_pairs={{1,5},{3,7},{4,12},{6,14},{9,1},{11,3},{13,21},{15,23},{16,8},{18,... | collective-permute-start | bytes 4718600 | tf_op jit(solution)/shard_map/ppermute | solution.py:356
  161.5 25.9 %collective-permute-start.17 = (bf16[1024,384]{1,0:T(8,128)(2,1)}, bf16[1024,384]{1,0:T(8,128)(2,1)}, u32[]{:S(2)}, u32[]{:S(2)}) collective-permute-start(bf16[1024,384]{1,0:T(8,128)(2,1)} %get-tuple-element.66), channel_id=1, source_target_pairs={{0,2},{1,3},{5,7},{4,6},{11,9},{9,11},{13,15},{15,13},{18,16},{16,... | collective-permute-start | bytes 2359304 | tf_op jit(solution)/shard_map/ppermute | solution.py:459
  169.7 31.1 %collective-permute-start.21 = (bf16[1024,384]{1,0:T(8,128)(2,1)}, bf16[1024,384]{1,0:T(8,128)(2,1)}, u32[]{:S(2)}, u32[]{:S(2)}) collective-permute-start(bf16[1024,384]{1,0:T(8,128)(2,1)} %get-tuple-element.72), channel_id=1, source_target_pairs={{0,2},{1,3},{5,7},{4,6},{11,9},{9,11},{13,15},{15,13},{18,16},{16,... | collective-permute-start | bytes 2359304 | tf_op jit(solution)/shard_map/ppermute | solution.py:459
  186.2 23.0 %collective-permute-start.20 = (bf16[1024,384]{1,0:T(8,128)(2,1)}, bf16[1024,384]{1,0:T(8,128)(2,1)}, u32[]{:S(2)}, u32[]{:S(2)}) collective-permute-start(bf16[1024,384]{1,0:T(8,128)(2,1)} %get-tuple-element.77), channel_id=1, source_target_pairs={{1,3},{5,7},{8,10},{12,14},{19,17},{23,21},{26,24},{30,28}} | collective-permute-start | bytes 2359304 | tf_op jit(solution)/shard_map/ppermute | solution.py:459
  197.4 20.2 %collective-permute-start.19 = (bf16[1024,384]{1,0:T(8,128)(2,1)}, bf16[1024,384]{1,0:T(8,128)(2,1)}, u32[]{:S(2)}, u32[]{:S(2)}) collective-permute-start(bf16[1024,384]{1,0:T(8,128)(2,1)} %get-tuple-element.83), channel_id=1, source_target_pairs={{1,3},{5,7},{8,10},{12,14},{19,17},{23,21},{26,24},{30,28}} | collective-permute-start | bytes 2359304 | tf_op jit(solution)/shard_map/ppermute | solution.py:459
